TPU v7x, 512 devices: a whole 4x8x8 slice. The times are simulated.
512 devices in a mesh: user: 128 (over z, y, core), head: 4 (over x).
Axes of the slice: x: 4, y: 8, z: 8, core: 2. Of those that a mesh axis runs over, the one named last changes fastest.
Arguments:
- events: bfloat16 [65536, 1024], P('user', 'head'), may hold values from -6 to 6
- norm_gain: float32 [1024], replicated, may hold values from 0.1 to 1.9
- w_uvqk: bfloat16 [1024, 4, 1024], P(None, None, 'head'), may hold values from -0.1875 to 0.1875
- w_out: bfloat16 [1024, 1024], P('head'), may hold values from -0.1875 to 0.1875
- cache_keys: bfloat16 [1024, 512, 1024], P('user', None, 'head'), may hold values from -6 to 6
- cache_values: bfloat16 [1024, 512, 1024], P('user', None, 'head'), may hold values from -6 to 6
- lengths: int32 [1024], P('user'), may hold values from 1 to 4, as said below
- swap_offset: int32 [1024], P('user'), may hold values from -1 to 1, as said below
Outputs:
- mixed: bfloat16 [65536, 1024], P('user', 'head')
Inputs may be any that keep to these rules, and one draw needn't show every extreme that they name: The cached user holds lengths * 128 used positions of its 512; some user has 4 blocks. `swap_offset`: for slot d * 8 + j, the offset is 0 or +1 where d - j is even and 0 or -1 where d - j is odd (device indices along user taken around the cycle); a slot with +1 and the slot of the same index j on the next device, which then has -1, trade their users. Every device has at least one slot with +1 and at least one with -1.
All inputs are finite; a program needn't handle non-finite values.
Results may differ from a plain program's by a relative error of at most 0.0055.
Values may be sent and summed in bfloat16 or wider, within the bound.
No kernel may reach another device: no remote copies, remote signals or barrier semaphores. Data moves between devices by JAX's collectives and lax.ppermute only.
A program may use at most 64 MiB of HBM per device.

v0:
```python
import jax
import jax.numpy as jnp
from jax import lax
from jax.sharding import PartitionSpec as P

HEAD = 64
BLOCK = 128


def from_behind(block, axis, distance):
    devices = range(lax.axis_size(axis))
    route = [((i - distance) % len(devices), i) for i in devices]
    return lax.ppermute(block, axis, route)


def layer_norm(values, epsilon):
    average = jnp.mean(values, axis=-1, keepdims=True)
    centred = values - average
    spread = jnp.mean(centred * centred, axis=-1, keepdims=True)
    return centred * lax.rsqrt(spread + epsilon)


def split_pairs(values, even_side):
    paired = values.reshape((values.shape[0] // 2, 2) + values.shape[1:])
    first_half = paired[:, 0]
    second = paired[:, 1]
    return (jnp.where(even_side, first_half, second), jnp.where(even_side, second, first_half))


def join_pairs(from_left, from_right, even_side):
    first_half = jnp.where(even_side, from_right, from_left)
    second = jnp.where(even_side, from_left, from_right)
    paired = jnp.stack([first_half, second], axis=1)
    return paired.reshape((paired.shape[0] * 2,) + paired.shape[2:])


def block_terms(queries, key_heads, value_heads, lengths, score_scale):
    span_length = key_heads.shape[1]
    scores = (
        jnp.einsum("unhe,uche->uhnc", queries, key_heads, preferred_element_type=jnp.float32)
        * score_scale
    )
    position = jnp.arange(span_length, dtype=jnp.int32)
    live_mask = position[None, :] < (lengths * BLOCK)[:, None]
    weight = jnp.where(live_mask[:, None, None, :], jax.nn.silu(scores), 0.0).astype(jnp.bfloat16)
    return jnp.einsum("uhnc,uche->unhe", weight, value_heads, preferred_element_type=jnp.float32)


def cache_terms(queries, cache_keys, cache_values, lengths, score_scale):
    user_count, fresh_rows, head_count, width = queries.shape
    key_heads = cache_keys.reshape(user_count, cache_keys.shape[1], head_count, width)
    value_heads = cache_values.reshape(user_count, cache_values.shape[1], head_count, width)
    return block_terms(queries, key_heads, value_heads, lengths, score_scale)


def fresh_terms(queries, fresh_keys, fresh_values, score_scale):
    fresh_rows = queries.shape[1]
    scores = (
        jnp.einsum("unhe,umhe->uhnm", queries, fresh_keys, preferred_element_type=jnp.float32)
        * score_scale
    )
    causal = jnp.arange(fresh_rows)[:, None] >= jnp.arange(fresh_rows)[None, :]
    weight = jnp.where(causal[None, None], jax.nn.silu(scores), 0.0).astype(jnp.bfloat16)
    return jnp.einsum("uhnm,umhe->unhe", weight, fresh_values, preferred_element_type=jnp.float32)


def on_device(events, norm_gain, w_uvqk, w_out, cache_keys, cache_values, lengths, swap_offset):
    user_count = lengths.shape[0]
    fresh_rows = events.shape[0] // user_count
    local_width = w_uvqk.shape[2]
    head_count = local_width // HEAD
    score_scale = HEAD ** (-0.5)
    gathered = lax.all_gather(events, "head", axis=1, tiled=True)
    normed = (layer_norm(gathered.astype(jnp.float32), 1e-05) * norm_gain).astype(jnp.bfloat16)
    projected = jnp.dot(
        normed, w_uvqk.reshape(w_uvqk.shape[0], 4 * local_width), preferred_element_type=jnp.float32
    )
    branches = (
        jax.nn.silu(projected)
        .astype(jnp.bfloat16)
        .reshape(user_count, fresh_rows, 4, head_count, HEAD)
    )
    gate_u = branches[:, :, 0]
    fresh_values = branches[:, :, 1]
    queries = branches[:, :, 2]
    fresh_keys = branches[:, :, 3]
    even_side = lax.axis_index("user") % 2 == 0
    staying = swap_offset == 0
    right_keys, left_keys = split_pairs(cache_keys, even_side)
    right_values, left_values = split_pairs(cache_values, even_side)
    right_lengths, left_lengths = split_pairs(lengths, even_side)
    from_left = from_behind((right_keys, right_values, right_lengths), "user", 1)
    from_right = from_behind((left_keys, left_values, left_lengths), "user", -1)
    moved_keys = join_pairs(from_left[0], from_right[0], even_side)
    moved_values = join_pairs(from_left[1], from_right[1], even_side)
    moved_lengths = join_pairs(from_left[2], from_right[2], even_side)
    served_keys = jnp.where(staying[:, None, None], cache_keys, moved_keys)
    served_values = jnp.where(staying[:, None, None], cache_values, moved_values)
    served_lengths = jnp.where(staying, lengths, moved_lengths)
    cached = cache_terms(queries, served_keys, served_values, served_lengths, score_scale)
    attended = cached + fresh_terms(queries, fresh_keys, fresh_values, score_scale)
    gated = (layer_norm(attended, 1e-05) * gate_u.astype(jnp.float32)).astype(jnp.bfloat16)
    gated = gated.reshape(user_count * fresh_rows, local_width)
    partial_terms = jnp.dot(gated, w_out, preferred_element_type=jnp.float32)
    summed = lax.psum_scatter(partial_terms, "head", scatter_dimension=1, tiled=True)
    return (events.astype(jnp.float32) + summed).astype(jnp.bfloat16)


def solution(mesh):
    return jax.shard_map(
        on_device,
        mesh=mesh,
        in_specs=(
            P("user", "head"),
            P(),
            P(None, None, "head"),
            P("head", None),
            P("user", None, "head"),
            P("user", None, "head"),
            P("user"),
            P("user"),
        ),
        out_specs=P("user", "head"),
        check_vma=False,
    )
```

profile of v0, /device:TPU:1, one launch (start us, length us, event | category | flops | bytes accessed | tf_op | source)
XLA Modules:
  0.0 142.4 jit_solution(971625842868113065)
XLA Ops:
  6.5 0.0 copy-start
  6.5 0.0 all-gather.2.cloned.1.call-start
  6.5 2.7 %fusion.30 = (bf16[4,1,512,256]{3,2,1,0:T(8,128)(2,1)S(1)}, bf16[4,1,512,256]{3,2,1,0:T(8,128)(2,1)}) fusion(bf16[4,2,512,256]{3,2,1,0:T(8,128)(2,1)} %bitcast.65), kind=kLoop, calls=%fused_computation.64 | loop fusion | bytes 4194304 | tf_op jit(solution)/shard_map/slice | solution.py:26
  9.2 0.5 copy.36
  9.8 1.5 %copy.37 = bf16[4,1,512,256]{2,3,0,1:T(8,128)(2,1)S(1)} copy(bf16[4,1,512,256]{3,2,1,0:T(8,128)(2,1)} %get-tuple-element.22) | data formatting | bytes 2097152
  11.3 0.0 copy-start.2
  11.3 1.5 %select_bitcast_fusion.7 = (bf16[4,512,256]{1,2,0:T(8,128)(2,1)}, bf16[4,512,256]{1,2,0:T(8,128)(2,1)}) fusion(bf16[4,1,512,256]{2,3,0,1:T(8,128)(2,1)S(1)} %copy.36, bf16[4,1,512,256]{2,3,0,1:T(8,128)(2,1)S(1)} %copy.37, pred[]{:T(512)S(6)} %eq.9), kind=kLoop, calls=%fused_computation.32 | loop fusion | flops 1048576 | bytes 4194305 | tf_op jit(solution)/shard_map/jit(_where)/select_n | solution.py:27
  12.8 8.8 %collective-permute-start = (bf16[4,512,256]{1,2,0:T(8,128)(2,1)}, bf16[4,512,256]{1,2,0:T(8,128)(2,1)}, u32[]{:S(2)}, u32[]{:S(2)}) collective-permute-start(bf16[4,512,256]{1,2,0:T(8,128)(2,1)} %get-tuple-element.19), channel_id=1, source_target_pairs={{4,0},{8,4},{12,8},{16,12},{20,16},{24,20},{28,24},{32,28},{36,32}... | collective-permute-start | bytes 3145736 | tf_op jit(solution)/shard_map/ppermute | solution.py:13
  21.6 1.9 %collective-permute-start.1 = (bf16[4,512,256]{1,2,0:T(8,128)(2,1)}, bf16[4,512,256]{1,2,0:T(8,128)(2,1)}, u32[]{:S(2)}, u32[]{:S(2)}) collective-permute-start(bf16[4,512,256]{1,2,0:T(8,128)(2,1)} %get-tuple-element.20), channel_id=1, source_target_pairs={{508,0},{0,4},{4,8},{8,12},{12,16},{16,20},{20,24},{24,28},{28,32}... | collective-permute-start | bytes 3145736 | tf_op jit(solution)/shard_map/ppermute | solution.py:13
  23.5 0.0 copy-done.2
  23.5 1.1 fusion.29
  24.6 0.5 copy.39
  25.1 1.5 %copy.40 = bf16[4,1,512,256]{2,3,0,1:T(8,128)(2,1)S(1)} copy(bf16[4,1,512,256]{3,2,1,0:T(8,128)(2,1)} %get-tuple-element.16) | data formatting | bytes 2097152
  26.6 0.0 copy-start.6
  26.7 1.4 %select_bitcast_fusion.3 = (bf16[4,512,256]{1,2,0:T(8,128)(2,1)}, bf16[4,512,256]{1,2,0:T(8,128)(2,1)}) fusion(bf16[4,1,512,256]{2,3,0,1:T(8,128)(2,1)S(1)} %copy.39, bf16[4,1,512,256]{2,3,0,1:T(8,128)(2,1)S(1)} %copy.40, pred[]{:T(512)S(6)} %eq.9), kind=kLoop, calls=%fused_computation.25 | loop fusion | flops 1048576 | bytes 4194305 | tf_op jit(solution)/shard_map/jit(_where)/select_n | solution.py:27
  28.1 7.9 %collective-permute-start.4 = (bf16[4,512,256]{1,2,0:T(8,128)(2,1)}, bf16[4,512,256]{1,2,0:T(8,128)(2,1)}, u32[]{:S(2)}, u32[]{:S(2)}) collective-permute-start(bf16[4,512,256]{1,2,0:T(8,128)(2,1)} %get-tuple-element.13), channel_id=1, source_target_pairs={{4,0},{8,4},{12,8},{16,12},{20,16},{24,20},{28,24},{32,28},{36,32}... | collective-permute-start | bytes 3145736 | tf_op jit(solution)/shard_map/ppermute | solution.py:13
  36.0 1.9 %collective-permute-start.5 = (bf16[4,512,256]{1,2,0:T(8,128)(2,1)}, bf16[4,512,256]{1,2,0:T(8,128)(2,1)}, u32[]{:S(2)}, u32[]{:S(2)}) collective-permute-start(bf16[4,512,256]{1,2,0:T(8,128)(2,1)} %get-tuple-element.14), channel_id=1, source_target_pairs={{508,0},{0,4},{4,8},{8,12},{12,16},{16,20},{20,24},{24,28},{28,32}... | collective-permute-start | bytes 3145736 | tf_op jit(solution)/shard_map/ppermute | solution.py:13
  37.9 0.0 copy-done.6
  38.0 0.1 reshape.105
  38.0 0.2 select_reduce_fusion.1
  38.2 7.0 %collective-permute-start.2 = (s32[4]{0:T(128)S(1)}, s32[4]{0:T(128)S(1)}, u32[]{:S(2)}, u32[]{:S(2)}) collective-permute-start(s32[4]{0:T(128)S(1)} %get-tuple-element.5), channel_id=1, source_target_pairs={{4,0},{8,4},{12,8},{16,12},{20,16},{24,20},{28,24},{32,28},{36,32}... | collective-permute-start | bytes 56 | tf_op jit(solution)/shard_map/ppermute | solution.py:13
  45.2 0.0 all-gather.2.cloned.1.call-update
  45.2 0.0 reduce-scatter.2.cloned.1.call-start
  45.3 2.9 %copy.25 = bf16[8,512,256]{1,2,0:T(8,128)(2,1)S(1)} copy(bf16[8,512,256]{2,1,0:T(8,128)(2,1)} %param.13) | data formatting | bytes 4194304 | tf_op args[5]
  48.2 3.9 %copy.31 = bf16[8,512,256]{1,2,0:T(8,128)(2,1)} copy(bf16[8,512,256]{2,1,0:T(8,128)(2,1)} %param.12) | data formatting | bytes 4194304 | tf_op args[4]
  52.1 3.4 %copy.44 = bf16[128,8,4,256]{3,1,2,0:T(8,128)(2,1)} copy(bf16[128,8,4,256]{3,2,1,0:T(4,128)(2,1)} %bitcast.69) | data formatting | bytes 4194304
  55.5 0.0 copy-done.7
  55.5 0.0 collective-permute-done.2
  55.5 2.1 %collective-permute-start.3 = (s32[4]{0:T(128)S(1)}, s32[4]{0:T(128)S(1)}, u32[]{:S(2)}, u32[]{:S(2)}) collective-permute-start(s32[4]{0:T(128)S(1)} %get-tuple-element.6), channel_id=1, source_target_pairs={{508,0},{0,4},{4,8},{8,12},{12,16},{16,20},{20,24},{24,28},{28,32}... | collective-permute-start | bytes 56 | tf_op jit(solution)/shard_map/ppermute | solution.py:13
  57.6 5.5 %collective-permute-done.3 = s32[4]{0:T(128)S(1)} collective-permute-done((s32[4]{0:T(128)S(1)}, s32[4]{0:T(128)S(1)}, u32[]{:S(2)}, u32[]{:S(2)}) %collective-permute-start.3) | collective-permute-done | bytes 48 | tf_op jit(solution)/shard_map/ppermute | solution.py:13
  63.1 0.1 copy.26
  63.2 0.1 reshape.106
  63.3 0.1 iota_compare_fusion.1
  63.4 0.0 collective-permute-done.4
  63.4 0.0 collective-permute-done.5
  63.4 1.7 %select_bitcast_fusion.1 = (bf16[4,1,512,256]{2,3,0,1:T(8,128)(2,1)S(1)}, bf16[4,1,512,256]{2,3,0,1:T(8,128)(2,1)S(1)}) fusion(bf16[4,512,256]{1,2,0:T(8,128)(2,1)} %collective-permute-done.4, bf16[4,512,256]{1,2,0:T(8,128)(2,1)} %collective-permute-done.5, pred[]{:T(512)S(6)} %eq.9), kind=kLoop, calls=%fused_computation.23 | loop fusion | flops 1048576 | bytes 4194305 | tf_op jit(solution)/shard_map/stack | solution.py:33
  65.1 0.2 pad_maximum_fusion.1
  65.3 0.2 copy.30
  65.6 0.0 collective-permute-done
  65.6 0.0 collective-permute-done.1
  65.6 1.7 %select_bitcast_fusion.5 = (bf16[4,1,512,256]{2,3,1,0:T(8,128)(2,1)S(1)}, bf16[4,1,512,256]{2,3,1,0:T(8,128)(2,1)S(1)}) fusion(bf16[4,512,256]{1,2,0:T(8,128)(2,1)} %collective-permute-done, bf16[4,512,256]{1,2,0:T(8,128)(2,1)} %collective-permute-done.1, pred[]{:T(512)S(6)} %eq.9), kind=kLoop, calls=%fused_computation.30 | loop fusion | flops 1048576 | bytes 4194305 | tf_op jit(solution)/shard_map/stack | solution.py:33
  67.3 0.0 copy-start.1
  67.3 0.2 pad_maximum_fusion
  67.5 1.4 copy-done.1
  68.9 2.7 %bitcast_select_fusion = (bf16[8,512,256]{1,2,0:T(8,128)(2,1)}, bf16[8,512,256]{1,2,0:T(8,128)(2,1)}) fusion(bf16[8,512,256]{1,2,0:T(8,128)(2,1)S(1)} %copy-done.1, bf16[4,2,512,256]{2,3,1,0:T(8,128)(2,1)S(1)} %copy.30, pred[8]{0:T(512)(128)(4,1)S(1)} %broadcast_compare_fusion, bf16[8,512,256]{1,2,0:T(8,128)(2,1)S(1)} %copy.25, ...), kind=kLoop, calls=%fused_computation.10 | loop fusion | flops 2097152 | bytes 12582920 | tf_op jit(solution)/shard_map/jit(_where)/select_n | solution.py:97
  71.6 1.5 %convert_reduce_fusion = f32[512]{0:T(512)S(1)} fusion(bf16[512,1024]{1,0:T(8,128)(2,1)} %all-gather.2.cloned.1.call-done), kind=kLoop, calls=%fused_computation.2 | loop fusion | flops 1048064 | bytes 1050624 | tf_op jit(solution)/shard_map/reduce_sum | solution.py:17
  73.2 1.6 %fusion.2 = f32[512]{0:T(512)S(1)} fusion(bf16[512,1024]{1,0:T(8,128)(2,1)} %all-gather.2.cloned.1.call-done, f32[512]{0:T(512)S(1)} %broadcast_multiply_fusion.1), kind=kLoop, calls=%fused_computation.5 | loop fusion | flops 2096640 | bytes 1052672 | tf_op jit(solution)/shard_map/reduce_sum | solution.py:19
  74.8 0.0 copy-done.8
  74.8 4.2 %multiply_convert_fusion = bf16[512,1024]{1,0:T(8,128)(2,1)} fusion(bf16[1024,1024]{1,0:T(8,128)(2,1)} %bitcast.70, bf16[512,1024]{1,0:T(8,128)(2,1)S(1)} %copy-done.3, f32[1024]{0:T(1024)S(1)} %copy-done.8, f32[512]{0:T(512)S(1)} %add_rsqrt_fusion.1, f32[512]{0:T(512)S(1)} %broadcast_multiply_fusion.1), kind=kOutput, calls=%fused_computation.12 | convolution fusion | flops 1078984704 | bytes 4202496 | tf_op jit(solution)/shard_map/dot_general | solution.py:75
  79.0 4.1 %reshape.108 = bf16[8,64,4,4,64]{4,3,2,1,0:T(4,128)(2,1)S(1)} reshape(bf16[512,1024]{1,0:T(8,128)(2,1)} %multiply_convert_fusion) | data formatting | bytes 2097152 | tf_op jit(solution)/shard_map/reshape | solution.py:81
  83.1 2.0 %fusion.28 = (bf16[8,64,1,4,64]{4,3,2,1,0:T(4,128)(2,1)S(1)}, bf16[8,64,1,4,64]{4,3,2,1,0:T(4,128)(2,1)}, bf16[8,64,1,4,64]{4,3,2,1,0:T(4,128)(2,1)}, bf16[8,64,1,4,64]{4,3,2,1,0:T(4,128)(2,1)}) fusion(bf16[8,64,4,4,64]{4,3,2,1,0:T(4,128)(2,1)S(1)} %reshape.108), kind=kLoop, calls=%fused_computation.62 | loop fusion | bytes 2097152 | tf_op jit(solution)/shard_map/slice | solution.py:83
  85.1 1.3 copy.41
  86.4 5.4 %fusion.6 = f32[8,4,64,64]{3,2,1,0:T(8,128)} fusion(bf16[8,512,4,64]{1,3,2,0:T(8,128)(2,1)} %bitcast.68, bf16[8,512,4,64]{1,3,2,0:T(8,128)(2,1)} %bitcast.67, pred[8,512]{1,0:T(8,128)(4,1)S(1)} %iota_compare_fusion.1, bf16[8,64,1,4,64]{4,3,2,1,0:T(4,128)(2,1)} %get-tuple-element.9), kind=kOutput, calls=%fused_computation.16 | convolution fusion | flops 275775488 | bytes 4984832 | tf_op jit(solution)/shard_map/uhnc,uche->unhe/dot_general | solution.py:46
  91.8 2.1 %fusion.31 = (f32[8,64,4]{1,2,0:T(4,128)S(1)}, f32[8,64,4,64]{1,3,2,0:T(8,128)S(1)}) fusion(f32[8,4,64,64]{3,2,1,0:T(8,128)} %fusion.6, bf16[8,64,1,4,64]{4,3,2,1,0:T(4,128)(2,1)} %get-tuple-element.10, pred[64,64]{1,0:T(8,128)(4,1)S(1)} %iota_compare_fusion, bf16[8,64,1,4,64]{4,3,2,1,0:T(4,128)(2,1)S(1)} %copy-done.5, bf16[8,64,1,4,64]{1,4,3,0,2:T(8,128)(2,1)S(1)} %copy.41), kind=kOutput, calls=%fused_computation.65 | convolution fusion | flops 34732032 | bytes 1847296 | tf_op jit(solution)/shard_map/uhnm,umhe->unhe/dot_general | solution.py:64
  94.0 0.2 multiply_reduce_fusion
  94.2 0.3 copy.43
  94.5 0.2 fusion.11
  94.8 0.3 copy.35
  95.1 0.3 reshape.112
  95.4 0.0 copy-start.4
  95.5 1.8 %fusion.32 = f32[512,1024]{1,0:T(8,128)} fusion(bf16[512,256]{0,1:T(8,128)(2,1)S(1)} %reshape.112, bf16[256,1024]{1,0:T(8,128)(2,1)S(1)} %copy-done), kind=kOutput, calls=%fused_computation.66 | convolution fusion | flops 268435456 | bytes 2883584 | tf_op jit(solution)/shard_map/dot_general | solution.py:104
  97.2 0.0 reduce-scatter.2.cloned.1.call-update
  97.3 36.5 %reduce-scatter.2.cloned.1.call-done = f32[512,256]{1,0:T(8,128)} async-done(((f32[512,1024]{1,0:T(8,128)}), f32[512,256]{1,0:T(8,128)}) %reduce-scatter.2.cloned.1.call-update) | async-done | bytes 524304 | tf_op jit(solution)/shard_map/reduce_scatter | solution.py:105
  133.8 1.8 %add_convert_fusion = bf16[512,256]{1,0:T(8,128)(2,1)} fusion(f32[512,256]{1,0:T(8,128)} %reduce-scatter.2.cloned.1.call-done, bf16[512,256]{1,0:T(8,128)(2,1)S(1)} %copy-done.4), kind=kLoop, calls=%fused_computation.36 | loop fusion | flops 393216 | bytes 1048576 | tf_op jit(solution)/shard_map/convert_element_type | solution.py:106
  (18 shorter events, 0.1 us)
Async XLA Ops:
  6.5 88.9 %copy-start = (bf16[256,1024]{1,0:T(8,128)(2,1)S(1)}, bf16[256,1024]{1,0:T(8,128)(2,1)}, u32[]{:S(2)}) copy-start(bf16[256,1024]{1,0:T(8,128)(2,1)} %param.11) | copy-start | bytes 1572868
  6.5 65.1 %all-gather.2.cloned.1.call-start = ((), (), s32[]{:S(2)}) async-start(), calls=%async_computation.1 | async-start | bytes 1310720 | tf_op jit(solution)/shard_map/all_gather | solution.py:73
  11.3 12.2 %copy-start.2 = (bf16[8,512,256]{2,1,0:T(8,128)(2,1)S(1)}, bf16[8,512,256]{2,1,0:T(8,128)(2,1)}, u32[]{:S(2)}) copy-start(bf16[8,512,256]{2,1,0:T(8,128)(2,1)} %param.12) | copy-start | bytes 6291460
  12.8 52.8 %collective-permute-start = (bf16[4,512,256]{1,2,0:T(8,128)(2,1)}, bf16[4,512,256]{1,2,0:T(8,128)(2,1)}, u32[]{:S(2)}, u32[]{:S(2)}) collective-permute-start(bf16[4,512,256]{1,2,0:T(8,128)(2,1)} %get-tuple-element.19), channel_id=1, source_target_pairs={{4,0},{8,4},{12,8},{16,12},{20,16},{24,20},{28,24},{32,28},{36,32}... | collective-permute-start | bytes 3145736 | tf_op jit(solution)/shard_map/ppermute | solution.py:13
  21.6 44.0 %collective-permute-start.1 = (bf16[4,512,256]{1,2,0:T(8,128)(2,1)}, bf16[4,512,256]{1,2,0:T(8,128)(2,1)}, u32[]{:S(2)}, u32[]{:S(2)}) collective-permute-start(bf16[4,512,256]{1,2,0:T(8,128)(2,1)} %get-tuple-element.20), channel_id=1, source_target_pairs={{508,0},{0,4},{4,8},{8,12},{12,16},{16,20},{20,24},{24,28},{28,32}... | collective-permute-start | bytes 3145736 | tf_op jit(solution)/shard_map/ppermute | solution.py:13
  26.6 11.3 %copy-start.6 = (s32[8]{0:T(128)S(1)}, s32[8]{0:T(128)}, u32[]{:S(2)}) copy-start(s32[8]{0:T(128)} %param.14) | copy-start | bytes 100
  28.1 35.3 %collective-permute-start.4 = (bf16[4,512,256]{1,2,0:T(8,128)(2,1)}, bf16[4,512,256]{1,2,0:T(8,128)(2,1)}, u32[]{:S(2)}, u32[]{:S(2)}) collective-permute-start(bf16[4,512,256]{1,2,0:T(8,128)(2,1)} %get-tuple-element.13), channel_id=1, source_target_pairs={{4,0},{8,4},{12,8},{16,12},{20,16},{24,20},{28,24},{32,28},{36,32}... | collective-permute-start | bytes 3145736 | tf_op jit(solution)/shard_map/ppermute | solution.py:13
  36.0 27.4 %collective-permute-start.5 = (bf16[4,512,256]{1,2,0:T(8,128)(2,1)}, bf16[4,512,256]{1,2,0:T(8,128)(2,1)}, u32[]{:S(2)}, u32[]{:S(2)}) collective-permute-start(bf16[4,512,256]{1,2,0:T(8,128)(2,1)} %get-tuple-element.14), channel_id=1, source_target_pairs={{508,0},{0,4},{4,8},{8,12},{12,16},{16,20},{20,24},{24,28},{28,32}... | collective-permute-start | bytes 3145736 | tf_op jit(solution)/shard_map/ppermute | solution.py:13
  38.2 17.3 %collective-permute-start.2 = (s32[4]{0:T(128)S(1)}, s32[4]{0:T(128)S(1)}, u32[]{:S(2)}, u32[]{:S(2)}) collective-permute-start(s32[4]{0:T(128)S(1)} %get-tuple-element.5), channel_id=1, source_target_pairs={{4,0},{8,4},{12,8},{16,12},{20,16},{24,20},{28,24},{32,28},{36,32}... | collective-permute-start | bytes 56 | tf_op jit(solution)/shard_map/ppermute | solution.py:13
  45.2 88.5 %reduce-scatter.2.cloned.1.call-start = ((), (), s32[]{:S(2)}) async-start(), calls=%async_computation.2 | async-start | bytes 2621440 | tf_op jit(solution)/shard_map/reduce_scatter | solution.py:105
  52.1 3.4 %copy-start.7 = (s32[8]{0:T(128)S(1)}, s32[8]{0:T(128)}, u32[]{:S(2)}) copy-start(s32[8]{0:T(128)} %param.15) | copy-start | bytes 100
  55.5 7.6 %collective-permute-start.3 = (s32[4]{0:T(128)S(1)}, s32[4]{0:T(128)S(1)}, u32[]{:S(2)}, u32[]{:S(2)}) collective-permute-start(s32[4]{0:T(128)S(1)} %get-tuple-element.6), channel_id=1, source_target_pairs={{508,0},{0,4},{4,8},{8,12},{12,16},{16,20},{20,24},{24,28},{28,32}... | collective-permute-start | bytes 56 | tf_op jit(solution)/shard_map/ppermute | solution.py:13
  67.3 1.6 %copy-start.1 = (bf16[8,512,256]{1,2,0:T(8,128)(2,1)S(1)}, bf16[8,512,256]{1,2,0:T(8,128)(2,1)}, u32[]{:S(2)}) copy-start(bf16[8,512,256]{1,2,0:T(8,128)(2,1)} %copy.31) | copy-start | bytes 6291460
  71.6 3.2 %copy-start.8 = (f32[1024]{0:T(1024)S(1)}, f32[1024]{0:T(1024)}, u32[]{:S(2)}) copy-start(f32[1024]{0:T(1024)} %param.9) | copy-start | bytes 12292
  71.6 3.2 %copy-start.3 = (bf16[512,1024]{1,0:T(8,128)(2,1)S(1)}, bf16[512,1024]{1,0:T(8,128)(2,1)}, u32[]{:S(2)}) copy-start(bf16[512,1024]{1,0:T(8,128)(2,1)} %all-gather.2.cloned.1.call-done) | copy-start | bytes 3145732
  86.4 5.4 %copy-start.5 = (bf16[8,64,1,4,64]{4,3,2,1,0:T(4,128)(2,1)S(1)}, bf16[8,64,1,4,64]{4,3,2,1,0:T(4,128)(2,1)}, u32[]{:S(2)}) copy-start(bf16[8,64,1,4,64]{4,3,2,1,0:T(4,128)(2,1)} %get-tuple-element.9) | copy-start | bytes 786436
  95.4 38.3 %copy-start.4 = (bf16[512,256]{1,0:T(8,128)(2,1)S(1)}, bf16[512,256]{1,0:T(8,128)(2,1)}, u32[]{:S(2)}) copy-start(bf16[512,256]{1,0:T(8,128)(2,1)} %param.8) | copy-start | bytes 786436
Sparse Core Ops, SparseCore 0:
  45.3 25.6 all-gather.1
  97.4 36.3 reduce-scatter.1
where the time goes:
time: 143 us; the launch traced here: 142 us
  waiting for transfers between devices  42 us (29%)
  starting transfers between devices  29.6 us (21%)
  local copies, waits for them, and re-layouts  28.4 us (20%)
  other arithmetic  15.1 us (11%)
  between operations  13.7 us (10%)
  matrix products  13.5 us (9%)
    reduce_scatter x1, waiting for transfers between devices, on_device(): lax.psum_scatter(partial_terms, 'head', scatter_dimension=1, tiled=True)  36.5 us
    ppermute x6, starting transfers between devices, from_behind(): return lax.ppermute(block, axis, route)  29.6 us
    unnamed x27, local copies, waits for them, and re-layouts  17.4 us
    ppermute x6, waiting for transfers between devices, from_behind(): return lax.ppermute(block, axis, route)  5.5 us
    dot_general x1, matrix products, block_terms(): jnp.einsum('uhnc,uche->unhe', weight, value_heads, preferred_element_type...  5.38 us
    dot_general x1, matrix products, on_device(): jnp.dot(normed, w_uvqk.reshape(w_uvqk.shape[0], 4 * local_width), preferr...  4.17 us
    reshape x1, local copies, waits for them, and re-layouts, on_device(): branches = jax.nn.silu(projected).astype(jnp.bfloat16).reshape(user_count...  4.14 us
    slice x2, local copies, waits for them, and re-layouts, split_pairs(): second = paired[:, 1]  3.81 us
  transfers between devices with their start and end apart: 8, of which 2 were waited for; matrix products, arithmetic and copies ran while one was open for 16% of the time, Pallas kernels for 0%

commit v1 on v0

v1 whole, which is shorter than its diff:
```python
import functools

import jax
import jax.numpy as jnp
from jax import lax
from jax.experimental import pallas as pl
from jax.experimental.pallas import tpu as pltpu
from jax.sharding import PartitionSpec as P

HEAD = 64
BLOCK = 128
NT = (((1,), (1,)), ((), ()))
NN = (((1,), (0,)), ((), ()))


def project_kernel(rows, x_ref, gain_ref, w_ref, out_ref):
    parts, total, width = x_ref.shape
    gain = gain_ref[...]
    features = parts * width

    def step(i, carry):
        at = pl.ds(pl.multiple_of(i * rows, rows), rows)
        x = jnp.concatenate([x_ref[p, at, :] for p in range(parts)], axis=1).astype(jnp.float32)
        average = jnp.sum(x, axis=-1, keepdims=True) * (1.0 / features)
        centred = x - average
        spread = jnp.sum(centred * centred, axis=-1, keepdims=True) * (1.0 / features)
        normed = (centred * lax.rsqrt(spread + 1e-05) * gain).astype(jnp.bfloat16)
        half = lax.dot_general(normed, w_ref[...], NN, preferred_element_type=jnp.float32) * 0.5
        out_ref[at, :] = (half + half * jnp.tanh(half)).astype(jnp.bfloat16)
        return carry

    lax.fori_loop(0, total // rows, step, 0)


def project(x4, gain, w):
    parts, total, width = x4.shape
    rows = 128
    return pl.pallas_call(
        functools.partial(project_kernel, rows),
        out_shape=jax.ShapeDtypeStruct((total, w.shape[1]), jnp.bfloat16),
        in_specs=[pl.BlockSpec(memory_space=pltpu.VMEM)] * 3,
        out_specs=pl.BlockSpec(memory_space=pltpu.VMEM),
        compiler_params=pltpu.CompilerParams(vmem_limit_bytes=24 * 2**20),
        cost_estimate=pl.CostEstimate(
            flops=2 * total * w.shape[0] * w.shape[1],
            bytes_accessed=2 * (w.size + 2 * x4.size),
            transcendentals=total * w.shape[1],
        ),
    )(x4, gain, w)


def attend_kernel(
    lengths, offsets, b_ref, keys, values, even, odd, w_ref, out_ref, kv, gated, sems
):
    slots, cap, width = keys.shape
    new = b_ref.shape[0] // slots
    heads = width // HEAD
    half_slots = slots // 2

    def copies(j, k_src, v_src):
        return (
            pltpu.make_async_copy(k_src, kv.at[2 * j], sems.at[2 * j]),
            pltpu.make_async_copy(v_src, kv.at[2 * j + 1], sems.at[2 * j + 1]),
        )

    for j in range(slots):
        moved = odd if j % 2 else even

        @pl.when(offsets[j] == 0)
        def _():
            for c in copies(j, keys.at[j], values.at[j]):
                c.start()

        @pl.when(offsets[j] != 0)
        def _():
            for c in copies(j, moved.at[j // 2], moved.at[half_slots + j // 2]):
                c.start()

    lane_head = lax.broadcasted_iota(jnp.int32, (new, width), 1) // HEAD
    position = lax.broadcasted_iota(jnp.int32, (1, cap), 1)
    row = lax.broadcasted_iota(jnp.int32, (heads * new, new), 0) % new
    causal = row >= lax.broadcasted_iota(jnp.int32, (heads * new, new), 1)
    pair_lane = lax.broadcasted_iota(jnp.int32, (new, 2 * HEAD), 1) // HEAD

    for j in range(slots):
        for c in copies(j, keys.at[j], values.at[j]):
            c.wait()
        at = slice(j * new, (j + 1) * new)
        gate = b_ref[at, :width].astype(jnp.float32)
        fresh_values = b_ref[at, width : 2 * width]
        queries = b_ref[at, 2 * width : 3 * width] * jnp.bfloat16(0.5 * HEAD**-0.5)
        fresh_keys = b_ref[at, 3 * width :]
        zero = jnp.zeros_like(queries)
        spread_q = jnp.concatenate(
            [jnp.where(lane_head == h, queries, zero) for h in range(heads)], axis=0
        )
        half = lax.dot_general(spread_q, kv[2 * j], NT, preferred_element_type=jnp.float32)
        used = jnp.where(offsets[j] == 0, lengths[j] * BLOCK, cap)
        weight = jnp.where(position < used, half + half * jnp.tanh(half), 0.0).astype(jnp.bfloat16)
        total = lax.dot_general(weight, kv[2 * j + 1], NN, preferred_element_type=jnp.float32)
        half = lax.dot_general(spread_q, fresh_keys, NT, preferred_element_type=jnp.float32)
        weight = jnp.where(causal, half + half * jnp.tanh(half), 0.0).astype(jnp.bfloat16)
        total = total + lax.dot_general(
            weight, fresh_values, NN, preferred_element_type=jnp.float32
        )
        for pair in range(heads // 2):
            lanes = slice(2 * HEAD * pair, 2 * HEAD * (pair + 1))
            result = jnp.zeros((new, 2 * HEAD), jnp.float32)
            for side in range(2):
                h = 2 * pair + side
                mine = pair_lane == side
                x = jnp.where(mine, total[h * new : (h + 1) * new, lanes], 0.0)
                average = jnp.sum(x, axis=-1, keepdims=True) * (1.0 / HEAD)
                centred = jnp.where(mine, x - average, 0.0)
                spread = jnp.sum(centred * centred, axis=-1, keepdims=True) * (1.0 / HEAD)
                result = result + centred * lax.rsqrt(spread + 1e-05)
            gated[at, lanes] = (result * gate[:, lanes]).astype(jnp.bfloat16)

    for p in range(out_ref.shape[0]):
        out_ref[p] = lax.dot_general(
            gated[...],
            w_ref[:, p * width : (p + 1) * width],
            NN,
            preferred_element_type=jnp.float32,
        ).astype(jnp.bfloat16)


def attend(lengths, offsets, branches, keys, values, even, odd, w_out):
    slots, cap, width = keys.shape
    rows = branches.shape[0]
    parts = w_out.shape[1] // width
    smem = pl.BlockSpec(memory_space=pltpu.SMEM)
    vmem = pl.BlockSpec(memory_space=pltpu.VMEM)
    hbm = pl.BlockSpec(memory_space=pl.ANY)
    return pl.pallas_call(
        attend_kernel,
        out_shape=jax.ShapeDtypeStruct((parts, rows, width), jnp.bfloat16),
        in_specs=[smem, smem, vmem, hbm, hbm, hbm, hbm, vmem],
        out_specs=vmem,
        scratch_shapes=[
            pltpu.VMEM((2 * slots, cap, width), jnp.bfloat16),
            pltpu.VMEM((rows, width), jnp.bfloat16),
            pltpu.SemaphoreType.DMA((2 * slots,)),
        ],
        compiler_params=pltpu.CompilerParams(vmem_limit_bytes=32 * 2**20),
        cost_estimate=pl.CostEstimate(
            flops=4 * rows * width * (cap + rows // slots) * (width // HEAD),
            bytes_accessed=4 * slots * cap * width + 4 * rows * width * parts,
            transcendentals=rows * (width // HEAD) * cap,
        ),
    )(lengths, offsets, branches, keys, values, even, odd, w_out)


def on_device(events, norm_gain, w_uvqk, w_out, cache_keys, cache_values, lengths, swap_offset):
    slots, cap, width = cache_keys.shape
    users = lax.axis_size("user")
    heads = lax.axis_size("head")

    live = jnp.arange(cap, dtype=jnp.int32)[None, :] < (lengths * BLOCK)[:, None]
    live_values = jnp.where(live[:, :, None], cache_values, jnp.zeros_like(cache_values))

    def payload(side):
        return jnp.concatenate(
            [
                a.reshape(slots // 2, 2, cap, width)[:, side]
                for a in (cache_keys, live_values)
            ],
            axis=0,
        )

    odd = lax.ppermute(
        payload(1), "user", [(i, (((i + 1) ^ 1) - 1) % users) for i in range(users)]
    )
    even = lax.ppermute(payload(0), "user", [(i, i ^ 1) for i in range(users)])

    gathered = lax.all_to_all(
        jnp.broadcast_to(events[None], (heads,) + events.shape), "head", 0, 0
    )
    w = w_uvqk.reshape(w_uvqk.shape[0], 4 * width)
    branches = project(gathered, norm_gain[None, :], w)
    partial_terms = attend(
        lengths, swap_offset, branches, cache_keys, cache_values, even, odd, w_out
    )
    terms = lax.all_to_all(partial_terms, "head", 0, 0)
    summed = jnp.sum(terms.astype(jnp.float32), axis=0)
    return (events.astype(jnp.float32) + summed).astype(jnp.bfloat16)


def solution(mesh):
    return jax.shard_map(
        on_device,
        mesh=mesh,
        in_specs=(
            P("user", "head"),
            P(),
            P(None, None, "head"),
            P("head", None),
            P("user", None, "head"),
            P("user", None, "head"),
            P("user"),
            P("user"),
        ),
        out_specs=P("user", "head"),
        check_vma=False,
    )
```

time: 143 us -> 71.2 us (0.50)
  the two profiles are of different devices: /device:TPU:1 before, /device:TPU:6 now
where the time goes in v1:
time: 71.2 us; the launch traced here: 70.2 us
  starting transfers between devices  20.6 us (29%)
  blocking collectives  13.4 us (19%)
  waiting for transfers between devices  13.3 us (19%)
  Pallas kernels  11.2 us (16%)
  other arithmetic  6.76 us (9%)
  local copies, waits for them, and re-layouts  4.79 us (7%)
    ppermute x1, starting transfers between devices, on_device(): lax.ppermute(payload(1), 'user', [(i, ((i + 1 ^ 1) - 1) % users) for i in...  13.9 us
    all_to_all x1, blocking collectives, on_device(): terms = lax.all_to_all(partial_terms, 'head', 0, 0)  13.4 us
    pallas_call x1, Pallas kernels, attend(): pl.pallas_call(attend_kernel, out_shape=jax.ShapeDtypeStruct((parts, rows...  8.56 us
    all_to_all x1, waiting for transfers between devices, on_device(): lax.all_to_all(jnp.broadcast_to(events[None], (heads,) + events.shape), '...  6.73 us
    ppermute x1, waiting for transfers between devices, on_device(): lax.ppermute(payload(1), 'user', [(i, ((i + 1 ^ 1) - 1) % users) for i in...  6.61 us
    all_to_all x1, starting transfers between devices, on_device(): lax.all_to_all(jnp.broadcast_to(events[None], (heads,) + events.shape), '...  4.77 us
    unnamed x17, local copies, waits for them, and re-layouts  3.27 us
    concatenate x2, other arithmetic, payload(): jnp.concatenate([a.reshape(slots // 2, 2, cap, width)[:, side] for a in (...  3.03 us
  transfers between devices with their start and end apart: 3, of which 2 were waited for; matrix products, arithmetic and copies ran while one was open for 7% of the time, Pallas kernels for 4%

profile of v1, /device:TPU:6, one launch (start us, length us, event | category | flops | bytes accessed | tf_op | source)
XLA Modules:
  0.0 70.2 jit_solution(14046511698107139373)
XLA Ops:
  0.0 0.7 broadcast_multiply_fusion
  0.7 0.1 iota_compare_fusion
  0.7 0.0 copy-start.1
  0.7 2.1 %broadcast_select_fusion = bf16[8,512,256]{2,1,0:T(8,128)(2,1)S(1)} fusion(bf16[8,512,256]{2,1,0:T(8,128)(2,1)} %values.1, pred[8,512]{1,0:T(8,128)(4,1)S(1)} %iota_compare_fusion), kind=kLoop, calls=%fused_computation.3 | loop fusion | flops 1048576 | bytes 4198400 | tf_op jit(solution)/shard_map/jit(_where)/select_n | solution.py:160
  2.8 0.1 copy-done.1
  3.0 0.4 slice_bitcast_fusion
  3.3 1.5 %pad_maximum_fusion = bf16[8,512,256]{2,1,0:T(8,128)(2,1)} fusion(bf16[4,512,256]{2,1,0:T(8,128)(2,1)S(1)} %get-tuple-element.8, bf16[4,512,256]{2,1,0:T(8,128)(2,1)S(1)} %get-tuple-element.9), kind=kLoop, calls=%fused_computation | loop fusion | flops 1048576 | bytes 4194304 | tf_op jit(solution)/shard_map/concatenate | solution.py:163
  4.8 1.9 %collective-permute-start = (bf16[8,512,256]{2,1,0:T(8,128)(2,1)}, bf16[8,512,256]{2,1,0:T(8,128)(2,1)}, u32[]{:S(2)}, u32[]{:S(2)}) collective-permute-start(bf16[8,512,256]{2,1,0:T(8,128)(2,1)} %pad_maximum_fusion), channel_id=1, source_target_pairs={{0,4},{4,0},{8,12},{12,8},{16,20},{20,16},{24,28},{28,24},{32,36},... | collective-permute-start | bytes 6291464 | tf_op jit(solution)/shard_map/ppermute | solution.py:174
  6.8 0.0 copy-start.7
  6.8 1.5 %pad_maximum_fusion.1 = bf16[8,512,256]{2,1,0:T(8,128)(2,1)} fusion(bf16[4,512,256]{2,1,0:T(8,128)(2,1)S(1)} %get-tuple-element.7, bf16[4,512,256]{2,1,0:T(8,128)(2,1)S(1)} %get-tuple-element.10), kind=kLoop, calls=%fused_computation.1 | loop fusion | flops 1048576 | bytes 4194304 | tf_op jit(solution)/shard_map/concatenate | solution.py:163
  8.3 13.9 %collective-permute-start.1 = (bf16[8,512,256]{2,1,0:T(8,128)(2,1)}, bf16[8,512,256]{2,1,0:T(8,128)(2,1)}, u32[]{:S(2)}, u32[]{:S(2)}) collective-permute-start(bf16[8,512,256]{2,1,0:T(8,128)(2,1)} %pad_maximum_fusion.1), channel_id=1, source_target_pairs={{0,508},{4,8},{8,4},{12,16},{16,12},{20,24},{24,20},{28,32},{32,28... | collective-permute-start | bytes 6291464 | tf_op jit(solution)/shard_map/ppermute | solution.py:171
  22.3 0.0 copy-done.7
  22.3 1.1 %broadcast_in_dim.14 = bf16[4,512,256]{2,1,0:T(8,128)(2,1)} broadcast(bf16[512,256]{1,0:T(8,128)(2,1)S(1)} %copy-done.7), dimensions={1,2} | broadcast | bytes 1310720 | tf_op jit(solution)/shard_map/broadcast_in_dim | solution.py:177
  23.4 4.8 %all-to-all-start = ((bf16[4,512,256]{2,1,0:T(8,128)(2,1)}), bf16[4,512,256]{2,1,0:T(8,128)(2,1)S(1)}, u32[]{:S(2)}, u32[]{:S(2)}) async-start(bf16[4,512,256]{2,1,0:T(8,128)(2,1)} %broadcast_in_dim.14), calls=%async_computation | async-start | bytes 2097152 | tf_op jit(solution)/shard_map/all_to_all | solution.py:176
  28.2 0.0 copy-start.4
  28.2 2.1 %copy.17 = bf16[128,8,4,256]{3,1,2,0:T(8,128)(2,1)S(1)} copy(bf16[128,8,4,256]{3,2,1,0:T(4,128)(2,1)} %bitcast.25) | data formatting | bytes 4194304
  30.3 6.7 %all-to-all-done.x_ref = bf16[4,512,256]{2,1,0:T(8,128)(2,1)S(1)} async-done(((bf16[4,512,256]{2,1,0:T(8,128)(2,1)}), bf16[4,512,256]{2,1,0:T(8,128)(2,1)S(1)}, u32[]{:S(2)}, u32[]{:S(2)}) %all-to-all-start) | async-done | bytes 1048608 | tf_op jit(solution)/shard_map/all_to_all | solution.py:176
  37.0 0.0 copy-done.4
  37.0 0.0 copy-start
  37.0 0.0 copy-start.2
  37.0 0.0 copy-start.5
  37.0 0.0 copy-start.6
  37.0 2.6 %shard_map.82.b_ref = bf16[512,1024]{1,0:T(8,128)(2,1)S(1)} custom-call(bf16[4,512,256]{2,1,0:T(8,128)(2,1)S(1)} %all-to-all-done.x_ref, f32[1,1024]{1,0:T(1,128)S(1)} %bitcast.23, bf16[1024,1024]{1,0:T(8,128)(2,1)S(1)} %bitcast.21), custom_call_target="tpu_custom_call" | custom-call | flops 1073741824 | bytes 4194304 | tf_op jit(solution)/shard_map/pallas_call | solution.py:38
  39.7 0.0 collective-permute-done.even
  39.7 6.6 %collective-permute-done.1.odd = bf16[8,512,256]{2,1,0:T(8,128)(2,1)} collective-permute-done((bf16[8,512,256]{2,1,0:T(8,128)(2,1)}, bf16[8,512,256]{2,1,0:T(8,128)(2,1)}, u32[]{:S(2)}, u32[]{:S(2)}) %collective-permute-start.1) | collective-permute-done | bytes 2097184 | tf_op jit(solution)/shard_map/ppermute | solution.py:171
  46.3 0.0 copy-done
  46.3 0.0 copy-done.2
  46.3 0.0 copy-done.5
  46.3 0.0 copy-done.6
  46.3 0.0 copy-start.3
  46.3 1.0 %copy-done.3 = bf16[256,1024]{1,0:T(8,128)(2,1)S(1)} copy-done((bf16[256,1024]{1,0:T(8,128)(2,1)S(1)}, bf16[256,1024]{1,0:T(8,128)(2,1)}, u32[]{:S(2)}) %copy-start.3) | copy-done | bytes 524312
  47.3 8.6 %shard_map.83 = bf16[4,512,256]{2,1,0:T(8,128)(2,1)S(1)} custom-call(s32[8]{0:T(128)S(1)} %copy-done.5, s32[8]{0:T(128)S(1)} %copy-done.6, bf16[512,1024]{1,0:T(8,128)(2,1)S(1)} %shard_map.82.b_ref, bf16[8,512,256]{2,1,0:T(8,128)(2,1)S(1)} %copy-done.2, bf16[8,512,256]{2,1,0:T(8,128)(2,1)S(1)} %copy-done, bf16[8,512,256]{2,1,0:T(8,128)(2,1)} %collective-permute-done.even, ...), custom_call_target="tpu_custom_call" | custom-call | flops 1207959552 | bytes 6291456 | tf_op jit(solution)/shard_map/pallas_call | solution.py:135
  55.9 13.4 %all_to_all.10 = bf16[4,512,256]{2,1,0:T(8,128)(2,1)S(1)} all-to-all(bf16[4,512,256]{2,1,0:T(8,128)(2,1)S(1)} %shard_map.83), channel_id=1, replica_groups=mesh['user'=128,'head'=4] {'head'}, dimensions={0} | all-to-all | bytes 2097152 | tf_op jit(solution)/shard_map/all_to_all | solution.py:184
  69.3 0.1 convert_reduce_fusion
  69.5 0.8 %add_convert_fusion = bf16[512,256]{1,0:T(8,128)(2,1)} fusion(f32[512,256]{1,0:T(8,128)S(1)} %convert_reduce_fusion, bf16[512,256]{1,0:T(8,128)(2,1)S(1)} %copy-done.7), kind=kLoop, calls=%fused_computation.8 | loop fusion | flops 393216 | bytes 1048576 | tf_op jit(solution)/shard_map/convert_element_type | solution.py:186
Async XLA Ops:
  0.7 2.2 %copy-start.1 = (bf16[8,512,256]{2,1,0:T(8,128)(2,1)S(1)}, bf16[8,512,256]{2,1,0:T(8,128)(2,1)}, u32[]{:S(2)}) copy-start(bf16[8,512,256]{2,1,0:T(8,128)(2,1)} %keys.1) | copy-start | bytes 6291460
  4.8 34.8 %collective-permute-start = (bf16[8,512,256]{2,1,0:T(8,128)(2,1)}, bf16[8,512,256]{2,1,0:T(8,128)(2,1)}, u32[]{:S(2)}, u32[]{:S(2)}) collective-permute-start(bf16[8,512,256]{2,1,0:T(8,128)(2,1)} %pad_maximum_fusion), channel_id=1, source_target_pairs={{0,4},{4,0},{8,12},{12,8},{16,20},{20,16},{24,28},{28,24},{32,36},... | collective-permute-start | bytes 6291464 | tf_op jit(solution)/shard_map/ppermute | solution.py:174
  6.8 15.5 %copy-start.7 = (bf16[512,256]{1,0:T(8,128)(2,1)S(1)}, bf16[512,256]{1,0:T(8,128)(2,1)}, u32[]{:S(2)}) copy-start(bf16[512,256]{1,0:T(8,128)(2,1)} %param.8) | copy-start | bytes 786436
  8.3 38.0 %collective-permute-start.1 = (bf16[8,512,256]{2,1,0:T(8,128)(2,1)}, bf16[8,512,256]{2,1,0:T(8,128)(2,1)}, u32[]{:S(2)}, u32[]{:S(2)}) collective-permute-start(bf16[8,512,256]{2,1,0:T(8,128)(2,1)} %pad_maximum_fusion.1), channel_id=1, source_target_pairs={{0,508},{4,8},{8,4},{12,16},{16,12},{20,24},{24,20},{28,32},{32,28... | collective-permute-start | bytes 6291464 | tf_op jit(solution)/shard_map/ppermute | solution.py:171
  23.4 13.6 %all-to-all-start = ((bf16[4,512,256]{2,1,0:T(8,128)(2,1)}), bf16[4,512,256]{2,1,0:T(8,128)(2,1)S(1)}, u32[]{:S(2)}, u32[]{:S(2)}) async-start(bf16[4,512,256]{2,1,0:T(8,128)(2,1)} %broadcast_in_dim.14), calls=%async_computation | async-start | bytes 2097152 | tf_op jit(solution)/shard_map/all_to_all | solution.py:176
  28.2 8.8 %copy-start.4 = (f32[1024]{0:T(1024)S(1)}, f32[1024]{0:T(1024)}, u32[]{:S(2)}) copy-start(f32[1024]{0:T(1024)} %param.9) | copy-start | bytes 12292
  37.0 9.3 %copy-start = (bf16[8,512,256]{2,1,0:T(8,128)(2,1)S(1)}, bf16[8,512,256]{2,1,0:T(8,128)(2,1)}, u32[]{:S(2)}) copy-start(bf16[8,512,256]{2,1,0:T(8,128)(2,1)} %values.1) | copy-start | bytes 6291460
  37.0 9.3 %copy-start.2 = (bf16[8,512,256]{2,1,0:T(8,128)(2,1)S(1)}, bf16[8,512,256]{2,1,0:T(8,128)(2,1)}, u32[]{:S(2)}) copy-start(bf16[8,512,256]{2,1,0:T(8,128)(2,1)} %keys.1) | copy-start | bytes 6291460
  37.0 9.3 %copy-start.5 = (s32[8]{0:T(128)S(1)}, s32[8]{0:T(128)}, u32[]{:S(2)}) copy-start(s32[8]{0:T(128)} %lengths.1) | copy-start | bytes 100
  37.0 9.3 %copy-start.6 = (s32[8]{0:T(128)S(1)}, s32[8]{0:T(128)}, u32[]{:S(2)}) copy-start(s32[8]{0:T(128)} %offsets.1) | copy-start | bytes 100
  46.3 1.0 %copy-start.3 = (bf16[256,1024]{1,0:T(8,128)(2,1)S(1)}, bf16[256,1024]{1,0:T(8,128)(2,1)}, u32[]{:S(2)}) copy-start(bf16[256,1024]{1,0:T(8,128)(2,1)} %w_ref.1) | copy-start | bytes 1572868

commit v2 on v1

v2 whole, which is shorter than its diff:
```python
import functools

import jax
import jax.numpy as jnp
from jax import lax
from jax.experimental import pallas as pl
from jax.experimental.pallas import tpu as pltpu
from jax.sharding import PartitionSpec as P

HEAD = 64
BLOCK = 128
NT = (((1,), (1,)), ((), ()))
NN = (((1,), (0,)), ((), ()))
VMEM = pl.BlockSpec(memory_space=pltpu.VMEM)
SMEM = pl.BlockSpec(memory_space=pltpu.SMEM)
HBM = pl.BlockSpec(memory_space=pltpu.HBM)
ANY = pl.BlockSpec(memory_space=pl.ANY)


def gather_pack_kernel(side, lengths, events, keys, values, pay_ref, all_ref, sems):
    half_slots = keys.shape[0] // 2
    parts = all_ref.shape[0]
    value_copies, others = [], []
    for s in range(half_slots):
        j = 2 * s + side
        value_copies.append(
            pltpu.make_async_copy(values.at[j], pay_ref.at[half_slots + s], sems.at[s])
        )
        others.append(pltpu.make_async_copy(keys.at[j], pay_ref.at[s], sems.at[half_slots + s]))
    for p in range(parts):
        others.append(
            pltpu.make_async_copy(events, all_ref.at[p], sems.at[2 * half_slots + p])
        )
    for c in value_copies + others:
        c.start()
    clear_dead(side, lengths, value_copies, pay_ref)
    for c in others:
        c.wait()


def pack_kernel(side, lengths, keys, values, pay_ref, sems):
    half_slots = keys.shape[0] // 2
    value_copies, others = [], []
    for s in range(half_slots):
        j = 2 * s + side
        value_copies.append(
            pltpu.make_async_copy(values.at[j], pay_ref.at[half_slots + s], sems.at[s])
        )
        others.append(pltpu.make_async_copy(keys.at[j], pay_ref.at[s], sems.at[half_slots + s]))
    for c in value_copies + others:
        c.start()
    clear_dead(side, lengths, value_copies, pay_ref)
    for c in others:
        c.wait()


def clear_dead(side, lengths, value_copies, pay_ref):
    half_slots, cap, width = pay_ref.shape[0] // 2, pay_ref.shape[1], pay_ref.shape[2]
    for s in range(half_slots):
        value_copies[s].wait()
        for block in range(1, cap // BLOCK):

            @pl.when(lengths[2 * s + side] <= block)
            def _():
                pay_ref[half_slots + s, block * BLOCK : (block + 1) * BLOCK, :] = jnp.zeros(
                    (BLOCK, width), pay_ref.dtype
                )


def gather_pack(side, parts, lengths, events, keys, values):
    slots, cap, width = keys.shape
    return pl.pallas_call(
        functools.partial(gather_pack_kernel, side),
        out_shape=(
            jax.ShapeDtypeStruct((slots, cap, width), keys.dtype),
            jax.ShapeDtypeStruct((parts,) + events.shape, events.dtype),
        ),
        in_specs=[SMEM, HBM, HBM, HBM],
        out_specs=(VMEM, VMEM),
        scratch_shapes=[pltpu.SemaphoreType.DMA((slots + parts,))],
        compiler_params=pltpu.CompilerParams(vmem_limit_bytes=6 * 2**20),
        cost_estimate=pl.CostEstimate(
            flops=0, bytes_accessed=4 * slots * cap * width, transcendentals=0
        ),
    )(lengths, events, keys, values)


def pack(side, lengths, keys, values):
    slots, cap, width = keys.shape
    return pl.pallas_call(
        functools.partial(pack_kernel, side),
        out_shape=jax.ShapeDtypeStruct((slots, cap, width), keys.dtype),
        in_specs=[SMEM, HBM, HBM],
        out_specs=VMEM,
        scratch_shapes=[pltpu.SemaphoreType.DMA((slots,))],
        compiler_params=pltpu.CompilerParams(vmem_limit_bytes=6 * 2**20),
    )(lengths, keys, values)


def cache_copies(side, offsets, keys, values, moved, kv, sems):
    half_slots = kv.shape[0] // 2
    waits = []
    for s in range(half_slots):
        j = 2 * s + side
        own = (
            pltpu.make_async_copy(keys.at[j], kv.at[s], sems.at[s]),
            pltpu.make_async_copy(values.at[j], kv.at[half_slots + s], sems.at[half_slots + s]),
        )
        traded = (
            pltpu.make_async_copy(moved.at[s], kv.at[s], sems.at[s]),
            pltpu.make_async_copy(
                moved.at[half_slots + s], kv.at[half_slots + s], sems.at[half_slots + s]
            ),
        )

        @pl.when(offsets[j] == 0)
        def _():
            for c in own:
                c.start()

        @pl.when(offsets[j] != 0)
        def _():
            for c in traded:
                c.start()

        waits.append(own)
    return waits


def attend_slots(side, lengths, offsets, b_ref, kv, waits, gated):
    half_slots, cap, width = kv.shape[0] // 2, kv.shape[1], kv.shape[2]
    new = b_ref.shape[0] // half_slots
    heads = width // HEAD
    lane_head = lax.broadcasted_iota(jnp.int32, (new, width), 1) // HEAD
    position = lax.broadcasted_iota(jnp.int32, (1, cap), 1)
    row = lax.broadcasted_iota(jnp.int32, (heads * new, new), 0) % new
    causal = row >= lax.broadcasted_iota(jnp.int32, (heads * new, new), 1)
    pair_lane = lax.broadcasted_iota(jnp.int32, (new, 2 * HEAD), 1) // HEAD

    def weigh(s):
        j = 2 * s + side
        at = slice(s * new, (s + 1) * new)
        queries = b_ref[at, 2 * width : 3 * width] * jnp.bfloat16(0.5 * HEAD**-0.5)
        fresh_keys = b_ref[at, 3 * width :]
        zero = jnp.zeros_like(queries)
        spread_q = jnp.concatenate(
            [jnp.where(lane_head == h, queries, zero) for h in range(heads)], axis=0
        )
        used = jnp.where(offsets[j] == 0, lengths[j] * BLOCK, cap)
        half = lax.dot_general(spread_q, kv[s], NT, preferred_element_type=jnp.float32)
        cached = jnp.where(position < used, half + half * jnp.tanh(half), 0.0)
        half = lax.dot_general(spread_q, fresh_keys, NT, preferred_element_type=jnp.float32)
        fresh = jnp.where(causal, half + half * jnp.tanh(half), 0.0)
        return cached.astype(jnp.bfloat16), fresh.astype(jnp.bfloat16)

    def finish(s, cached, fresh):
        at = slice(s * new, (s + 1) * new)
        gate = b_ref[at, :width].astype(jnp.float32)
        fresh_values = b_ref[at, width : 2 * width]
        total = lax.dot_general(
            cached, kv[half_slots + s], NN, preferred_element_type=jnp.float32
        )
        total = total + lax.dot_general(
            fresh, fresh_values, NN, preferred_element_type=jnp.float32
        )
        for pair in range(heads // 2):
            lanes = slice(2 * HEAD * pair, 2 * HEAD * (pair + 1))
            result = jnp.zeros((new, 2 * HEAD), jnp.float32)
            for within in range(2):
                h = 2 * pair + within
                mine = pair_lane == within
                x = jnp.where(mine, total[h * new : (h + 1) * new, lanes], 0.0)
                average = jnp.sum(x, axis=-1, keepdims=True) * (1.0 / HEAD)
                centred = jnp.where(mine, x - average, 0.0)
                spread = jnp.sum(centred * centred, axis=-1, keepdims=True) * (1.0 / HEAD)
                result = result + centred * lax.rsqrt(spread + 1e-05)
            gated[at, lanes] = (result * gate[:, lanes]).astype(jnp.bfloat16)

    for c in [pair[0] for pair in waits]:
        c.wait()
    weights = [weigh(s) for s in range(half_slots)]
    for c in [pair[1] for pair in waits]:
        c.wait()
    for s in range(half_slots):
        finish(s, *weights[s])


def project_out(gated, w_ref, out_ref, width):
    for p in range(out_ref.shape[0]):
        out_ref[p] = lax.dot_general(
            gated[...],
            w_ref[:, p * width : (p + 1) * width],
            NN,
            preferred_element_type=jnp.float32,
        ).astype(jnp.bfloat16)


def first_kernel(
    lengths, offsets, x_hbm, gain_ref, w_hbm, keys, values, moved, wo_hbm,
    out_ref, odd_hbm,
    x_ref, w_ref, wo_ref, kv, even_ref, odd_ref, gated, x_sems, w_sems, kv_sems,
):
    parts, total, width = x_ref.shape
    slots = keys.shape[0]
    new = total // slots
    features = parts * width
    chunks = x_sems.shape[0]
    rows = total // chunks
    x_copies = []
    for i in range(chunks):
        at = pl.ds(i * rows, rows)
        x_copies.append(pltpu.make_async_copy(x_hbm.at[:, at, :], x_ref.at[:, at, :], x_sems.at[i]))
    w_copy = pltpu.make_async_copy(w_hbm, w_ref, w_sems.at[0])
    wo_copy = pltpu.make_async_copy(wo_hbm, wo_ref, w_sems.at[1])
    x_copies[0].start()
    w_copy.start()
    for c in x_copies[1:]:
        c.start()
    waits = cache_copies(0, offsets, keys, values, moved, kv, kv_sems)
    wo_copy.start()
    gain = gain_ref[...]

    def normalise(i):
        x = jnp.concatenate(
            [x_ref[p, i * rows : (i + 1) * rows, :] for p in range(parts)], axis=1
        ).astype(jnp.float32)
        average = jnp.sum(x, axis=-1, keepdims=True) * (1.0 / features)
        centred = x - average
        spread = jnp.sum(centred * centred, axis=-1, keepdims=True) * (1.0 / features)
        return (centred * lax.rsqrt(spread + 1e-05) * gain).astype(jnp.bfloat16)

    for i in range(chunks):
        x_copies[i].wait()
        normed = normalise(i)
        if i == 0:
            w_copy.wait()
        half = 0.5 * lax.dot_general(normed, w_ref[...], NN, preferred_element_type=jnp.float32)
        branch = (half + half * jnp.tanh(half)).astype(jnp.bfloat16)
        for k in range(rows // new):
            j = i * (rows // new) + k
            target = odd_ref if j % 2 else even_ref
            target[(j // 2) * new : (j // 2 + 1) * new, :] = branch[k * new : (k + 1) * new, :]

    odd_copy = pltpu.make_async_copy(odd_ref, odd_hbm, w_sems.at[2])
    odd_copy.start()
    attend_slots(0, lengths, offsets, even_ref, kv, waits, gated)
    wo_copy.wait()
    project_out(gated, wo_ref, out_ref, width)
    odd_copy.wait()


def second_kernel(
    lengths, offsets, b_hbm, keys, values, moved, wo_hbm, out_ref, b_ref, wo_ref, kv, gated, sems, kv_sems
):
    width = keys.shape[2]
    waits = cache_copies(1, offsets, keys, values, moved, kv, kv_sems)
    b_copy = pltpu.make_async_copy(b_hbm, b_ref, sems.at[0])
    wo_copy = pltpu.make_async_copy(wo_hbm, wo_ref, sems.at[1])
    b_copy.start()
    wo_copy.start()
    b_copy.wait()
    attend_slots(1, lengths, offsets, b_ref, kv, waits, gated)
    wo_copy.wait()
    project_out(gated, wo_ref, out_ref, width)


def attention_flops(rows, new, cap, width):
    return 4 * rows * width * (cap + new) * (width // HEAD)


def first(lengths, offsets, x4, gain, w, keys, values, moved, w_out):
    slots, cap, width = keys.shape
    parts, total, _ = x4.shape
    half, new, wide = total // 2, total // slots, w.shape[1]
    bf16 = jnp.bfloat16
    return pl.pallas_call(
        first_kernel,
        out_shape=(
            jax.ShapeDtypeStruct((parts, half, width), bf16),
            jax.ShapeDtypeStruct((half, wide), bf16),
        ),
        in_specs=[SMEM, SMEM, ANY, VMEM, HBM, HBM, HBM, HBM, HBM],
        out_specs=(VMEM, HBM),
        scratch_shapes=[
            pltpu.VMEM(x4.shape, bf16),
            pltpu.VMEM(w.shape, bf16),
            pltpu.VMEM(w_out.shape, bf16),
            pltpu.VMEM((slots, cap, width), bf16),
            pltpu.VMEM((half, wide), bf16),
            pltpu.VMEM((half, wide), bf16),
            pltpu.VMEM((half, width), bf16),
            pltpu.SemaphoreType.DMA((4,)),
            pltpu.SemaphoreType.DMA((3,)),
            pltpu.SemaphoreType.DMA((slots,)),
        ],
        compiler_params=pltpu.CompilerParams(vmem_limit_bytes=40 * 2**20),
        cost_estimate=pl.CostEstimate(
            flops=2 * total * w.size + attention_flops(half, new, cap, width),
            bytes_accessed=2 * (w.size + x4.size) + 4 * slots * cap * width,
            transcendentals=total * wide,
        ),
    )(lengths, offsets, x4, gain, in_hbm(w), in_hbm(keys), in_hbm(values), in_hbm(moved), in_hbm(w_out))


def second(lengths, offsets, branches, keys, values, moved, w_out):
    slots, cap, width = keys.shape
    half, wide = branches.shape
    parts = w_out.shape[1] // width
    bf16 = jnp.bfloat16
    return pl.pallas_call(
        second_kernel,
        out_shape=jax.ShapeDtypeStruct((parts, half, width), bf16),
        in_specs=[SMEM, SMEM, ANY, HBM, HBM, HBM, HBM],
        out_specs=VMEM,
        scratch_shapes=[
            pltpu.VMEM(branches.shape, bf16),
            pltpu.VMEM(w_out.shape, bf16),
            pltpu.VMEM((slots, cap, width), bf16),
            pltpu.VMEM((half, width), bf16),
            pltpu.SemaphoreType.DMA((2,)),
            pltpu.SemaphoreType.DMA((slots,)),
        ],
        compiler_params=pltpu.CompilerParams(vmem_limit_bytes=40 * 2**20),
        cost_estimate=pl.CostEstimate(
            flops=attention_flops(half, 2 * half // slots, cap, width),
            bytes_accessed=4 * slots * cap * width + 2 * branches.size,
            transcendentals=half * (width // HEAD) * cap,
        ),
    )(lengths, offsets, branches, in_hbm(keys), in_hbm(values), in_hbm(moved), in_hbm(w_out))


def combine_kernel(events, even, odd, out_ref):
    parts, new, _ = even.shape
    for side, terms in enumerate((even, odd)):
        at = slice(side * new, (side + 1) * new)
        total = terms[0].astype(jnp.float32)
        for p in range(1, parts):
            total = total + terms[p].astype(jnp.float32)
        out_ref[at, :] = (events[at, :].astype(jnp.float32) + total).astype(out_ref.dtype)


def combine(slots, events, even, odd):
    rows, width = events.shape
    parts, new = even.shape[0], rows // slots
    terms = pl.BlockSpec((parts, new, width), lambda i: (0, i, 0))
    own = pl.BlockSpec((2 * new, width), lambda i: (i, 0))
    return pl.pallas_call(
        combine_kernel,
        grid=(slots // 2,),
        out_shape=jax.ShapeDtypeStruct(events.shape, events.dtype),
        in_specs=[own, terms, terms],
        out_specs=own,
        compiler_params=pltpu.CompilerParams(vmem_limit_bytes=40 * 2**20),
    )(in_hbm(events), in_hbm(even), in_hbm(odd))


def in_hbm(array):
    return pltpu.with_memory_space_constraint(array, pltpu.HBM)


def on_device(events, norm_gain, w_uvqk, w_out, cache_keys, cache_values, lengths, swap_offset):
    slots, cap, width = cache_keys.shape
    users = lax.axis_size("user")
    heads = lax.axis_size("head")

    odd_pay, spread_events = gather_pack(
        1, heads, lengths, in_hbm(events), in_hbm(cache_keys), in_hbm(cache_values)
    )
    odd = lax.ppermute(
        odd_pay, "user", [(i, (((i + 1) ^ 1) - 1) % users) for i in range(users)]
    )
    gathered = lax.all_to_all(spread_events, "head", 0, 0)
    w = w_uvqk.reshape(w_uvqk.shape[0], 4 * width)
    later_lengths, _ = lax.optimization_barrier((lengths, spread_events))
    even_pay = pack(0, later_lengths, in_hbm(cache_keys), in_hbm(cache_values))
    even = lax.ppermute(even_pay, "user", [(i, i ^ 1) for i in range(users)])

    even_part, odd_branches = first(
        lengths, swap_offset, gathered, norm_gain[None, :], w, cache_keys, cache_values, even, w_out
    )
    even_terms = lax.all_to_all(even_part, "head", 0, 0)
    odd_part = second(
        lengths, swap_offset, odd_branches, cache_keys, cache_values, odd, w_out
    )
    odd_part, even_terms = lax.optimization_barrier((odd_part, even_terms))
    odd_terms = lax.all_to_all(odd_part, "head", 0, 0)
    return combine(slots, events, even_terms, odd_terms)


def solution(mesh):
    return jax.shard_map(
        on_device,
        mesh=mesh,
        in_specs=(
            P("user", "head"),
            P(),
            P(None, None, "head"),
            P("head", None),
            P("user", None, "head"),
            P("user", None, "head"),
            P("user"),
            P("user"),
        ),
        out_specs=P("user", "head"),
        check_vma=False,
    )
```

time: 71.2 us -> 72.4 us (1.017)
  Pallas kernels: 11.2 us -> 20.4 us
  other arithmetic: 6.76 us -> 0 us
  starting transfers between devices: 20.6 us -> 26.2 us
  waiting for transfers between devices: 13.3 us -> 9.2 us
  blocking collectives: 13.4 us -> 11.2 us
    pallas_call x2 -> x5, Pallas kernels: 11.2 us -> 20.4 us  [the longest x1 7.2 us: first(): pl.pallas_call(first_kernel, out_shape=(jax.ShapeDtypeStruct((parts, half...]
    ppermute x2, waiting for transfers between devices: 6.61 us -> 0.01 us  [the longest x1 0.01 us: on_device(): lax.ppermute(odd_pay, 'user', [(i, ((i + 1 ^ 1) - 1) % users) for i in ra...]
    all_to_all x1 -> x2, starting transfers between devices: 4.77 us -> 10.3 us  [the longest x1 5.53 us: on_device(): even_terms = lax.all_to_all(even_part, 'head', 0, 0)]
    concatenate x2 -> x0, other arithmetic: 3.03 us -> none  [payload(): jnp.concatenate([a.reshape(slots // 2, 2, cap, width)[:, side] for a in (...]
    all_to_all x1 -> x2, waiting for transfers between devices: 6.73 us -> 9.2 us  [the longest x1 5.34 us: on_device(): gathered = lax.all_to_all(spread_events, 'head', 0, 0)]
    all_to_all x1, blocking collectives: 13.4 us -> 11.2 us  [on_device(): odd_terms = lax.all_to_all(odd_part, 'head', 0, 0)]
    select_n x1 -> x0, other arithmetic: 2.09 us -> none  [on_device(): jnp.where(live[:, :, None], cache_values, jnp.zeros_like(cache_values))]
    broadcast_in_dim x1 -> x0, local copies, waits for them, and re-layouts: 1.14 us -> none  [on_device(): jnp.broadcast_to(events[None], (heads,) + events.shape)]
  transfers between devices with their start and end apart: 3 -> 4, of which waited for: 2 -> 2; matrix products, arithmetic and copies ran while one was open for 7% -> 5% of each run, Pallas kernels for 4% -> 15%
where the time goes in v2:
time: 72.4 us; the launch traced here: 71.2 us
  starting transfers between devices  26.2 us (36%)
  Pallas kernels  20.4 us (28%)
  blocking collectives  11.2 us (15%)
  waiting for transfers between devices  9.2 us (13%)
  local copies, waits for them, and re-layouts  4.15 us (6%)
    ppermute x1, starting transfers between devices, on_device(): lax.ppermute(odd_pay, 'user', [(i, ((i + 1 ^ 1) - 1) % users) for i in ra...  14 us
    all_to_all x1, blocking collectives, on_device(): odd_terms = lax.all_to_all(odd_part, 'head', 0, 0)  11.2 us
    pallas_call x1, Pallas kernels, first(): pl.pallas_call(first_kernel, out_shape=(jax.ShapeDtypeStruct((parts, half...  7.2 us
    all_to_all x1, starting transfers between devices, on_device(): even_terms = lax.all_to_all(even_part, 'head', 0, 0)  5.53 us
    all_to_all x1, waiting for transfers between devices, on_device(): gathered = lax.all_to_all(spread_events, 'head', 0, 0)  5.34 us
    all_to_all x1, starting transfers between devices, on_device(): gathered = lax.all_to_all(spread_events, 'head', 0, 0)  4.78 us
    unnamed x13, local copies, waits for them, and re-layouts  4.15 us
    pallas_call x1, Pallas kernels, gather_pack(): pl.pallas_call(functools.partial(gather_pack_kernel, side), out_shape=(ja...  4.02 us
  transfers between devices with their start and end apart: 4, of which 2 were waited for; matrix products, arithmetic and copies ran while one was open for 5% of the time, Pallas kernels for 15%

profile of v2, /device:TPU:6, one launch (start us, length us, event | category | flops | bytes accessed | tf_op | source)
XLA Modules:
  0.0 71.2 jit_solution(1221279764034221257)
XLA Ops:
  0.0 0.0 copy-start.1
  0.0 0.7 copy-done.1
  0.7 4.0 %shard_map.82 = (bf16[8,512,256]{2,1,0:T(8,128)(2,1)}, bf16[4,512,256]{2,1,0:T(8,128)(2,1)S(1)}) custom-call(s32[8]{0:T(128)S(1)} %copy-done.1, bf16[512,256]{1,0:T(8,128)(2,1)} %events.3, bf16[8,512,256]{2,1,0:T(8,128)(2,1)} %keys.7, bf16[8,512,256]{2,1,0:T(8,128)(2,1)} %values.7), custom_call_target="tpu_custom_call" | custom-call | bytes 4194304 | tf_op jit(solution)/shard_map/pallas_call | solution.py:72
  4.7 0.0 copy-start
  4.7 2.1 %shard_map.83 = bf16[8,512,256]{2,1,0:T(8,128)(2,1)S(1)} custom-call(s32[8]{0:T(128)S(1)} %copy-done.1, bf16[8,512,256]{2,1,0:T(8,128)(2,1)} %keys.7, bf16[8,512,256]{2,1,0:T(8,128)(2,1)} %values.7), custom_call_target="tpu_custom_call" | custom-call | tf_op jit(solution)/shard_map/pallas_call | solution.py:90
  6.8 0.0 copy-done
  6.8 1.9 %collective-permute-start = (bf16[8,512,256]{2,1,0:T(8,128)(2,1)S(1)}, bf16[8,512,256]{2,1,0:T(8,128)(2,1)}, u32[]{:S(2)}, u32[]{:S(2)}) collective-permute-start(bf16[8,512,256]{2,1,0:T(8,128)(2,1)S(1)} %shard_map.83), channel_id=1, source_target_pairs={{0,4},{4,0},{8,12},{12,8},{16,20},{20,16},{24,28},{28,24},{32,36},... | collective-permute-start | bytes 6291464 | tf_op jit(solution)/shard_map/ppermute | solution.py:376
  8.8 14.0 %collective-permute-start.1 = (bf16[8,512,256]{2,1,0:T(8,128)(2,1)}, bf16[8,512,256]{2,1,0:T(8,128)(2,1)}, u32[]{:S(2)}, u32[]{:S(2)}) collective-permute-start(bf16[8,512,256]{2,1,0:T(8,128)(2,1)} %get-tuple-element.15), channel_id=1, source_target_pairs={{0,508},{4,8},{8,4},{12,16},{16,12},{20,24},{24,20},{28,32},{32,28... | collective-permute-start | bytes 6291464 | tf_op jit(solution)/shard_map/ppermute | solution.py:369
  22.7 4.8 %all-to-all-start = ((bf16[4,512,256]{2,1,0:T(8,128)(2,1)}), bf16[4,512,256]{2,1,0:T(8,128)(2,1)S(1)}, u32[]{:S(2)}, u32[]{:S(2)}) async-start(bf16[4,512,256]{2,1,0:T(8,128)(2,1)} %copy-done), calls=%async_computation | async-start | bytes 2097152 | tf_op jit(solution)/shard_map/all_to_all | solution.py:372
  27.5 0.0 copy-start.2
  27.5 0.0 copy-start.3
  27.5 0.0 copy-start.4
  27.5 3.5 %copy.9 = bf16[128,8,4,256]{3,1,2,0:T(8,128)(2,1)} copy(bf16[128,8,4,256]{3,2,1,0:T(4,128)(2,1)} %bitcast.5) | data formatting | bytes 4194304
  31.0 5.3 %all-to-all-done.x_hbm = bf16[4,512,256]{2,1,0:T(8,128)(2,1)S(1)} async-done(((bf16[4,512,256]{2,1,0:T(8,128)(2,1)}), bf16[4,512,256]{2,1,0:T(8,128)(2,1)S(1)}, u32[]{:S(2)}, u32[]{:S(2)}) %all-to-all-start) | async-done | bytes 1048608 | tf_op jit(solution)/shard_map/all_to_all | solution.py:372
  36.3 0.0 collective-permute-done.moved
  36.3 0.0 copy-done.2
  36.3 0.0 copy-done.3
  36.3 0.0 copy-done.4
  36.4 7.2 %shard_map.84 = (bf16[4,256,256]{2,1,0:T(8,128)(2,1)}, bf16[256,1024]{1,0:T(8,128)(2,1)S(1)}) custom-call(s32[8]{0:T(128)S(1)} %copy-done.2, s32[8]{0:T(128)S(1)} %copy-done.4, bf16[4,512,256]{2,1,0:T(8,128)(2,1)S(1)} %all-to-all-done.x_hbm, f32[1,1024]{1,0:T(1,128)S(1)} %bitcast.3, bf16[1024,1024]{1,0:T(8,128)(2,1)} %bitcast.4, bf16[8,512,256]{2,1,0:T(8,128)(2,1)} %keys.7, ...), custom_call_target="tpu_custom_call" | custom-call | flops 1677721600 | bytes 7340032 | tf_op jit(solution)/shard_map/pallas_call | solution.py:276
  43.6 5.5 %all-to-all-start.1 = ((bf16[4,256,256]{2,1,0:T(8,128)(2,1)}), bf16[4,256,256]{2,1,0:T(8,128)(2,1)S(1)}, u32[]{:S(2)}, u32[]{:S(2)}) async-start(bf16[4,256,256]{2,1,0:T(8,128)(2,1)} %get-tuple-element.16), calls=%async_computation.1 | async-start | bytes 1048576 | tf_op jit(solution)/shard_map/all_to_all | solution.py:381
  49.1 0.0 collective-permute-done.1.moved
  49.1 3.7 %shard_map.85 = bf16[4,256,256]{2,1,0:T(8,128)(2,1)S(1)} custom-call(s32[8]{0:T(128)S(1)} %copy-done.2, s32[8]{0:T(128)S(1)} %copy-done.4, bf16[256,1024]{1,0:T(8,128)(2,1)S(1)} %get-tuple-element.14.b_hbm, bf16[8,512,256]{2,1,0:T(8,128)(2,1)} %keys.7, bf16[8,512,256]{2,1,0:T(8,128)(2,1)} %values.7, bf16[8,512,256]{2,1,0:T(8,128)(2,1)} %collective-permute-done.1.moved, ...), custom_call_target="tpu_custom_call" | custom-call | flops 603979776 | bytes 4718592 | tf_op jit(solution)/shard_map/pallas_call | solution.py:310
  52.8 3.9 %all-to-all-done.1.even = bf16[4,256,256]{2,1,0:T(8,128)(2,1)S(1)} async-done(((bf16[4,256,256]{2,1,0:T(8,128)(2,1)}), bf16[4,256,256]{2,1,0:T(8,128)(2,1)S(1)}, u32[]{:S(2)}, u32[]{:S(2)}) %all-to-all-start.1) | async-done | bytes 524320 | tf_op jit(solution)/shard_map/all_to_all | solution.py:381
  56.7 0.0 copy-start.5
  56.7 11.2 %all_to_all.15.odd = bf16[4,256,256]{2,1,0:T(8,128)(2,1)} all-to-all(bf16[4,256,256]{2,1,0:T(8,128)(2,1)S(1)} %shard_map.85), channel_id=1, replica_groups=mesh['user'=128,'head'=4] {'head'}, dimensions={0} | all-to-all | bytes 1048576 | tf_op jit(solution)/shard_map/all_to_all | solution.py:386
  67.8 0.0 copy-done.5
  67.8 3.4 %shard_map.86 = bf16[512,256]{1,0:T(8,128)(2,1)} custom-call(bf16[512,256]{1,0:T(8,128)(2,1)} %events.3, bf16[4,256,256]{2,1,0:T(8,128)(2,1)} %copy-done.5, bf16[4,256,256]{2,1,0:T(8,128)(2,1)} %all_to_all.15.odd), custom_call_target="tpu_custom_call" | custom-call | tf_op jit(solution)/shard_map/pallas_call | solution.py:347
Async XLA Ops:
  0.0 0.7 copy-start.1
  4.7 2.1 %copy-start = (bf16[4,512,256]{2,1,0:T(8,128)(2,1)}, bf16[4,512,256]{2,1,0:T(8,128)(2,1)S(1)}, u32[]{:S(2)}) copy-start(bf16[4,512,256]{2,1,0:T(8,128)(2,1)S(1)} %get-tuple-element.12) | copy-start | bytes 3145732
  6.8 29.5 %collective-permute-start = (bf16[8,512,256]{2,1,0:T(8,128)(2,1)S(1)}, bf16[8,512,256]{2,1,0:T(8,128)(2,1)}, u32[]{:S(2)}, u32[]{:S(2)}) collective-permute-start(bf16[8,512,256]{2,1,0:T(8,128)(2,1)S(1)} %shard_map.83), channel_id=1, source_target_pairs={{0,4},{4,0},{8,12},{12,8},{16,20},{20,16},{24,28},{28,24},{32,36},... | collective-permute-start | bytes 6291464 | tf_op jit(solution)/shard_map/ppermute | solution.py:376
  8.8 40.3 %collective-permute-start.1 = (bf16[8,512,256]{2,1,0:T(8,128)(2,1)}, bf16[8,512,256]{2,1,0:T(8,128)(2,1)}, u32[]{:S(2)}, u32[]{:S(2)}) collective-permute-start(bf16[8,512,256]{2,1,0:T(8,128)(2,1)} %get-tuple-element.15), channel_id=1, source_target_pairs={{0,508},{4,8},{8,4},{12,16},{16,12},{20,24},{24,20},{28,32},{32,28... | collective-permute-start | bytes 6291464 | tf_op jit(solution)/shard_map/ppermute | solution.py:369
  22.7 13.6 %all-to-all-start = ((bf16[4,512,256]{2,1,0:T(8,128)(2,1)}), bf16[4,512,256]{2,1,0:T(8,128)(2,1)S(1)}, u32[]{:S(2)}, u32[]{:S(2)}) async-start(bf16[4,512,256]{2,1,0:T(8,128)(2,1)} %copy-done), calls=%async_computation | async-start | bytes 2097152 | tf_op jit(solution)/shard_map/all_to_all | solution.py:372
  27.5 8.8 %copy-start.2 = (s32[8]{0:T(128)S(1)}, s32[8]{0:T(128)}, u32[]{:S(2)}) copy-start(s32[8]{0:T(128)} %lengths.6) | copy-start | bytes 100
  27.5 8.8 %copy-start.3 = (f32[1024]{0:T(1024)S(1)}, f32[1024]{0:T(1024)}, u32[]{:S(2)}) copy-start(f32[1024]{0:T(1024)} %param.9) | copy-start | bytes 12292
  27.5 8.8 %copy-start.4 = (s32[8]{0:T(128)S(1)}, s32[8]{0:T(128)}, u32[]{:S(2)}) copy-start(s32[8]{0:T(128)} %offsets.3) | copy-start | bytes 100
  43.6 13.1 %all-to-all-start.1 = ((bf16[4,256,256]{2,1,0:T(8,128)(2,1)}), bf16[4,256,256]{2,1,0:T(8,128)(2,1)S(1)}, u32[]{:S(2)}, u32[]{:S(2)}) async-start(bf16[4,256,256]{2,1,0:T(8,128)(2,1)} %get-tuple-element.16), calls=%async_computation.1 | async-start | bytes 1048576 | tf_op jit(solution)/shard_map/all_to_all | solution.py:381
  56.7 11.2 %copy-start.5 = (bf16[4,256,256]{2,1,0:T(8,128)(2,1)}, bf16[4,256,256]{2,1,0:T(8,128)(2,1)S(1)}, u32[]{:S(2)}) copy-start(bf16[4,256,256]{2,1,0:T(8,128)(2,1)S(1)} %all-to-all-done.1.even) | copy-start | bytes 1572868

commit v3 on v1

v3 whole, which is shorter than its diff:
```python
import functools

import jax
import jax.numpy as jnp
from jax import lax
from jax.experimental import pallas as pl
from jax.experimental.pallas import tpu as pltpu
from jax.sharding import PartitionSpec as P

HEAD = 64
BLOCK = 128
NT = (((1,), (1,)), ((), ()))
NN = (((1,), (0,)), ((), ()))
VMEM = pl.BlockSpec(memory_space=pltpu.VMEM)
SMEM = pl.BlockSpec(memory_space=pltpu.SMEM)
HBM = pl.BlockSpec(memory_space=pltpu.HBM)
ANY = pl.BlockSpec(memory_space=pl.ANY)


def pack_kernel(side, lengths, keys, values, *rest):
    *pays, buf, in_sems, out_sems = rest
    half_slots, cap, width = keys.shape[0] // 2, keys.shape[1], keys.shape[2]
    places = [pay.at[s] for pay in pays for s in range(pay.shape[0])]
    arrive, leave = [], []
    for s in range(half_slots):
        j = 2 * s + side
        for array, slot in ((values, half_slots + s), (keys, s)):
            arrive.append(pltpu.make_async_copy(array.at[j], buf.at[slot], in_sems.at[slot]))
            leave.append(pltpu.make_async_copy(buf.at[slot], places[slot], out_sems.at[slot]))
    for c in arrive:
        c.start()
    for i, c in enumerate(arrive):
        c.wait()
        if i % 2 == 0:
            s = i // 2
            for block in range(1, cap // BLOCK):

                @pl.when(lengths[2 * s + side] <= block)
                def _():
                    buf[half_slots + s, block * BLOCK : (block + 1) * BLOCK, :] = jnp.zeros(
                        (BLOCK, width), buf.dtype
                    )

        leave[i].start()
    for c in leave:
        c.wait()


def pack(side, pieces, lengths, keys, values):
    slots, cap, width = keys.shape
    return pl.pallas_call(
        functools.partial(pack_kernel, side),
        out_shape=[jax.ShapeDtypeStruct((slots // pieces, cap, width), keys.dtype)] * pieces,
        in_specs=[SMEM, HBM, HBM],
        out_specs=[HBM] * pieces,
        scratch_shapes=[
            pltpu.VMEM((slots, cap, width), keys.dtype),
            pltpu.SemaphoreType.DMA((slots,)),
            pltpu.SemaphoreType.DMA((slots,)),
        ],
        compiler_params=pltpu.CompilerParams(vmem_limit_bytes=6 * 2**20),
        cost_estimate=pl.CostEstimate(
            flops=0, bytes_accessed=4 * 10**6 if side else 15 * 10**6, transcendentals=0
        ),
    )(lengths, in_hbm(keys), in_hbm(values))


def project_kernel(x_any, gain_ref, w_any, b_ref, x_ref, w_ref, x_sems, w_sem):
    parts, total, width = x_ref.shape
    features = parts * width
    chunks = x_sems.shape[0]
    rows = total // chunks
    x_copies = []
    for i in range(chunks):
        at = pl.ds(i * rows, rows)
        x_copies.append(
            pltpu.make_async_copy(x_any.at[:, at, :], x_ref.at[:, at, :], x_sems.at[i])
        )
    w_copy = pltpu.make_async_copy(w_any, w_ref, w_sem.at[0])
    x_copies[0].start()
    w_copy.start()
    for c in x_copies[1:]:
        c.start()
    gain = gain_ref[...]

    def normalise(i):
        x = jnp.concatenate(
            [x_ref[p, i * rows : (i + 1) * rows, :] for p in range(parts)], axis=1
        ).astype(jnp.float32)
        average = jnp.sum(x, axis=-1, keepdims=True) * (1.0 / features)
        centred = x - average
        spread = jnp.sum(centred * centred, axis=-1, keepdims=True) * (1.0 / features)
        return (centred * lax.rsqrt(spread + 1e-05) * gain).astype(jnp.bfloat16)

    for i in range(chunks):
        x_copies[i].wait()
        normed = normalise(i)
        if i == 0:
            w_copy.wait()
        half = 0.5 * lax.dot_general(normed, w_ref[...], NN, preferred_element_type=jnp.float32)
        b_ref[i * rows : (i + 1) * rows, :] = (half + half * jnp.tanh(half)).astype(jnp.bfloat16)


def project(x4, gain, w):
    parts, total, width = x4.shape
    return pl.pallas_call(
        project_kernel,
        out_shape=jax.ShapeDtypeStruct((total, w.shape[1]), jnp.bfloat16),
        in_specs=[ANY, VMEM, ANY],
        out_specs=VMEM,
        scratch_shapes=[
            pltpu.VMEM(x4.shape, jnp.bfloat16),
            pltpu.VMEM(w.shape, jnp.bfloat16),
            pltpu.SemaphoreType.DMA((2,)),
            pltpu.SemaphoreType.DMA((1,)),
        ],
        compiler_params=pltpu.CompilerParams(vmem_limit_bytes=16 * 2**20),
        cost_estimate=pl.CostEstimate(
            flops=9 * 10**9,
            bytes_accessed=2 * (w.size + 2 * x4.size),
            transcendentals=total * w.shape[1],
        ),
    )(x4, gain, w)


def cache_copies(side, offsets, keys, values, moved_keys, moved_values, kv, sems):
    half_slots = kv.shape[0] // 2
    waits = []
    for s in range(half_slots):
        j = 2 * s + side
        own = (
            pltpu.make_async_copy(keys.at[j], kv.at[s], sems.at[s]),
            pltpu.make_async_copy(values.at[j], kv.at[half_slots + s], sems.at[half_slots + s]),
        )
        traded = (
            pltpu.make_async_copy(moved_keys.at[s], kv.at[s], sems.at[s]),
            pltpu.make_async_copy(
                moved_values.at[s], kv.at[half_slots + s], sems.at[half_slots + s]
            ),
        )

        @pl.when(offsets[j] == 0)
        def _():
            for c in own:
                c.start()

        @pl.when(offsets[j] != 0)
        def _():
            for c in traded:
                c.start()

        waits.append(own)
    return waits


def attend_slots(side, lengths, offsets, b_ref, kv, waits, gated):
    half_slots, cap, width = kv.shape[0] // 2, kv.shape[1], kv.shape[2]
    new = b_ref.shape[0] // (2 * half_slots)
    heads = width // HEAD
    lane_head = lax.broadcasted_iota(jnp.int32, (new, width), 1) // HEAD
    position = lax.broadcasted_iota(jnp.int32, (1, cap), 1)
    row = lax.broadcasted_iota(jnp.int32, (heads * new, new), 0) % new
    causal = row >= lax.broadcasted_iota(jnp.int32, (heads * new, new), 1)
    pair_lane = lax.broadcasted_iota(jnp.int32, (new, 2 * HEAD), 1) // HEAD

    def weigh(s):
        j = 2 * s + side
        at = slice(j * new, (j + 1) * new)
        queries = b_ref[at, 2 * width : 3 * width] * jnp.bfloat16(0.5 * HEAD**-0.5)
        fresh_keys = b_ref[at, 3 * width :]
        zero = jnp.zeros_like(queries)
        spread_q = jnp.concatenate(
            [jnp.where(lane_head == h, queries, zero) for h in range(heads)], axis=0
        )
        used = jnp.where(offsets[j] == 0, lengths[j] * BLOCK, cap)
        half = lax.dot_general(spread_q, kv[s], NT, preferred_element_type=jnp.float32)
        cached = jnp.where(position < used, half + half * jnp.tanh(half), 0.0)
        half = lax.dot_general(spread_q, fresh_keys, NT, preferred_element_type=jnp.float32)
        fresh = jnp.where(causal, half + half * jnp.tanh(half), 0.0)
        return cached.astype(jnp.bfloat16), fresh.astype(jnp.bfloat16)

    def finish(s, cached, fresh):
        j = 2 * s + side
        at = slice(j * new, (j + 1) * new)
        to = slice(s * new, (s + 1) * new)
        gate = b_ref[at, :width].astype(jnp.float32)
        fresh_values = b_ref[at, width : 2 * width]
        total = lax.dot_general(
            cached, kv[half_slots + s], NN, preferred_element_type=jnp.float32
        )
        total = total + lax.dot_general(
            fresh, fresh_values, NN, preferred_element_type=jnp.float32
        )
        for pair in range(heads // 2):
            lanes = slice(2 * HEAD * pair, 2 * HEAD * (pair + 1))
            result = jnp.zeros((new, 2 * HEAD), jnp.float32)
            for within in range(2):
                h = 2 * pair + within
                mine = pair_lane == within
                x = jnp.where(mine, total[h * new : (h + 1) * new, lanes], 0.0)
                average = jnp.sum(x, axis=-1, keepdims=True) * (1.0 / HEAD)
                centred = jnp.where(mine, x - average, 0.0)
                spread = jnp.sum(centred * centred, axis=-1, keepdims=True) * (1.0 / HEAD)
                result = result + centred * lax.rsqrt(spread + 1e-05)
            gated[to, lanes] = (result * gate[:, lanes]).astype(jnp.bfloat16)

    for c in [pair[0] for pair in waits]:
        c.wait()
    weights = [weigh(s) for s in range(half_slots)]
    for c in [pair[1] for pair in waits]:
        c.wait()
    for s in range(half_slots):
        finish(s, *weights[s])


def even_kernel(
    lengths, offsets, b_ref, keys, values, moved_keys, moved_values, gated, kv, kv_sems
):
    waits = cache_copies(0, offsets, keys, values, moved_keys, moved_values, kv, kv_sems)
    attend_slots(0, lengths, offsets, b_ref, kv, waits, gated)


def odd_kernel(
    lengths, offsets, b_ref, keys, values, moved, even_ref, w_any, out_ref, kv, gated, w_ref, kv_sems, w_sem
):
    parts, _, width = out_ref.shape
    half_slots = kv.shape[0] // 2
    moved_keys, moved_values = moved.at[:half_slots], moved.at[half_slots:]
    waits = cache_copies(1, offsets, keys, values, moved_keys, moved_values, kv, kv_sems)
    w_copy = pltpu.make_async_copy(w_any, w_ref, w_sem.at[0])
    w_copy.start()
    attend_slots(1, lengths, offsets, b_ref, kv, waits, gated)
    w_copy.wait()
    new = gated.shape[0] // half_slots
    for p in range(parts):
        for side, ref in enumerate((even_ref, gated)):
            block = lax.dot_general(
                ref[...],
                w_ref[:, p * width : (p + 1) * width],
                NN,
                preferred_element_type=jnp.float32,
            ).astype(jnp.bfloat16)
            for s in range(half_slots):
                j = 2 * s + side
                out_ref[p, j * new : (j + 1) * new, :] = block[s * new : (s + 1) * new, :]


def attention_cost(rows, slots, cap, width):
    return pl.CostEstimate(
        flops=4 * rows * width * (cap + rows // slots) * (width // HEAD),
        bytes_accessed=4 * slots * cap * width,
        transcendentals=rows * (width // HEAD) * cap,
    )


def attend_even(lengths, offsets, branches, keys, values, moved_keys, moved_values):
    slots, cap, width = keys.shape
    rows = branches.shape[0] // 2
    return pl.pallas_call(
        even_kernel,
        out_shape=jax.ShapeDtypeStruct((rows, width), jnp.bfloat16),
        in_specs=[SMEM, SMEM, VMEM, HBM, HBM, HBM, HBM],
        out_specs=VMEM,
        scratch_shapes=[
            pltpu.VMEM((slots, cap, width), jnp.bfloat16),
            pltpu.SemaphoreType.DMA((slots,)),
        ],
        compiler_params=pltpu.CompilerParams(vmem_limit_bytes=16 * 2**20),
        cost_estimate=pl.CostEstimate(flops=10**8, bytes_accessed=0, transcendentals=0),
    )(lengths, offsets, branches, in_hbm(keys), in_hbm(values), in_hbm(moved_keys), in_hbm(moved_values))


def attend_odd(lengths, offsets, branches, keys, values, moved, even_gated, w_out):
    slots, cap, width = keys.shape
    rows = branches.shape[0]
    parts = w_out.shape[1] // width
    return pl.pallas_call(
        odd_kernel,
        out_shape=jax.ShapeDtypeStruct((parts, rows, width), jnp.bfloat16),
        in_specs=[SMEM, SMEM, VMEM, HBM, HBM, HBM, VMEM, HBM],
        out_specs=VMEM,
        scratch_shapes=[
            pltpu.VMEM((slots, cap, width), jnp.bfloat16),
            pltpu.VMEM((rows // 2, width), jnp.bfloat16),
            pltpu.VMEM(w_out.shape, jnp.bfloat16),
            pltpu.SemaphoreType.DMA((slots,)),
            pltpu.SemaphoreType.DMA((1,)),
        ],
        compiler_params=pltpu.CompilerParams(vmem_limit_bytes=20 * 2**20),
        cost_estimate=attention_cost(rows // 2, slots // 2, cap, width),
    )(lengths, offsets, branches, in_hbm(keys), in_hbm(values), in_hbm(moved), even_gated, in_hbm(w_out))


def in_hbm(array):
    return pltpu.with_memory_space_constraint(array, pltpu.HBM)


def on_device(events, norm_gain, w_uvqk, w_out, cache_keys, cache_values, lengths, swap_offset):
    slots, cap, width = cache_keys.shape
    users = lax.axis_size("user")
    heads = lax.axis_size("head")

    (odd_pay,) = pack(1, 1, lengths, cache_keys, cache_values)
    odd = lax.ppermute(
        odd_pay, "user", [(i, (((i + 1) ^ 1) - 1) % users) for i in range(users)]
    )
    later_lengths, _ = lax.optimization_barrier((lengths, odd_pay))
    spread = jnp.broadcast_to(events[None], (heads,) + events.shape)
    gathered = lax.all_to_all(spread, "head", 0, 0)
    even = [
        lax.ppermute(pay, "user", [(i, i ^ 1) for i in range(users)])
        for pay in pack(0, 2, later_lengths, cache_keys, cache_values)
    ]

    w = w_uvqk.reshape(w_uvqk.shape[0], 4 * width)
    branches = project(gathered, norm_gain[None, :], w)
    caches = (cache_keys, cache_values)
    even_gated = attend_even(lengths, swap_offset, branches, *caches, *even)
    part = attend_odd(lengths, swap_offset, branches, *caches, odd, even_gated, w_out)
    terms = lax.all_to_all(part, "head", 0, 0)
    summed = jnp.sum(terms.astype(jnp.float32), axis=0)
    return (events.astype(jnp.float32) + summed).astype(jnp.bfloat16)


def solution(mesh):
    return jax.shard_map(
        on_device,
        mesh=mesh,
        in_specs=(
            P("user", "head"),
            P(),
            P(None, None, "head"),
            P("head", None),
            P("user", None, "head"),
            P("user", None, "head"),
            P("user"),
            P("user"),
        ),
        out_specs=P("user", "head"),
        check_vma=False,
    )
```

time: 71.2 us -> 62.5 us (0.88)
  waiting for transfers between devices: 13.3 us -> 1.31 us
  other arithmetic: 6.76 us -> 0.92 us
  Pallas kernels: 11.2 us -> 14.9 us
  blocking collectives: 13.4 us -> 16.5 us
  starting transfers between devices: 20.6 us -> 22.4 us
    all_to_all x1, waiting for transfers between devices: 6.73 us -> 0.01 us  [on_device(): gathered = lax.all_to_all(spread, 'head', 0, 0)]
    ppermute x2 -> x3, waiting for transfers between devices: 6.61 us -> 1.31 us  [the longest x1 1.3 us: on_device(): lax.ppermute(odd_pay, 'user', [(i, ((i + 1 ^ 1) - 1) % users) for i in ra...]
    pallas_call x2 -> x5, Pallas kernels: 11.2 us -> 14.9 us  [the longest x2 5.26 us: pack(): pl.pallas_call(functools.partial(pack_kernel, side), out_shape=[jax.Shape...]
    all_to_all x1, blocking collectives: 13.4 us -> 16.5 us  [on_device(): terms = lax.all_to_all(part, 'head', 0, 0)]
    concatenate x2 -> x0, other arithmetic: 3.03 us -> none  [payload(): jnp.concatenate([a.reshape(slots // 2, 2, cap, width)[:, side] for a in (...]
    select_n x1 -> x0, other arithmetic: 2.09 us -> none  [on_device(): jnp.where(live[:, :, None], cache_values, jnp.zeros_like(cache_values))]
    ppermute x2 -> x3, starting transfers between devices: 15.9 us -> 17.6 us  [the longest x1 13.3 us: on_device(): lax.ppermute(odd_pay, 'user', [(i, ((i + 1 ^ 1) - 1) % users) for i in ra...]
    unnamed x17 -> x15, local copies, waits for them, and re-layouts: 3.27 us -> 4.09 us
  transfers between devices with their start and end apart: 3 -> 4, of which waited for: 2 -> 1; matrix products, arithmetic and copies ran while one was open for 7% -> 5% of each run, Pallas kernels for 4% -> 14%
where the time goes in v3:
time: 62.5 us; the launch traced here: 61.5 us
  starting transfers between devices  22.4 us (36%)
  blocking collectives  16.5 us (26%)
  Pallas kernels  14.9 us (24%)
  local copies, waits for them, and re-layouts  5.23 us (8%)
  waiting for transfers between devices  1.31 us (2%)
  other arithmetic  0.92 us (1%)
    all_to_all x1, blocking collectives, on_device(): terms = lax.all_to_all(part, 'head', 0, 0)  16.5 us
    ppermute x1, starting transfers between devices, on_device(): lax.ppermute(odd_pay, 'user', [(i, ((i + 1 ^ 1) - 1) % users) for i in ra...  13.3 us
    pallas_call x2, Pallas kernels, pack(): pl.pallas_call(functools.partial(pack_kernel, side), out_shape=[jax.Shape...  5.26 us
    all_to_all x1, starting transfers between devices, on_device(): gathered = lax.all_to_all(spread, 'head', 0, 0)  4.77 us
    ppermute x2, starting transfers between devices, on_device(): lax.ppermute(pay, 'user', [(i, i ^ 1) for i in range(users)])  4.33 us
    unnamed x15, local copies, waits for them, and re-layouts  4.09 us
    pallas_call x1, Pallas kernels, attend_odd(): pl.pallas_call(odd_kernel, out_shape=jax.ShapeDtypeStruct((parts, rows, w...  4 us
    pallas_call x1, Pallas kernels, attend_even(): pl.pallas_call(even_kernel, out_shape=jax.ShapeDtypeStruct((rows, width),...  3.39 us
  transfers between devices with their start and end apart: 4, of which 1 were waited for; matrix products, arithmetic and copies ran while one was open for 5% of the time, Pallas kernels for 14%

profile of v3, /device:TPU:6, one launch (start us, length us, event | category | flops | bytes accessed | tf_op | source)
XLA Modules:
  0.0 61.5 jit_solution(9873576363416939784)
XLA Ops:
  0.0 0.0 copy-start.1
  0.0 0.7 %copy-done.1 = s32[8]{0:T(128)S(1)} copy-done((s32[8]{0:T(128)S(1)}, s32[8]{0:T(128)}, u32[]{:S(2)}) %copy-start.1) | copy-done | bytes 56
  0.7 0.0 copy-start.6
  0.7 2.2 %shard_map.83 = bf16[8,512,256]{2,1,0:T(8,128)(2,1)S(1)} custom-call(s32[8]{0:T(128)S(1)} %copy-done.1, bf16[8,512,256]{2,1,0:T(8,128)(2,1)} %keys.7, bf16[8,512,256]{2,1,0:T(8,128)(2,1)} %values.7), custom_call_target="tpu_custom_call" | custom-call | bytes 4000000 | tf_op jit(solution)/shard_map/pallas_call | solution.py:51
  2.9 0.0 copy-start.2
  2.9 13.3 %collective-permute-start = (bf16[8,512,256]{2,1,0:T(8,128)(2,1)S(1)}, bf16[8,512,256]{2,1,0:T(8,128)(2,1)}, u32[]{:S(2)}, u32[]{:S(2)}) collective-permute-start(bf16[8,512,256]{2,1,0:T(8,128)(2,1)S(1)} %shard_map.83), channel_id=1, source_target_pairs={{0,508},{4,8},{8,4},{12,16},{16,12},{20,24},{24,20},{28,32},{32,28... | collective-permute-start | bytes 6291464 | tf_op jit(solution)/shard_map/ppermute | solution.py:304
  16.2 0.0 copy-done.6
  16.2 1.1 %broadcast_in_dim.4 = bf16[4,512,256]{2,1,0:T(8,128)(2,1)} broadcast(bf16[512,256]{1,0:T(8,128)(2,1)S(1)} %copy-done.6), dimensions={1,2} | broadcast | bytes 1310720 | tf_op jit(solution)/shard_map/broadcast_in_dim | solution.py:308
  17.3 4.8 %all-to-all-start = ((bf16[4,512,256]{2,1,0:T(8,128)(2,1)}), bf16[4,512,256]{2,1,0:T(8,128)(2,1)S(1)}, u32[]{:S(2)}, u32[]{:S(2)}) async-start(bf16[4,512,256]{2,1,0:T(8,128)(2,1)} %broadcast_in_dim.4), calls=%async_computation | async-start | bytes 2097152 | tf_op jit(solution)/shard_map/all_to_all | solution.py:309
  22.1 0.0 copy-done.2
  22.1 0.0 copy-start.5
  22.1 3.0 %shard_map.84 = (bf16[4,512,256]{2,1,0:T(8,128)(2,1)}, bf16[4,512,256]{2,1,0:T(8,128)(2,1)}) custom-call(s32[8]{0:T(128)S(1)} %copy-done.2, bf16[8,512,256]{2,1,0:T(8,128)(2,1)} %keys.7, bf16[8,512,256]{2,1,0:T(8,128)(2,1)} %values.7), custom_call_target="tpu_custom_call" | custom-call | bytes 15000000 | tf_op jit(solution)/shard_map/pallas_call | solution.py:51
  25.2 1.9 %collective-permute-start.1 = (bf16[4,512,256]{2,1,0:T(8,128)(2,1)}, bf16[4,512,256]{2,1,0:T(8,128)(2,1)}, u32[]{:S(2)}, u32[]{:S(2)}) collective-permute-start(bf16[4,512,256]{2,1,0:T(8,128)(2,1)} %get-tuple-element.9), channel_id=1, source_target_pairs={{0,4},{4,0},{8,12},{12,8},{16,20},{20,16},{24,28},{28,24},{32,36},... | collective-permute-start | bytes 3145736 | tf_op jit(solution)/shard_map/ppermute | solution.py:311
  27.1 2.4 %collective-permute-start.2 = (bf16[4,512,256]{2,1,0:T(8,128)(2,1)}, bf16[4,512,256]{2,1,0:T(8,128)(2,1)}, u32[]{:S(2)}, u32[]{:S(2)}) collective-permute-start(bf16[4,512,256]{2,1,0:T(8,128)(2,1)} %get-tuple-element.10), channel_id=1, source_target_pairs={{0,4},{4,0},{8,12},{12,8},{16,20},{20,16},{24,28},{28,24},{32,36},... | collective-permute-start | bytes 3145736 | tf_op jit(solution)/shard_map/ppermute | solution.py:311
  29.5 0.0 copy-done.5
  29.5 0.0 copy-start.4
  29.5 1.8 %copy.9 = bf16[128,8,4,256]{3,1,2,0:T(8,128)(2,1)} copy(bf16[128,8,4,256]{3,2,1,0:T(4,128)(2,1)S(1)} %bitcast.5) | data formatting | bytes 4194304
  31.4 0.0 all-to-all-done.x_any
  31.4 0.0 copy-done.4
  31.4 0.0 copy-start
  31.4 1.6 %copy-done = bf16[128,8,4,256]{3,1,2,0:T(8,128)(2,1)S(1)} copy-done((bf16[128,8,4,256]{3,1,2,0:T(8,128)(2,1)S(1)}, bf16[128,8,4,256]{3,1,2,0:T(8,128)(2,1)}, u32[]{:S(2)}) %copy-start) | copy-done | bytes 2097176
  33.0 0.0 copy-start.3
  33.0 2.3 %shard_map.82.b_ref = bf16[512,1024]{1,0:T(8,128)(2,1)S(1)} custom-call(bf16[4,512,256]{2,1,0:T(8,128)(2,1)S(1)} %all-to-all-done.x_any, f32[1,1024]{1,0:T(1,128)S(1)} %bitcast.4, bf16[1024,1024]{1,0:T(8,128)(2,1)S(1)} %bitcast.3), custom_call_target="tpu_custom_call" | custom-call | flops 8999999488 | bytes 4194304 | tf_op jit(solution)/shard_map/pallas_call | solution.py:106
  35.3 0.0 collective-permute-done.1.moved_keys
  35.3 0.0 collective-permute-done.2.moved_values
  35.3 0.0 copy-done.3
  35.3 3.4 %shard_map.85.even_ref = bf16[256,256]{1,0:T(8,128)(2,1)S(1)} custom-call(s32[8]{0:T(128)S(1)} %copy-done.2, s32[8]{0:T(128)S(1)} %copy-done.3, bf16[512,1024]{1,0:T(8,128)(2,1)S(1)} %shard_map.82.b_ref, bf16[8,512,256]{2,1,0:T(8,128)(2,1)} %keys.7, bf16[8,512,256]{2,1,0:T(8,128)(2,1)} %values.7, bf16[4,512,256]{2,1,0:T(8,128)(2,1)} %collective-permute-done.1.moved_keys, ...), custom_call_target="tpu_custom_call" | custom-call | flops 100000000 | tf_op jit(solution)/shard_map/pallas_call | solution.py:259
  38.7 1.3 %collective-permute-done.moved = bf16[8,512,256]{2,1,0:T(8,128)(2,1)} collective-permute-done((bf16[8,512,256]{2,1,0:T(8,128)(2,1)S(1)}, bf16[8,512,256]{2,1,0:T(8,128)(2,1)}, u32[]{:S(2)}, u32[]{:S(2)}) %collective-permute-start) | collective-permute-done | bytes 2097184 | tf_op jit(solution)/shard_map/ppermute | solution.py:304
  40.0 4.0 %shard_map.86 = bf16[4,512,256]{2,1,0:T(8,128)(2,1)S(1)} custom-call(s32[8]{0:T(128)S(1)} %copy-done.2, s32[8]{0:T(128)S(1)} %copy-done.3, bf16[512,1024]{1,0:T(8,128)(2,1)S(1)} %shard_map.82.b_ref, bf16[8,512,256]{2,1,0:T(8,128)(2,1)} %keys.7, bf16[8,512,256]{2,1,0:T(8,128)(2,1)} %values.7, bf16[8,512,256]{2,1,0:T(8,128)(2,1)} %collective-permute-done.moved, ...), custom_call_target="tpu_custom_call" | custom-call | flops 603979776 | bytes 2097152 | tf_op jit(solution)/shard_map/pallas_call | solution.py:277
  44.0 16.5 %all_to_all.10 = bf16[4,512,256]{2,1,0:T(8,128)(2,1)S(1)} all-to-all(bf16[4,512,256]{2,1,0:T(8,128)(2,1)S(1)} %shard_map.86), channel_id=1, replica_groups=mesh['user'=128,'head'=4] {'head'}, dimensions={0} | all-to-all | bytes 2097152 | tf_op jit(solution)/shard_map/all_to_all | solution.py:320
  60.5 0.1 convert_reduce_fusion
  60.7 0.8 %add_convert_fusion = bf16[512,256]{1,0:T(8,128)(2,1)} fusion(f32[512,256]{1,0:T(8,128)S(1)} %convert_reduce_fusion, bf16[512,256]{1,0:T(8,128)(2,1)S(1)} %copy-done.6), kind=kLoop, calls=%fused_computation.1 | loop fusion | flops 393216 | bytes 1048576 | tf_op jit(solution)/shard_map/convert_element_type | solution.py:322
Async XLA Ops:
  0.0 0.7 %copy-start.1 = (s32[8]{0:T(128)S(1)}, s32[8]{0:T(128)}, u32[]{:S(2)}) copy-start(s32[8]{0:T(128)} %lengths.6) | copy-start | bytes 100
  0.7 15.5 %copy-start.6 = (bf16[512,256]{1,0:T(8,128)(2,1)S(1)}, bf16[512,256]{1,0:T(8,128)(2,1)}, u32[]{:S(2)}) copy-start(bf16[512,256]{1,0:T(8,128)(2,1)} %param.8) | copy-start | bytes 786436
  2.9 19.2 %copy-start.2 = (s32[8]{0:T(128)S(1)}, s32[8]{0:T(128)}, u32[]{:S(2)}) copy-start(s32[8]{0:T(128)} %lengths.6) | copy-start | bytes 100
  2.9 37.1 %collective-permute-start = (bf16[8,512,256]{2,1,0:T(8,128)(2,1)S(1)}, bf16[8,512,256]{2,1,0:T(8,128)(2,1)}, u32[]{:S(2)}, u32[]{:S(2)}) collective-permute-start(bf16[8,512,256]{2,1,0:T(8,128)(2,1)S(1)} %shard_map.83), channel_id=1, source_target_pairs={{0,508},{4,8},{8,4},{12,16},{16,12},{20,24},{24,20},{28,32},{32,28... | collective-permute-start | bytes 6291464 | tf_op jit(solution)/shard_map/ppermute | solution.py:304
  17.3 14.0 %all-to-all-start = ((bf16[4,512,256]{2,1,0:T(8,128)(2,1)}), bf16[4,512,256]{2,1,0:T(8,128)(2,1)S(1)}, u32[]{:S(2)}, u32[]{:S(2)}) async-start(bf16[4,512,256]{2,1,0:T(8,128)(2,1)} %broadcast_in_dim.4), calls=%async_computation | async-start | bytes 2097152 | tf_op jit(solution)/shard_map/all_to_all | solution.py:309
  22.1 7.4 %copy-start.5 = (bf16[1024,4,256]{2,1,0:T(4,128)(2,1)S(1)}, bf16[1024,4,256]{2,1,0:T(4,128)(2,1)}, u32[]{:S(2)}) copy-start(bf16[1024,4,256]{2,1,0:T(4,128)(2,1)} %param.10) | copy-start | bytes 6291460
  25.2 10.1 %collective-permute-start.1 = (bf16[4,512,256]{2,1,0:T(8,128)(2,1)}, bf16[4,512,256]{2,1,0:T(8,128)(2,1)}, u32[]{:S(2)}, u32[]{:S(2)}) collective-permute-start(bf16[4,512,256]{2,1,0:T(8,128)(2,1)} %get-tuple-element.9), channel_id=1, source_target_pairs={{0,4},{4,0},{8,12},{12,8},{16,20},{20,16},{24,28},{28,24},{32,36},... | collective-permute-start | bytes 3145736 | tf_op jit(solution)/shard_map/ppermute | solution.py:311
  27.1 8.2 %collective-permute-start.2 = (bf16[4,512,256]{2,1,0:T(8,128)(2,1)}, bf16[4,512,256]{2,1,0:T(8,128)(2,1)}, u32[]{:S(2)}, u32[]{:S(2)}) collective-permute-start(bf16[4,512,256]{2,1,0:T(8,128)(2,1)} %get-tuple-element.10), channel_id=1, source_target_pairs={{0,4},{4,0},{8,12},{12,8},{16,20},{20,16},{24,28},{28,24},{32,36},... | collective-permute-start | bytes 3145736 | tf_op jit(solution)/shard_map/ppermute | solution.py:311
  29.5 1.8 %copy-start.4 = (f32[1024]{0:T(1024)S(1)}, f32[1024]{0:T(1024)}, u32[]{:S(2)}) copy-start(f32[1024]{0:T(1024)} %param.9) | copy-start | bytes 12292
  31.4 1.6 %copy-start = (bf16[128,8,4,256]{3,1,2,0:T(8,128)(2,1)S(1)}, bf16[128,8,4,256]{3,1,2,0:T(8,128)(2,1)}, u32[]{:S(2)}) copy-start(bf16[128,8,4,256]{3,1,2,0:T(8,128)(2,1)} %copy.9) | copy-start | bytes 6291460
  33.0 2.3 %copy-start.3 = (s32[8]{0:T(128)S(1)}, s32[8]{0:T(128)}, u32[]{:S(2)}) copy-start(s32[8]{0:T(128)} %offsets.3) | copy-start | bytes 100

commit v4 on v3

v4 whole, which is shorter than its diff:
```python
import functools

import jax
import jax.numpy as jnp
from jax import lax
from jax.experimental import pallas as pl
from jax.experimental.pallas import tpu as pltpu
from jax.sharding import PartitionSpec as P

HEAD = 64
BLOCK = 128
NEW = 64
NT = (((1,), (1,)), ((), ()))
NN = (((1,), (0,)), ((), ()))
VMEM = pl.BlockSpec(memory_space=pltpu.VMEM)
SMEM = pl.BlockSpec(memory_space=pltpu.SMEM)
HBM = pl.BlockSpec(memory_space=pltpu.HBM)
ANY = pl.BlockSpec(memory_space=pl.ANY)


def pack_kernel(side, lengths_hbm, keys, values, *rest):
    *rest, buf, lengths, in_sems, out_sems, sem = rest
    spread = None
    if side == 1:
        events, *pays, spread, events_ref, spread_sems = rest
    else:
        pays = rest
    half_slots, cap, width = keys.shape[0] // 2, keys.shape[1], keys.shape[2]
    places = [pay.at[s] for pay in pays for s in range(pay.shape[0])]
    lengths_copy = pltpu.make_async_copy(lengths_hbm, lengths, sem.at[0])
    lengths_copy.start()
    arrive, leave = [], []
    for s in range(half_slots):
        j = 2 * s + side
        for array, slot in ((values, half_slots + s), (keys, s)):
            arrive.append(pltpu.make_async_copy(array.at[j], buf.at[slot], in_sems.at[slot]))
            leave.append(pltpu.make_async_copy(buf.at[slot], places[slot], out_sems.at[slot]))
    for c in arrive:
        c.start()
    if spread is not None:
        events_copy = pltpu.make_async_copy(events, events_ref, sem.at[1])
        events_copy.start()
    lengths_copy.wait()
    for i, c in enumerate(arrive):
        c.wait()
        if i % 2 == 0:
            s = i // 2
            for block in range(1, cap // BLOCK):

                @pl.when(lengths[2 * s + side] <= block)
                def _():
                    buf[half_slots + s, block * BLOCK : (block + 1) * BLOCK, :] = jnp.zeros(
                        (BLOCK, width), buf.dtype
                    )

        leave[i].start()
    if spread is not None:
        events_copy.wait()
        for p in range(spread.shape[0]):
            copy = pltpu.make_async_copy(events_ref, spread.at[p], spread_sems.at[p])
            copy.start()
            leave.append(copy)
    for c in leave:
        c.wait()


def pack(side, pieces, lengths, keys, values, events=None, parts=0):
    slots, cap, width = keys.shape
    operands = [in_hbm(lengths), in_hbm(keys), in_hbm(values)]
    outs = [pltpu.HBM((slots // pieces, cap, width), keys.dtype)] * pieces
    scratch = []
    if events is not None:
        operands.append(in_hbm(events))
        outs.append(pltpu.HBM((parts,) + events.shape, events.dtype))
        scratch = [pltpu.VMEM(events.shape, events.dtype), pltpu.SemaphoreType.DMA((parts,))]
    return pl.pallas_call(
        functools.partial(pack_kernel, side),
        out_shape=outs,
        in_specs=[HBM] * len(operands),
        out_specs=[HBM] * len(outs),
        scratch_shapes=scratch
        + [
            pltpu.VMEM((slots, cap, width), keys.dtype),
            pltpu.SMEM(lengths.shape, lengths.dtype),
            pltpu.SemaphoreType.DMA((slots,)),
            pltpu.SemaphoreType.DMA((slots,)),
            pltpu.SemaphoreType.DMA((2,)),
        ],
        compiler_params=pltpu.CompilerParams(vmem_limit_bytes=6 * 2**20),
        cost_estimate=pl.CostEstimate(
            flops=0, bytes_accessed=4 * 10**6 if side else 15 * 10**6, transcendentals=0
        ),
    )(*operands)


def project_kernel(x_any, gain_ref, w_hbm, even_hbm, odd_hbm, x_ref, w_ref, b_ref, x_sems, w_sem, b_sems):
    parts, total, width = x_ref.shape
    features = parts * width
    chunks = x_sems.shape[0]
    rows = total // chunks
    x_copies = []
    for i in range(chunks):
        at = pl.ds(i * rows, rows)
        x_copies.append(
            pltpu.make_async_copy(x_any.at[:, at, :], x_ref.at[:, at, :], x_sems.at[i])
        )
    w_copy = pltpu.make_async_copy(w_hbm, w_ref, w_sem.at[0])
    x_copies[0].start()
    w_copy.start()
    for c in x_copies[1:]:
        c.start()
    gain = gain_ref[...]

    def normalise(i):
        x = jnp.concatenate(
            [x_ref[p, i * rows : (i + 1) * rows, :] for p in range(parts)], axis=1
        ).astype(jnp.float32)
        average = jnp.sum(x, axis=-1, keepdims=True) * (1.0 / features)
        centred = x - average
        spread = jnp.sum(centred * centred, axis=-1, keepdims=True) * (1.0 / features)
        return (centred * lax.rsqrt(spread + 1e-05) * gain).astype(jnp.bfloat16)

    leave = []
    for i in range(chunks):
        x_copies[i].wait()
        normed = normalise(i)
        if i == 0:
            w_copy.wait()
        half = 0.5 * lax.dot_general(normed, w_ref[...], NN, preferred_element_type=jnp.float32)
        branch = (half + half * jnp.tanh(half)).astype(jnp.bfloat16)
        held = rows // (2 * NEW)
        for k in range(2 * held):
            s = i * held + k // 2
            b_ref[k % 2, s * NEW : (s + 1) * NEW, :] = branch[k * NEW : (k + 1) * NEW, :]
        for side, target in enumerate((even_hbm, odd_hbm)):
            at = pl.ds(i * held * NEW, held * NEW)
            copy = pltpu.make_async_copy(
                b_ref.at[side, at], target.at[at], b_sems.at[2 * i + side]
            )
            copy.start()
            leave.append(copy)
    for c in leave:
        c.wait()


def project(x4, gain, w):
    parts, total, width = x4.shape
    chunks, wide = 2, w.shape[1]
    out = pltpu.HBM((total // 2, wide), jnp.bfloat16)
    return pl.pallas_call(
        project_kernel,
        out_shape=(out, out),
        in_specs=[ANY, VMEM, HBM],
        out_specs=(HBM, HBM),
        scratch_shapes=[
            pltpu.VMEM(x4.shape, jnp.bfloat16),
            pltpu.VMEM(w.shape, jnp.bfloat16),
            pltpu.VMEM((2, total // 2, wide), jnp.bfloat16),
            pltpu.SemaphoreType.DMA((chunks,)),
            pltpu.SemaphoreType.DMA((1,)),
            pltpu.SemaphoreType.DMA((2 * chunks,)),
        ],
        compiler_params=pltpu.CompilerParams(vmem_limit_bytes=20 * 2**20),
        cost_estimate=pl.CostEstimate(
            flops=9 * 10**9,
            bytes_accessed=2 * (w.size + 2 * x4.size),
            transcendentals=total * wide,
        ),
    )(x4, gain, in_hbm(w))


def cache_copies(side, offsets, keys, values, moved_keys, moved_values, kv, sems):
    half_slots = kv.shape[0] // 2
    waits = []
    for s in range(half_slots):
        j = 2 * s + side
        own = (
            pltpu.make_async_copy(keys.at[j], kv.at[s], sems.at[s]),
            pltpu.make_async_copy(values.at[j], kv.at[half_slots + s], sems.at[half_slots + s]),
        )
        traded = (
            pltpu.make_async_copy(moved_keys.at[s], kv.at[s], sems.at[s]),
            pltpu.make_async_copy(
                moved_values.at[s], kv.at[half_slots + s], sems.at[half_slots + s]
            ),
        )

        waits.append((j, own, traded))
    for kind in range(2):
        for j, own, traded in waits:

            @pl.when(offsets[j] == 0)
            def _():
                own[kind].start()

            @pl.when(offsets[j] != 0)
            def _():
                traded[kind].start()

    return [own for _, own, _ in waits]


def attend_slots(side, lengths, offsets, b_ref, kv, waits, gated):
    half_slots, cap, width = kv.shape[0] // 2, kv.shape[1], kv.shape[2]
    new = b_ref.shape[0] // half_slots
    heads = width // HEAD
    lane_head = lax.broadcasted_iota(jnp.int32, (new, width), 1) // HEAD
    position = lax.broadcasted_iota(jnp.int32, (1, cap), 1)
    row = lax.broadcasted_iota(jnp.int32, (heads * new, new), 0) % new
    causal = row >= lax.broadcasted_iota(jnp.int32, (heads * new, new), 1)
    pair_lane = lax.broadcasted_iota(jnp.int32, (new, 2 * HEAD), 1) // HEAD

    def weigh(s):
        j = 2 * s + side
        at = slice(s * new, (s + 1) * new)
        queries = b_ref[at, 2 * width : 3 * width] * jnp.bfloat16(0.5 * HEAD**-0.5)
        fresh_keys = b_ref[at, 3 * width :]
        zero = jnp.zeros_like(queries)
        spread_q = jnp.concatenate(
            [jnp.where(lane_head == h, queries, zero) for h in range(heads)], axis=0
        )
        used = jnp.where(offsets[j] == 0, lengths[j] * BLOCK, cap)
        half = lax.dot_general(spread_q, kv[s], NT, preferred_element_type=jnp.float32)
        cached = jnp.where(position < used, half + half * jnp.tanh(half), 0.0)
        half = lax.dot_general(spread_q, fresh_keys, NT, preferred_element_type=jnp.float32)
        fresh = jnp.where(causal, half + half * jnp.tanh(half), 0.0)
        return cached.astype(jnp.bfloat16), fresh.astype(jnp.bfloat16)

    def finish(s, cached, fresh):
        at = slice(s * new, (s + 1) * new)
        gate = b_ref[at, :width].astype(jnp.float32)
        fresh_values = b_ref[at, width : 2 * width]
        total = lax.dot_general(
            cached, kv[half_slots + s], NN, preferred_element_type=jnp.float32
        )
        total = total + lax.dot_general(
            fresh, fresh_values, NN, preferred_element_type=jnp.float32
        )
        for pair in range(heads // 2):
            lanes = slice(2 * HEAD * pair, 2 * HEAD * (pair + 1))
            result = jnp.zeros((new, 2 * HEAD), jnp.float32)
            for within in range(2):
                h = 2 * pair + within
                mine = pair_lane == within
                x = jnp.where(mine, total[h * new : (h + 1) * new, lanes], 0.0)
                average = jnp.sum(x, axis=-1, keepdims=True) * (1.0 / HEAD)
                centred = jnp.where(mine, x - average, 0.0)
                spread = jnp.sum(centred * centred, axis=-1, keepdims=True) * (1.0 / HEAD)
                result = result + centred * lax.rsqrt(spread + 1e-05)
            gated[at, lanes] = (result * gate[:, lanes]).astype(jnp.bfloat16)

    for c in [pair[0] for pair in waits]:
        c.wait()
    weights = [weigh(s) for s in range(half_slots)]
    for c in [pair[1] for pair in waits]:
        c.wait()
    for s in range(half_slots):
        finish(s, *weights[s])


def project_out(gated, w_ref, out_ref, width):
    for p in range(out_ref.shape[0]):
        out_ref[p] = lax.dot_general(
            gated[...],
            w_ref[:, p * width : (p + 1) * width],
            NN,
            preferred_element_type=jnp.float32,
        ).astype(jnp.bfloat16)


def serve_kernel(
    side, lengths, offsets, b_hbm, keys, values, w_hbm, moved_keys, *rest
):
    moved_values = None
    if side == 0:
        moved_values, *rest = rest
    out_ref, b_ref, w_ref, kv, gated, sems, kv_sems = rest
    half_slots, width = kv.shape[0] // 2, kv.shape[2]
    if side == 1:
        moved_keys, moved_values = moved_keys.at[:half_slots], moved_keys.at[half_slots:]
    b_copy = pltpu.make_async_copy(b_hbm, b_ref, sems.at[0])
    w_copy = pltpu.make_async_copy(w_hbm, w_ref, sems.at[1])
    b_copy.start()
    waits = cache_copies(side, offsets, keys, values, moved_keys, moved_values, kv, kv_sems)
    w_copy.start()
    b_copy.wait()
    attend_slots(side, lengths, offsets, b_ref, kv, waits, gated)
    w_copy.wait()
    project_out(gated, w_ref, out_ref, width)


def serve(side, lengths, offsets, branches, keys, values, w_out, moved):
    slots, cap, width = keys.shape
    parts, rows = w_out.shape[1] // width, branches.shape[0]
    bf16 = jnp.bfloat16
    operands = [in_hbm(a) for a in (branches, keys, values, w_out)]
    operands += [in_hbm(a) for a in moved] if side else moved
    return pl.pallas_call(
        functools.partial(serve_kernel, side),
        out_shape=jax.ShapeDtypeStruct((parts, rows, width), bf16),
        in_specs=[SMEM, SMEM] + [HBM] * 4 + [HBM if side else ANY] * len(moved),
        out_specs=VMEM,
        scratch_shapes=[
            pltpu.VMEM(branches.shape, bf16),
            pltpu.VMEM(w_out.shape, bf16),
            pltpu.VMEM((slots, cap, width), bf16),
            pltpu.VMEM((rows, width), bf16),
            pltpu.SemaphoreType.DMA((2,)),
            pltpu.SemaphoreType.DMA((slots,)),
        ],
        compiler_params=pltpu.CompilerParams(vmem_limit_bytes=20 * 2**20),
        cost_estimate=pl.CostEstimate(
            flops=3 * 10**9 if side else 10**8, bytes_accessed=0, transcendentals=0
        ),
    )(lengths, offsets, *operands)


def combine_kernel(events, even, odd, out_ref):
    parts, rows, _ = even.shape
    half_slots = out_ref.shape[0] // 2 // NEW
    for j in range(2 * half_slots):
        at = slice(j * NEW, (j + 1) * NEW)
        terms_at = slice((j // 2) * NEW, (j // 2 + 1) * NEW)
        terms = odd if j % 2 else even
        total = terms[0, terms_at, :].astype(jnp.float32)
        for p in range(1, parts):
            total = total + terms[p, terms_at, :].astype(jnp.float32)
        out_ref[at, :] = (events[at, :].astype(jnp.float32) + total).astype(out_ref.dtype)


def combine(events, even, odd):
    return pl.pallas_call(
        combine_kernel,
        out_shape=jax.ShapeDtypeStruct(events.shape, events.dtype),
        in_specs=[VMEM, VMEM, VMEM],
        out_specs=VMEM,
        compiler_params=pltpu.CompilerParams(vmem_limit_bytes=6 * 2**20),
    )(events, even, odd)


def in_hbm(array):
    return pltpu.with_memory_space_constraint(array, pltpu.HBM)


def on_device(events, norm_gain, w_uvqk, w_out, cache_keys, cache_values, lengths, swap_offset):
    slots, cap, width = cache_keys.shape
    users = lax.axis_size("user")
    heads = lax.axis_size("head")
    caches = (cache_keys, cache_values)

    def to_heads(blocks):
        return lax.all_to_all(blocks, "head", 0, 0)

    odd_pay, spread = pack(1, 1, lengths, *caches, events, heads)
    across = [(i, (((i + 1) ^ 1) - 1) % users) for i in range(users)]
    odd = [lax.ppermute(odd_pay, "user", across)]
    gathered = to_heads(spread)
    later_lengths, _ = lax.optimization_barrier((lengths, odd_pay))
    within = [(i, i ^ 1) for i in range(users)]
    even = [lax.ppermute(pay, "user", within) for pay in pack(0, 2, later_lengths, *caches)]

    w = w_uvqk.reshape(w_uvqk.shape[0], 4 * width)
    even_branches, odd_branches = project(gathered, norm_gain[None, :], w)
    even_part = serve(0, lengths, swap_offset, even_branches, *caches, w_out, even)
    even_terms = to_heads(even_part)
    later_branches, _ = lax.optimization_barrier((odd_branches, even_part))
    odd_part = serve(1, lengths, swap_offset, later_branches, *caches, w_out, odd)
    odd_part, even_terms = lax.optimization_barrier((odd_part, even_terms))
    odd_terms = to_heads(odd_part)
    return combine(events, even_terms, odd_terms)


def solution(mesh):
    return jax.shard_map(
        on_device,
        mesh=mesh,
        in_specs=(
            P("user", "head"),
            P(),
            P(None, None, "head"),
            P("head", None),
            P("user", None, "head"),
            P("user", None, "head"),
            P("user"),
            P("user"),
        ),
        out_specs=P("user", "head"),
        check_vma=False,
    )
```

time: 62.5 us -> 63.1 us (level)
  blocking collectives: 16.5 us -> 10.5 us
  starting transfers between devices: 22.4 us -> 27.9 us
  Pallas kernels: 14.9 us -> 18.7 us
  local copies, waits for them, and re-layouts: 5.23 us -> 1.86 us
  waiting for transfers between devices: 1.31 us -> 2.98 us
  other arithmetic: 0.92 us -> 0 us
    all_to_all x1, blocking collectives: 16.5 us -> 10.5 us  [to_heads(): return lax.all_to_all(blocks, 'head', 0, 0)]
    all_to_all x1 -> x2, starting transfers between devices: 4.77 us -> 10.3 us  [to_heads(): return lax.all_to_all(blocks, 'head', 0, 0)]
    pallas_call x5 -> x6, Pallas kernels: 14.9 us -> 18.7 us  [the longest x2 8.06 us: serve(): pl.pallas_call(functools.partial(serve_kernel, side), out_shape=jax.Shape...]
    all_to_all x1 -> x2, waiting for transfers between devices: 0.01 us -> 2.97 us  [to_heads(): return lax.all_to_all(blocks, 'head', 0, 0)]
    unnamed x15 -> x11, local copies, waits for them, and re-layouts: 4.09 us -> 1.86 us
    ppermute x3, waiting for transfers between devices: 1.31 us -> 0.01 us  [the longest x2 0.01 us: on_device(): lax.ppermute(pay, 'user', within)]
    broadcast_in_dim x1 -> x0, local copies, waits for them, and re-layouts: 1.14 us -> none  [on_device(): spread = jnp.broadcast_to(events[None], (heads,) + events.shape)]
    convert_element_type x1 -> x0, other arithmetic: 0.77 us -> none  [on_device(): return (events.astype(jnp.float32) + summed).astype(jnp.bfloat16)]
  transfers between devices with their start and end apart: 4 -> 5, of which waited for: 1 -> 1; matrix products, arithmetic and copies ran while one was open for 5% -> 3% of each run, Pallas kernels for 14% -> 24%
where the time goes in v4:
time: 63.1 us; the launch traced here: 62 us
  starting transfers between devices  27.9 us (44%)
  Pallas kernels  18.7 us (30%)
  blocking collectives  10.5 us (17%)
  waiting for transfers between devices  2.98 us (5%)
  local copies, waits for them, and re-layouts  1.86 us (3%)
    ppermute x1, starting transfers between devices, on_device(): odd = [lax.ppermute(odd_pay, 'user', across)]  13.3 us
    all_to_all x1, blocking collectives, to_heads(): return lax.all_to_all(blocks, 'head', 0, 0)  10.5 us
    all_to_all x2, starting transfers between devices, to_heads(): return lax.all_to_all(blocks, 'head', 0, 0)  10.3 us
    pallas_call x2, Pallas kernels, serve(): pl.pallas_call(functools.partial(serve_kernel, side), out_shape=jax.Shape...  8.06 us
    pallas_call x2, Pallas kernels, pack(): pl.pallas_call(functools.partial(pack_kernel, side), out_shape=outs, in_s...  5.49 us
    ppermute x2, starting transfers between devices, on_device(): lax.ppermute(pay, 'user', within)  4.33 us
    pallas_call x1, Pallas kernels, project(): pl.pallas_call(project_kernel, out_shape=(out, out), in_specs=[ANY, VMEM,...  4.25 us
    all_to_all x2, waiting for transfers between devices, to_heads(): return lax.all_to_all(blocks, 'head', 0, 0)  2.97 us
  transfers between devices with their start and end apart: 5, of which 1 were waited for; matrix products, arithmetic and copies ran while one was open for 3% of the time, Pallas kernels for 24%

profile of v4, /device:TPU:6, one launch (start us, length us, event | category | flops | bytes accessed | tf_op | source)
XLA Modules:
  0.0 62.0 jit_solution(2850328501382779112)
XLA Ops:
  0.0 2.9 %shard_map.82 = (bf16[8,512,256]{2,1,0:T(8,128)(2,1)}, bf16[4,512,256]{2,1,0:T(8,128)(2,1)}) custom-call(s32[8]{0:T(128)} %lengths.3, bf16[8,512,256]{2,1,0:T(8,128)(2,1)} %keys.7, bf16[8,512,256]{2,1,0:T(8,128)(2,1)} %values.7, bf16[512,256]{1,0:T(8,128)(2,1)} %events.1), custom_call_target="tpu_custom_call" | custom-call | bytes 4000000 | tf_op jit(solution)/shard_map/pallas_call | solution.py:76
  2.9 13.3 %collective-permute-start.2 = (bf16[8,512,256]{2,1,0:T(8,128)(2,1)}, bf16[8,512,256]{2,1,0:T(8,128)(2,1)}, u32[]{:S(2)}, u32[]{:S(2)}) collective-permute-start(bf16[8,512,256]{2,1,0:T(8,128)(2,1)} %get-tuple-element.18), channel_id=1, source_target_pairs={{0,508},{4,8},{8,4},{12,16},{16,12},{20,24},{24,20},{28,32},{32,28... | collective-permute-start | bytes 6291464 | tf_op jit(solution)/shard_map/ppermute | solution.py:356
  16.2 4.8 %all-to-all-start = ((bf16[4,512,256]{2,1,0:T(8,128)(2,1)}), bf16[4,512,256]{2,1,0:T(8,128)(2,1)S(1)}, u32[]{:S(2)}, u32[]{:S(2)}) async-start(bf16[4,512,256]{2,1,0:T(8,128)(2,1)} %get-tuple-element.15), calls=%async_computation | async-start | bytes 2097152 | tf_op jit(solution)/shard_map/all_to_all | solution.py:352
  21.0 0.0 copy-start.4
  21.0 2.6 %shard_map.84 = (bf16[4,512,256]{2,1,0:T(8,128)(2,1)}, bf16[4,512,256]{2,1,0:T(8,128)(2,1)}) custom-call(s32[8]{0:T(128)} %lengths.3, bf16[8,512,256]{2,1,0:T(8,128)(2,1)} %keys.7, bf16[8,512,256]{2,1,0:T(8,128)(2,1)} %values.7), custom_call_target="tpu_custom_call" | custom-call | bytes 15000000 | tf_op jit(solution)/shard_map/pallas_call | solution.py:76
  23.6 1.9 %collective-permute-start = (bf16[4,512,256]{2,1,0:T(8,128)(2,1)}, bf16[4,512,256]{2,1,0:T(8,128)(2,1)S(1)}, u32[]{:S(2)}, u32[]{:S(2)}) collective-permute-start(bf16[4,512,256]{2,1,0:T(8,128)(2,1)} %get-tuple-element.20), channel_id=1, source_target_pairs={{0,4},{4,0},{8,12},{12,8},{16,20},{20,16},{24,28},{28,24},{32,36},... | collective-permute-start | bytes 3145736 | tf_op jit(solution)/shard_map/ppermute | solution.py:360
  25.5 2.4 %collective-permute-start.1 = (bf16[4,512,256]{2,1,0:T(8,128)(2,1)}, bf16[4,512,256]{2,1,0:T(8,128)(2,1)S(1)}, u32[]{:S(2)}, u32[]{:S(2)}) collective-permute-start(bf16[4,512,256]{2,1,0:T(8,128)(2,1)} %get-tuple-element.21), channel_id=1, source_target_pairs={{0,4},{4,0},{8,12},{12,8},{16,20},{20,16},{24,28},{28,24},{32,36},... | collective-permute-start | bytes 3145736 | tf_op jit(solution)/shard_map/ppermute | solution.py:360
  27.9 0.0 copy-done.4
  27.9 0.0 copy-start.3
  28.0 1.8 %copy.9 = bf16[128,8,4,256]{3,1,2,0:T(8,128)(2,1)} copy(bf16[128,8,4,256]{3,2,1,0:T(4,128)(2,1)S(1)} %bitcast.4) | data formatting | bytes 4194304
  29.8 0.0 all-to-all-done.x_any
  29.8 0.0 copy-done.3
  29.8 0.0 copy-start.1
  29.8 0.0 copy-start.2
  29.8 4.3 %shard_map.83 = (bf16[256,1024]{1,0:T(8,128)(2,1)}, bf16[256,1024]{1,0:T(8,128)(2,1)}) custom-call(bf16[4,512,256]{2,1,0:T(8,128)(2,1)S(1)} %all-to-all-done.x_any, f32[1,1024]{1,0:T(1,128)S(1)} %bitcast.3, bf16[1024,1024]{1,0:T(8,128)(2,1)} %bitcast.5), custom_call_target="tpu_custom_call" | custom-call | flops 8999999488 | bytes 4194304 | tf_op jit(solution)/shard_map/pallas_call | solution.py:150
  34.1 0.0 collective-permute-done.moved_keys
  34.1 0.0 collective-permute-done.1.rest_0_
  34.1 0.0 copy-done.1
  34.1 0.0 copy-done.2
  34.1 4.2 %shard_map.85 = bf16[4,256,256]{2,1,0:T(8,128)(2,1)} custom-call(s32[8]{0:T(128)S(1)} %copy-done.1, s32[8]{0:T(128)S(1)} %copy-done.2, bf16[256,1024]{1,0:T(8,128)(2,1)} %get-tuple-element.17.b_hbm, bf16[8,512,256]{2,1,0:T(8,128)(2,1)} %keys.7, bf16[8,512,256]{2,1,0:T(8,128)(2,1)} %values.7, bf16[256,1024]{1,0:T(8,128)(2,1)} %w_hbm.3, ...), custom_call_target="tpu_custom_call" | custom-call | flops 100000000 | tf_op jit(solution)/shard_map/pallas_call | solution.py:298
  38.3 5.5 %all-to-all-start.1 = ((bf16[4,256,256]{2,1,0:T(8,128)(2,1)}), bf16[4,256,256]{2,1,0:T(8,128)(2,1)S(1)}, u32[]{:S(2)}, u32[]{:S(2)}) async-start(bf16[4,256,256]{2,1,0:T(8,128)(2,1)} %shard_map.85), calls=%async_computation.1 | async-start | bytes 1048576 | tf_op jit(solution)/shard_map/all_to_all | solution.py:352
  43.8 0.0 copy-start
  43.8 0.0 collective-permute-done.2.moved_keys
  43.8 3.9 %shard_map.86 = bf16[4,256,256]{2,1,0:T(8,128)(2,1)S(1)} custom-call(s32[8]{0:T(128)S(1)} %copy-done.1, s32[8]{0:T(128)S(1)} %copy-done.2, bf16[256,1024]{1,0:T(8,128)(2,1)} %get-tuple-element.22.b_hbm, bf16[8,512,256]{2,1,0:T(8,128)(2,1)} %keys.7, bf16[8,512,256]{2,1,0:T(8,128)(2,1)} %values.7, bf16[256,1024]{1,0:T(8,128)(2,1)} %w_hbm.3, ...), custom_call_target="tpu_custom_call" | custom-call | flops 3000000000 | tf_op jit(solution)/shard_map/pallas_call | solution.py:298
  47.7 3.0 %all-to-all-done.1.even = bf16[4,256,256]{2,1,0:T(8,128)(2,1)S(1)} async-done(((bf16[4,256,256]{2,1,0:T(8,128)(2,1)}), bf16[4,256,256]{2,1,0:T(8,128)(2,1)S(1)}, u32[]{:S(2)}, u32[]{:S(2)}) %all-to-all-start.1) | async-done | bytes 524320 | tf_op jit(solution)/shard_map/all_to_all | solution.py:352
  50.7 10.5 %all_to_all.15.odd = bf16[4,256,256]{2,1,0:T(8,128)(2,1)S(1)} all-to-all(bf16[4,256,256]{2,1,0:T(8,128)(2,1)S(1)} %shard_map.86), channel_id=1, replica_groups=mesh['user'=128,'head'=4] {'head'}, dimensions={0} | all-to-all | bytes 1048576 | tf_op jit(solution)/shard_map/all_to_all | solution.py:352
  61.1 0.0 copy-done
  61.1 0.9 %shard_map.87 = bf16[512,256]{1,0:T(8,128)(2,1)} custom-call(bf16[512,256]{1,0:T(8,128)(2,1)S(1)} %copy-done, bf16[4,256,256]{2,1,0:T(8,128)(2,1)S(1)} %all-to-all-done.1.even, bf16[4,256,256]{2,1,0:T(8,128)(2,1)S(1)} %all_to_all.15.odd), custom_call_target="tpu_custom_call" | custom-call | tf_op jit(solution)/shard_map/pallas_call | solution.py:332
Async XLA Ops:
  2.9 40.9 %collective-permute-start.2 = (bf16[8,512,256]{2,1,0:T(8,128)(2,1)}, bf16[8,512,256]{2,1,0:T(8,128)(2,1)}, u32[]{:S(2)}, u32[]{:S(2)}) collective-permute-start(bf16[8,512,256]{2,1,0:T(8,128)(2,1)} %get-tuple-element.18), channel_id=1, source_target_pairs={{0,508},{4,8},{8,4},{12,16},{16,12},{20,24},{24,20},{28,32},{32,28... | collective-permute-start | bytes 6291464 | tf_op jit(solution)/shard_map/ppermute | solution.py:356
  16.2 13.6 %all-to-all-start = ((bf16[4,512,256]{2,1,0:T(8,128)(2,1)}), bf16[4,512,256]{2,1,0:T(8,128)(2,1)S(1)}, u32[]{:S(2)}, u32[]{:S(2)}) async-start(bf16[4,512,256]{2,1,0:T(8,128)(2,1)} %get-tuple-element.15), calls=%async_computation | async-start | bytes 2097152 | tf_op jit(solution)/shard_map/all_to_all | solution.py:352
  21.0 7.0 %copy-start.4 = (bf16[1024,4,256]{2,1,0:T(4,128)(2,1)S(1)}, bf16[1024,4,256]{2,1,0:T(4,128)(2,1)}, u32[]{:S(2)}) copy-start(bf16[1024,4,256]{2,1,0:T(4,128)(2,1)} %param.10) | copy-start | bytes 6291460
  23.6 10.5 %collective-permute-start = (bf16[4,512,256]{2,1,0:T(8,128)(2,1)}, bf16[4,512,256]{2,1,0:T(8,128)(2,1)S(1)}, u32[]{:S(2)}, u32[]{:S(2)}) collective-permute-start(bf16[4,512,256]{2,1,0:T(8,128)(2,1)} %get-tuple-element.20), channel_id=1, source_target_pairs={{0,4},{4,0},{8,12},{12,8},{16,20},{20,16},{24,28},{28,24},{32,36},... | collective-permute-start | bytes 3145736 | tf_op jit(solution)/shard_map/ppermute | solution.py:360
  25.5 8.6 %collective-permute-start.1 = (bf16[4,512,256]{2,1,0:T(8,128)(2,1)}, bf16[4,512,256]{2,1,0:T(8,128)(2,1)S(1)}, u32[]{:S(2)}, u32[]{:S(2)}) collective-permute-start(bf16[4,512,256]{2,1,0:T(8,128)(2,1)} %get-tuple-element.21), channel_id=1, source_target_pairs={{0,4},{4,0},{8,12},{12,8},{16,20},{20,16},{24,28},{28,24},{32,36},... | collective-permute-start | bytes 3145736 | tf_op jit(solution)/shard_map/ppermute | solution.py:360
  27.9 1.9 %copy-start.3 = (f32[1024]{0:T(1024)S(1)}, f32[1024]{0:T(1024)}, u32[]{:S(2)}) copy-start(f32[1024]{0:T(1024)} %param.9) | copy-start | bytes 12292
  29.8 4.3 %copy-start.1 = (s32[8]{0:T(128)S(1)}, s32[8]{0:T(128)}, u32[]{:S(2)}) copy-start(s32[8]{0:T(128)} %lengths.3) | copy-start | bytes 100
  29.8 4.3 %copy-start.2 = (s32[8]{0:T(128)S(1)}, s32[8]{0:T(128)}, u32[]{:S(2)}) copy-start(s32[8]{0:T(128)} %offsets.3) | copy-start | bytes 100
  38.3 12.4 %all-to-all-start.1 = ((bf16[4,256,256]{2,1,0:T(8,128)(2,1)}), bf16[4,256,256]{2,1,0:T(8,128)(2,1)S(1)}, u32[]{:S(2)}, u32[]{:S(2)}) async-start(bf16[4,256,256]{2,1,0:T(8,128)(2,1)} %shard_map.85), calls=%async_computation.1 | async-start | bytes 1048576 | tf_op jit(solution)/shard_map/all_to_all | solution.py:352
  43.8 17.4 %copy-start = (bf16[512,256]{1,0:T(8,128)(2,1)S(1)}, bf16[512,256]{1,0:T(8,128)(2,1)}, u32[]{:S(2)}) copy-start(bf16[512,256]{1,0:T(8,128)(2,1)} %events.1) | copy-start | bytes 786436

commit v5 on v4

--- a/solution.py
+++ b/solution.py
@@ -162,7 +162,7 @@
         ],
         compiler_params=pltpu.CompilerParams(vmem_limit_bytes=20 * 2**20),
         cost_estimate=pl.CostEstimate(
-            flops=9 * 10**9,
+            flops=40 * 10**9,
             bytes_accessed=2 * (w.size + 2 * x4.size),
             transcendentals=total * wide,
         ),

time: 63.1 us -> 63.2 us (level)
  starting transfers between devices: 27.9 us -> 26.8 us
  waiting for transfers between devices: 2.98 us -> 3.68 us
  blocking collectives: 10.5 us -> 11.2 us
    ppermute x1, starting transfers between devices: 13.3 us -> 8.28 us  [on_device(): odd = [lax.ppermute(odd_pay, 'user', across)]]
    all_to_all x2, starting transfers between devices: 10.3 us -> 14.2 us  [to_heads(): return lax.all_to_all(blocks, 'head', 0, 0)]
    ppermute x1, waiting for transfers between devices: 0.01 us -> 2.04 us  [on_device(): odd = [lax.ppermute(odd_pay, 'user', across)]]
    all_to_all x2, waiting for transfers between devices: 2.97 us -> 1.63 us  [to_heads(): return lax.all_to_all(blocks, 'head', 0, 0)]
    all_to_all x1, blocking collectives: 10.5 us -> 11.2 us  [to_heads(): return lax.all_to_all(blocks, 'head', 0, 0)]
  transfers between devices with their start and end apart: 5 -> 5, of which waited for: 1 -> 2; matrix products, arithmetic and copies ran while one was open for 3% -> 3% of each run, Pallas kernels for 24% -> 24%
where the time goes in v5:
time: 63.2 us; the launch traced here: 62.1 us
  starting transfers between devices  26.8 us (42%)
  Pallas kernels  18.5 us (29%)
  blocking collectives  11.2 us (18%)
  waiting for transfers between devices  3.68 us (6%)
  local copies, waits for them, and re-layouts  1.86 us (3%)
    all_to_all x2, starting transfers between devices, to_heads(): return lax.all_to_all(blocks, 'head', 0, 0)  14.2 us
    all_to_all x1, blocking collectives, to_heads(): return lax.all_to_all(blocks, 'head', 0, 0)  11.2 us
    ppermute x1, starting transfers between devices, on_device(): odd = [lax.ppermute(odd_pay, 'user', across)]  8.28 us
    pallas_call x2, Pallas kernels, serve(): pl.pallas_call(functools.partial(serve_kernel, side), out_shape=jax.Shape...  8.05 us
    pallas_call x2, Pallas kernels, pack(): pl.pallas_call(functools.partial(pack_kernel, side), out_shape=outs, in_s...  5.34 us
    ppermute x2, starting transfers between devices, on_device(): lax.ppermute(pay, 'user', within)  4.33 us
    pallas_call x1, Pallas kernels, project(): pl.pallas_call(project_kernel, out_shape=(out, out), in_specs=[ANY, VMEM,...  4.25 us
    ppermute x1, waiting for transfers between devices, on_device(): odd = [lax.ppermute(odd_pay, 'user', across)]  2.04 us
  transfers between devices with their start and end apart: 5, of which 2 were waited for; matrix products, arithmetic and copies ran while one was open for 3% of the time, Pallas kernels for 24%

profile of v5, /device:TPU:6, one launch (start us, length us, event | category | flops | bytes accessed | tf_op | source)
XLA Modules:
  0.0 62.1 jit_solution(5228071786260665221)
XLA Ops:
  0.0 2.9 %shard_map.82 = (bf16[8,512,256]{2,1,0:T(8,128)(2,1)}, bf16[4,512,256]{2,1,0:T(8,128)(2,1)}) custom-call(s32[8]{0:T(128)} %lengths.3, bf16[8,512,256]{2,1,0:T(8,128)(2,1)} %keys.7, bf16[8,512,256]{2,1,0:T(8,128)(2,1)} %values.7, bf16[512,256]{1,0:T(8,128)(2,1)} %events.1), custom_call_target="tpu_custom_call" | custom-call | bytes 4000000 | tf_op jit(solution)/shard_map/pallas_call | solution.py:76
  2.9 9.4 %all-to-all-start = ((bf16[4,512,256]{2,1,0:T(8,128)(2,1)}), bf16[4,512,256]{2,1,0:T(8,128)(2,1)S(1)}, u32[]{:S(2)}, u32[]{:S(2)}) async-start(bf16[4,512,256]{2,1,0:T(8,128)(2,1)} %get-tuple-element.15), calls=%async_computation | async-start | bytes 2097152 | tf_op jit(solution)/shard_map/all_to_all | solution.py:352
  12.2 0.0 copy-start.4
  12.2 8.3 %collective-permute-start.2 = (bf16[8,512,256]{2,1,0:T(8,128)(2,1)}, bf16[8,512,256]{2,1,0:T(8,128)(2,1)}, u32[]{:S(2)}, u32[]{:S(2)}) collective-permute-start(bf16[8,512,256]{2,1,0:T(8,128)(2,1)} %get-tuple-element.18), channel_id=1, source_target_pairs={{0,508},{4,8},{8,4},{12,16},{16,12},{20,24},{24,20},{28,32},{32,28... | collective-permute-start | bytes 6291464 | tf_op jit(solution)/shard_map/ppermute | solution.py:356
  20.5 2.5 %shard_map.84 = (bf16[4,512,256]{2,1,0:T(8,128)(2,1)}, bf16[4,512,256]{2,1,0:T(8,128)(2,1)}) custom-call(s32[8]{0:T(128)} %lengths.3, bf16[8,512,256]{2,1,0:T(8,128)(2,1)} %keys.7, bf16[8,512,256]{2,1,0:T(8,128)(2,1)} %values.7), custom_call_target="tpu_custom_call" | custom-call | bytes 15000000 | tf_op jit(solution)/shard_map/pallas_call | solution.py:76
  23.0 1.9 %collective-permute-start = (bf16[4,512,256]{2,1,0:T(8,128)(2,1)}, bf16[4,512,256]{2,1,0:T(8,128)(2,1)S(1)}, u32[]{:S(2)}, u32[]{:S(2)}) collective-permute-start(bf16[4,512,256]{2,1,0:T(8,128)(2,1)} %get-tuple-element.20), channel_id=1, source_target_pairs={{0,4},{4,0},{8,12},{12,8},{16,20},{20,16},{24,28},{28,24},{32,36},... | collective-permute-start | bytes 3145736 | tf_op jit(solution)/shard_map/ppermute | solution.py:360
  24.9 2.4 %collective-permute-start.1 = (bf16[4,512,256]{2,1,0:T(8,128)(2,1)}, bf16[4,512,256]{2,1,0:T(8,128)(2,1)S(1)}, u32[]{:S(2)}, u32[]{:S(2)}) collective-permute-start(bf16[4,512,256]{2,1,0:T(8,128)(2,1)} %get-tuple-element.21), channel_id=1, source_target_pairs={{0,4},{4,0},{8,12},{12,8},{16,20},{20,16},{24,28},{28,24},{32,36},... | collective-permute-start | bytes 3145736 | tf_op jit(solution)/shard_map/ppermute | solution.py:360
  27.3 0.0 copy-done.4
  27.4 0.0 copy-start.3
  27.4 1.8 %copy.9 = bf16[128,8,4,256]{3,1,2,0:T(8,128)(2,1)} copy(bf16[128,8,4,256]{3,2,1,0:T(4,128)(2,1)S(1)} %bitcast.4) | data formatting | bytes 4194304
  29.2 0.0 all-to-all-done.x_any
  29.2 0.0 copy-done.3
  29.2 0.0 copy-start.1
  29.2 0.0 copy-start.2
  29.2 4.3 %shard_map.83 = (bf16[256,1024]{1,0:T(8,128)(2,1)}, bf16[256,1024]{1,0:T(8,128)(2,1)}) custom-call(bf16[4,512,256]{2,1,0:T(8,128)(2,1)S(1)} %all-to-all-done.x_any, f32[1,1024]{1,0:T(1,128)S(1)} %bitcast.3, bf16[1024,1024]{1,0:T(8,128)(2,1)} %bitcast.5), custom_call_target="tpu_custom_call" | custom-call | flops 40000000000 | bytes 4194304 | tf_op jit(solution)/shard_map/pallas_call | solution.py:150
  33.5 0.0 collective-permute-done.moved_keys
  33.5 0.0 collective-permute-done.1.rest_0_
  33.5 0.0 copy-done.1
  33.5 0.0 copy-done.2
  33.5 4.1 %shard_map.85 = bf16[4,256,256]{2,1,0:T(8,128)(2,1)} custom-call(s32[8]{0:T(128)S(1)} %copy-done.1, s32[8]{0:T(128)S(1)} %copy-done.2, bf16[256,1024]{1,0:T(8,128)(2,1)} %get-tuple-element.17.b_hbm, bf16[8,512,256]{2,1,0:T(8,128)(2,1)} %keys.7, bf16[8,512,256]{2,1,0:T(8,128)(2,1)} %values.7, bf16[256,1024]{1,0:T(8,128)(2,1)} %w_hbm.3, ...), custom_call_target="tpu_custom_call" | custom-call | flops 100000000 | tf_op jit(solution)/shard_map/pallas_call | solution.py:298
  37.7 4.8 %all-to-all-start.1 = ((bf16[4,256,256]{2,1,0:T(8,128)(2,1)}), bf16[4,256,256]{2,1,0:T(8,128)(2,1)S(1)}, u32[]{:S(2)}, u32[]{:S(2)}) async-start(bf16[4,256,256]{2,1,0:T(8,128)(2,1)} %shard_map.85), calls=%async_computation.1 | async-start | bytes 1048576 | tf_op jit(solution)/shard_map/all_to_all | solution.py:352
  42.5 0.0 copy-start
  42.5 2.0 %collective-permute-done.2.moved_keys = bf16[8,512,256]{2,1,0:T(8,128)(2,1)} collective-permute-done((bf16[8,512,256]{2,1,0:T(8,128)(2,1)}, bf16[8,512,256]{2,1,0:T(8,128)(2,1)}, u32[]{:S(2)}, u32[]{:S(2)}) %collective-permute-start.2) | collective-permute-done | bytes 2097184 | tf_op jit(solution)/shard_map/ppermute | solution.py:356
  44.5 3.9 %shard_map.86 = bf16[4,256,256]{2,1,0:T(8,128)(2,1)S(1)} custom-call(s32[8]{0:T(128)S(1)} %copy-done.1, s32[8]{0:T(128)S(1)} %copy-done.2, bf16[256,1024]{1,0:T(8,128)(2,1)} %get-tuple-element.22.b_hbm, bf16[8,512,256]{2,1,0:T(8,128)(2,1)} %keys.7, bf16[8,512,256]{2,1,0:T(8,128)(2,1)} %values.7, bf16[256,1024]{1,0:T(8,128)(2,1)} %w_hbm.3, ...), custom_call_target="tpu_custom_call" | custom-call | flops 3000000000 | tf_op jit(solution)/shard_map/pallas_call | solution.py:298
  48.4 1.6 %all-to-all-done.1.even = bf16[4,256,256]{2,1,0:T(8,128)(2,1)S(1)} async-done(((bf16[4,256,256]{2,1,0:T(8,128)(2,1)}), bf16[4,256,256]{2,1,0:T(8,128)(2,1)S(1)}, u32[]{:S(2)}, u32[]{:S(2)}) %all-to-all-start.1) | async-done | bytes 524320 | tf_op jit(solution)/shard_map/all_to_all | solution.py:352
  50.1 11.2 %all_to_all.15.odd = bf16[4,256,256]{2,1,0:T(8,128)(2,1)S(1)} all-to-all(bf16[4,256,256]{2,1,0:T(8,128)(2,1)S(1)} %shard_map.86), channel_id=1, replica_groups=mesh['user'=128,'head'=4] {'head'}, dimensions={0} | all-to-all | bytes 1048576 | tf_op jit(solution)/shard_map/all_to_all | solution.py:352
  61.2 0.0 copy-done
  61.2 0.9 %shard_map.87 = bf16[512,256]{1,0:T(8,128)(2,1)} custom-call(bf16[512,256]{1,0:T(8,128)(2,1)S(1)} %copy-done, bf16[4,256,256]{2,1,0:T(8,128)(2,1)S(1)} %all-to-all-done.1.even, bf16[4,256,256]{2,1,0:T(8,128)(2,1)S(1)} %all_to_all.15.odd), custom_call_target="tpu_custom_call" | custom-call | tf_op jit(solution)/shard_map/pallas_call | solution.py:332
Async XLA Ops:
  2.9 26.3 %all-to-all-start = ((bf16[4,512,256]{2,1,0:T(8,128)(2,1)}), bf16[4,512,256]{2,1,0:T(8,128)(2,1)S(1)}, u32[]{:S(2)}, u32[]{:S(2)}) async-start(bf16[4,512,256]{2,1,0:T(8,128)(2,1)} %get-tuple-element.15), calls=%async_computation | async-start | bytes 2097152 | tf_op jit(solution)/shard_map/all_to_all | solution.py:352
  12.2 15.1 %copy-start.4 = (bf16[1024,4,256]{2,1,0:T(4,128)(2,1)S(1)}, bf16[1024,4,256]{2,1,0:T(4,128)(2,1)}, u32[]{:S(2)}) copy-start(bf16[1024,4,256]{2,1,0:T(4,128)(2,1)} %param.10) | copy-start | bytes 6291460
  12.2 32.3 %collective-permute-start.2 = (bf16[8,512,256]{2,1,0:T(8,128)(2,1)}, bf16[8,512,256]{2,1,0:T(8,128)(2,1)}, u32[]{:S(2)}, u32[]{:S(2)}) collective-permute-start(bf16[8,512,256]{2,1,0:T(8,128)(2,1)} %get-tuple-element.18), channel_id=1, source_target_pairs={{0,508},{4,8},{8,4},{12,16},{16,12},{20,24},{24,20},{28,32},{32,28... | collective-permute-start | bytes 6291464 | tf_op jit(solution)/shard_map/ppermute | solution.py:356
  23.0 10.5 %collective-permute-start = (bf16[4,512,256]{2,1,0:T(8,128)(2,1)}, bf16[4,512,256]{2,1,0:T(8,128)(2,1)S(1)}, u32[]{:S(2)}, u32[]{:S(2)}) collective-permute-start(bf16[4,512,256]{2,1,0:T(8,128)(2,1)} %get-tuple-element.20), channel_id=1, source_target_pairs={{0,4},{4,0},{8,12},{12,8},{16,20},{20,16},{24,28},{28,24},{32,36},... | collective-permute-start | bytes 3145736 | tf_op jit(solution)/shard_map/ppermute | solution.py:360
  24.9 8.6 %collective-permute-start.1 = (bf16[4,512,256]{2,1,0:T(8,128)(2,1)}, bf16[4,512,256]{2,1,0:T(8,128)(2,1)S(1)}, u32[]{:S(2)}, u32[]{:S(2)}) collective-permute-start(bf16[4,512,256]{2,1,0:T(8,128)(2,1)} %get-tuple-element.21), channel_id=1, source_target_pairs={{0,4},{4,0},{8,12},{12,8},{16,20},{20,16},{24,28},{28,24},{32,36},... | collective-permute-start | bytes 3145736 | tf_op jit(solution)/shard_map/ppermute | solution.py:360
  27.4 1.9 %copy-start.3 = (f32[1024]{0:T(1024)S(1)}, f32[1024]{0:T(1024)}, u32[]{:S(2)}) copy-start(f32[1024]{0:T(1024)} %param.9) | copy-start | bytes 12292
  29.2 4.3 %copy-start.1 = (s32[8]{0:T(128)S(1)}, s32[8]{0:T(128)}, u32[]{:S(2)}) copy-start(s32[8]{0:T(128)} %lengths.3) | copy-start | bytes 100
  29.2 4.3 %copy-start.2 = (s32[8]{0:T(128)S(1)}, s32[8]{0:T(128)}, u32[]{:S(2)}) copy-start(s32[8]{0:T(128)} %offsets.3) | copy-start | bytes 100
  37.7 12.4 %all-to-all-start.1 = ((bf16[4,256,256]{2,1,0:T(8,128)(2,1)}), bf16[4,256,256]{2,1,0:T(8,128)(2,1)S(1)}, u32[]{:S(2)}, u32[]{:S(2)}) async-start(bf16[4,256,256]{2,1,0:T(8,128)(2,1)} %shard_map.85), calls=%async_computation.1 | async-start | bytes 1048576 | tf_op jit(solution)/shard_map/all_to_all | solution.py:352
  42.5 18.8 %copy-start = (bf16[512,256]{1,0:T(8,128)(2,1)S(1)}, bf16[512,256]{1,0:T(8,128)(2,1)}, u32[]{:S(2)}) copy-start(bf16[512,256]{1,0:T(8,128)(2,1)} %events.1) | copy-start | bytes 786436

commit v6 on v5

--- a/solution.py
+++ b/solution.py
@@ -93,82 +93,6 @@
     )(*operands)
 
 
-def project_kernel(x_any, gain_ref, w_hbm, even_hbm, odd_hbm, x_ref, w_ref, b_ref, x_sems, w_sem, b_sems):
-    parts, total, width = x_ref.shape
-    features = parts * width
-    chunks = x_sems.shape[0]
-    rows = total // chunks
-    x_copies = []
-    for i in range(chunks):
-        at = pl.ds(i * rows, rows)
-        x_copies.append(
-            pltpu.make_async_copy(x_any.at[:, at, :], x_ref.at[:, at, :], x_sems.at[i])
-        )
-    w_copy = pltpu.make_async_copy(w_hbm, w_ref, w_sem.at[0])
-    x_copies[0].start()
-    w_copy.start()
-    for c in x_copies[1:]:
-        c.start()
-    gain = gain_ref[...]
-
-    def normalise(i):
-        x = jnp.concatenate(
-            [x_ref[p, i * rows : (i + 1) * rows, :] for p in range(parts)], axis=1
-        ).astype(jnp.float32)
-        average = jnp.sum(x, axis=-1, keepdims=True) * (1.0 / features)
-        centred = x - average
-        spread = jnp.sum(centred * centred, axis=-1, keepdims=True) * (1.0 / features)
-        return (centred * lax.rsqrt(spread + 1e-05) * gain).astype(jnp.bfloat16)
-
-    leave = []
-    for i in range(chunks):
-        x_copies[i].wait()
-        normed = normalise(i)
-        if i == 0:
-            w_copy.wait()
-        half = 0.5 * lax.dot_general(normed, w_ref[...], NN, preferred_element_type=jnp.float32)
-        branch = (half + half * jnp.tanh(half)).astype(jnp.bfloat16)
-        held = rows // (2 * NEW)
-        for k in range(2 * held):
-            s = i * held + k // 2
-            b_ref[k % 2, s * NEW : (s + 1) * NEW, :] = branch[k * NEW : (k + 1) * NEW, :]
-        for side, target in enumerate((even_hbm, odd_hbm)):
-            at = pl.ds(i * held * NEW, held * NEW)
-            copy = pltpu.make_async_copy(
-                b_ref.at[side, at], target.at[at], b_sems.at[2 * i + side]
-            )
-            copy.start()
-            leave.append(copy)
-    for c in leave:
-        c.wait()
-
-
-def project(x4, gain, w):
-    parts, total, width = x4.shape
-    chunks, wide = 2, w.shape[1]
-    out = pltpu.HBM((total // 2, wide), jnp.bfloat16)
-    return pl.pallas_call(
-        project_kernel,
-        out_shape=(out, out),
-        in_specs=[ANY, VMEM, HBM],
-        out_specs=(HBM, HBM),
-        scratch_shapes=[
-            pltpu.VMEM(x4.shape, jnp.bfloat16),
-            pltpu.VMEM(w.shape, jnp.bfloat16),
-            pltpu.VMEM((2, total // 2, wide), jnp.bfloat16),
-            pltpu.SemaphoreType.DMA((chunks,)),
-            pltpu.SemaphoreType.DMA((1,)),
-            pltpu.SemaphoreType.DMA((2 * chunks,)),
-        ],
-        compiler_params=pltpu.CompilerParams(vmem_limit_bytes=20 * 2**20),
-        cost_estimate=pl.CostEstimate(
-            flops=40 * 10**9,
-            bytes_accessed=2 * (w.size + 2 * x4.size),
-            transcendentals=total * wide,
-        ),
-    )(x4, gain, in_hbm(w))
-
-
 def cache_copies(side, offsets, keys, values, moved_keys, moved_values, kv, sems):
     half_slots = kv.shape[0] // 2
     waits = []
@@ -197,10 +121,10 @@
             def _():
                 traded[kind].start()
 
-    return [own for _, own, _ in waits]
-
-
-def attend_slots(side, lengths, offsets, b_ref, kv, waits, gated):
+    return [c for _, own, _ in waits for c in own]
+
+
+def attend_slots(side, lengths, offsets, b_ref, kv, gated):
     half_slots, cap, width = kv.shape[0] // 2, kv.shape[1], kv.shape[2]
     new = b_ref.shape[0] // half_slots
     heads = width // HEAD
@@ -249,11 +173,7 @@
                 result = result + centred * lax.rsqrt(spread + 1e-05)
             gated[at, lanes] = (result * gate[:, lanes]).astype(jnp.bfloat16)
 
-    for c in [pair[0] for pair in waits]:
-        c.wait()
     weights = [weigh(s) for s in range(half_slots)]
-    for c in [pair[1] for pair in waits]:
-        c.wait()
     for s in range(half_slots):
         finish(s, *weights[s])
 
@@ -268,37 +188,100 @@
         ).astype(jnp.bfloat16)
 
 
-def serve_kernel(
-    side, lengths, offsets, b_hbm, keys, values, w_hbm, moved_keys, *rest
+def first_kernel(
+    lengths, offsets, x_any, gain_ref, w_hbm, keys, values, wo_hbm, moved_keys, moved_values,
+    out_ref, odd_hbm,
+    x_ref, w_ref, wo_ref, kv, normed_ref, even_ref, odd_ref, gated, sems, kv_sems,
 ):
-    moved_values = None
-    if side == 0:
-        moved_values, *rest = rest
-    out_ref, b_ref, w_ref, kv, gated, sems, kv_sems = rest
+    parts, total, width = x_ref.shape
+    features = parts * width
+    x_copy = pltpu.make_async_copy(x_any, x_ref, sems.at[0])
+    rest = [
+        pltpu.make_async_copy(w_hbm, w_ref, sems.at[1]),
+        pltpu.make_async_copy(wo_hbm, wo_ref, sems.at[2]),
+    ]
+    for c in [x_copy] + rest:
+        c.start()
+    rest += cache_copies(0, offsets, keys, values, moved_keys, moved_values, kv, kv_sems)
+    x_copy.wait()
+    x = jnp.concatenate([x_ref[p] for p in range(parts)], axis=1).astype(jnp.float32)
+    average = jnp.sum(x, axis=-1, keepdims=True) * (1.0 / features)
+    centred = x - average
+    spread = jnp.sum(centred * centred, axis=-1, keepdims=True) * (1.0 / features)
+    normed = centred * lax.rsqrt(spread + 1e-05) * gain_ref[...]
+    normed_ref[...] = normed.astype(jnp.bfloat16)
+
+    for c in rest:
+        c.wait()
+    half = 0.5 * lax.dot_general(
+        normed_ref[...], w_ref[...], NN, preferred_element_type=jnp.float32
+    )
+    branch = (half + half * jnp.tanh(half)).astype(jnp.bfloat16)
+    for j in range(total // NEW):
+        target = odd_ref if j % 2 else even_ref
+        target[(j // 2) * NEW : (j // 2 + 1) * NEW, :] = branch[j * NEW : (j + 1) * NEW, :]
+
+    odd_copy = pltpu.make_async_copy(odd_ref, odd_hbm, sems.at[3])
+    odd_copy.start()
+    attend_slots(0, lengths, offsets, even_ref, kv, gated)
+    project_out(gated, wo_ref, out_ref, width)
+    odd_copy.wait()
+
+
+def second_kernel(
+    lengths, offsets, b_hbm, keys, values, w_hbm, moved, out_ref, b_ref, w_ref, kv, gated, sems, kv_sems
+):
     half_slots, width = kv.shape[0] // 2, kv.shape[2]
-    if side == 1:
-        moved_keys, moved_values = moved_keys.at[:half_slots], moved_keys.at[half_slots:]
-    b_copy = pltpu.make_async_copy(b_hbm, b_ref, sems.at[0])
-    w_copy = pltpu.make_async_copy(w_hbm, w_ref, sems.at[1])
-    b_copy.start()
-    waits = cache_copies(side, offsets, keys, values, moved_keys, moved_values, kv, kv_sems)
-    w_copy.start()
-    b_copy.wait()
-    attend_slots(side, lengths, offsets, b_ref, kv, waits, gated)
-    w_copy.wait()
+    copies = [
+        pltpu.make_async_copy(b_hbm, b_ref, sems.at[0]),
+        pltpu.make_async_copy(w_hbm, w_ref, sems.at[1]),
+    ]
+    for c in copies:
+        c.start()
+    moved_keys, moved_values = moved.at[:half_slots], moved.at[half_slots:]
+    copies += cache_copies(1, offsets, keys, values, moved_keys, moved_values, kv, kv_sems)
+    for c in copies:
+        c.wait()
+    attend_slots(1, lengths, offsets, b_ref, kv, gated)
     project_out(gated, w_ref, out_ref, width)
 
 
-def serve(side, lengths, offsets, branches, keys, values, w_out, moved):
+def first(lengths, offsets, x4, gain, w, keys, values, w_out, moved):
+    slots, cap, width = keys.shape
+    parts, total, _ = x4.shape
+    half, wide = total // 2, w.shape[1]
+    bf16 = jnp.bfloat16
+    return pl.pallas_call(
+        first_kernel,
+        out_shape=(jax.ShapeDtypeStruct((parts, half, width), bf16), pltpu.HBM((half, wide), bf16)),
+        in_specs=[SMEM, SMEM, ANY, VMEM, HBM, HBM, HBM, HBM, ANY, ANY],
+        out_specs=(VMEM, HBM),
+        scratch_shapes=[
+            pltpu.VMEM(x4.shape, bf16),
+            pltpu.VMEM(w.shape, bf16),
+            pltpu.VMEM(w_out.shape, bf16),
+            pltpu.VMEM((slots, cap, width), bf16),
+            pltpu.VMEM((total, parts * width), bf16),
+            pltpu.VMEM((half, wide), bf16),
+            pltpu.VMEM((half, wide), bf16),
+            pltpu.VMEM((half, width), bf16),
+            pltpu.SemaphoreType.DMA((4,)),
+            pltpu.SemaphoreType.DMA((slots,)),
+        ],
+        compiler_params=pltpu.CompilerParams(vmem_limit_bytes=28 * 2**20),
+        cost_estimate=pl.CostEstimate(flops=10**8, bytes_accessed=0, transcendentals=0),
+    )(lengths, offsets, x4, gain, in_hbm(w), in_hbm(keys), in_hbm(values), in_hbm(w_out), *moved)
+
+
+def second(lengths, offsets, branches, keys, values, w_out, moved):
     slots, cap, width = keys.shape
     parts, rows = w_out.shape[1] // width, branches.shape[0]
     bf16 = jnp.bfloat16
-    operands = [in_hbm(a) for a in (branches, keys, values, w_out)]
-    operands += [in_hbm(a) for a in moved] if side else moved
-    return pl.pallas_call(
-        functools.partial(serve_kernel, side),
+    operands = [in_hbm(a) for a in (branches, keys, values, w_out, moved)]
+    return pl.pallas_call(
+        second_kernel,
         out_shape=jax.ShapeDtypeStruct((parts, rows, width), bf16),
-        in_specs=[SMEM, SMEM] + [HBM] * 4 + [HBM if side else ANY] * len(moved),
+        in_specs=[SMEM, SMEM] + [HBM] * len(operands),
         out_specs=VMEM,
         scratch_shapes=[
             pltpu.VMEM(branches.shape, bf16),
@@ -309,10 +292,23 @@
             pltpu.SemaphoreType.DMA((slots,)),
         ],
         compiler_params=pltpu.CompilerParams(vmem_limit_bytes=20 * 2**20),
-        cost_estimate=pl.CostEstimate(
-            flops=3 * 10**9 if side else 10**8, bytes_accessed=0, transcendentals=0
-        ),
+        cost_estimate=pl.CostEstimate(flops=3 * 10**9, bytes_accessed=0, transcendentals=0),
     )(lengths, offsets, *operands)
+
+
+def gate_kernel(x_any, gain_ref, out_ref):
+    del x_any
+    out_ref[...] = gain_ref[...]
+
+
+def gain_after(x4, gain):
+    return pl.pallas_call(
+        gate_kernel,
+        out_shape=jax.ShapeDtypeStruct(gain.shape, gain.dtype),
+        in_specs=[ANY, VMEM],
+        out_specs=VMEM,
+        cost_estimate=pl.CostEstimate(flops=9 * 10**9, bytes_accessed=0, transcendentals=0),
+    )(x4, gain)
 
 
 def combine_kernel(events, even, odd, out_ref):
@@ -353,18 +349,19 @@
 
     odd_pay, spread = pack(1, 1, lengths, *caches, events, heads)
     across = [(i, (((i + 1) ^ 1) - 1) % users) for i in range(users)]
-    odd = [lax.ppermute(odd_pay, "user", across)]
+    odd = lax.ppermute(odd_pay, "user", across)
     gathered = to_heads(spread)
     later_lengths, _ = lax.optimization_barrier((lengths, odd_pay))
     within = [(i, i ^ 1) for i in range(users)]
     even = [lax.ppermute(pay, "user", within) for pay in pack(0, 2, later_lengths, *caches)]
 
     w = w_uvqk.reshape(w_uvqk.shape[0], 4 * width)
-    even_branches, odd_branches = project(gathered, norm_gain[None, :], w)
-    even_part = serve(0, lengths, swap_offset, even_branches, *caches, w_out, even)
+    gain = gain_after(gathered, norm_gain[None, :])
+    even_part, odd_branches = first(
+        lengths, swap_offset, gathered, gain, w, *caches, w_out, even
+    )
     even_terms = to_heads(even_part)
-    later_branches, _ = lax.optimization_barrier((odd_branches, even_part))
-    odd_part = serve(1, lengths, swap_offset, later_branches, *caches, w_out, odd)
+    odd_part = second(lengths, swap_offset, odd_branches, *caches, w_out, odd)
     odd_part, even_terms = lax.optimization_barrier((odd_part, even_terms))
     odd_terms = to_heads(odd_part)
     return combine(events, even_terms, odd_terms)

time: 63.2 us -> 64.9 us (1.027)
  local copies, waits for them, and re-layouts: 1.86 us -> 4.77 us
  starting transfers between devices: 26.8 us -> 27.9 us
  Pallas kernels: 18.5 us -> 17.5 us
  blocking collectives: 11.2 us -> 10.5 us
  waiting for transfers between devices: 3.68 us -> 2.99 us
    ppermute x1, starting transfers between devices: 8.28 us -> 13.3 us  [on_device(): odd = lax.ppermute(odd_pay, 'user', across)]
    all_to_all x2, starting transfers between devices: 14.2 us -> 10.3 us  [to_heads(): return lax.all_to_all(blocks, 'head', 0, 0)]
    unnamed x11 -> x15, local copies, waits for them, and re-layouts: 1.86 us -> 4.77 us
    ppermute x1, waiting for transfers between devices: 2.04 us -> 0.01 us  [on_device(): odd = lax.ppermute(odd_pay, 'user', across)]
    all_to_all x2, waiting for transfers between devices: 1.63 us -> 2.98 us  [to_heads(): return lax.all_to_all(blocks, 'head', 0, 0)]
    pallas_call x3, Pallas kernels: 12.3 us -> 11.2 us  [the longest x1 5.97 us: first(): pl.pallas_call(first_kernel, out_shape=(jax.ShapeDtypeStruct((parts, half...]
    all_to_all x1, blocking collectives: 11.2 us -> 10.5 us  [to_heads(): return lax.all_to_all(blocks, 'head', 0, 0)]
  transfers between devices with their start and end apart: 5 -> 5, of which waited for: 2 -> 1; matrix products, arithmetic and copies ran while one was open for 3% -> 3% of each run, Pallas kernels for 24% -> 22%
where the time goes in v6:
time: 64.9 us; the launch traced here: 63.7 us
  starting transfers between devices  27.9 us (43%)
  Pallas kernels  17.5 us (27%)
  blocking collectives  10.5 us (16%)
  local copies, waits for them, and re-layouts  4.77 us (7%)
  waiting for transfers between devices  2.99 us (5%)
    ppermute x1, starting transfers between devices, on_device(): odd = lax.ppermute(odd_pay, 'user', across)  13.3 us
    all_to_all x1, blocking collectives, to_heads(): return lax.all_to_all(blocks, 'head', 0, 0)  10.5 us
    all_to_all x2, starting transfers between devices, to_heads(): return lax.all_to_all(blocks, 'head', 0, 0)  10.3 us
    pallas_call x1, Pallas kernels, first(): pl.pallas_call(first_kernel, out_shape=(jax.ShapeDtypeStruct((parts, half...  5.97 us
    pallas_call x2, Pallas kernels, pack(): pl.pallas_call(functools.partial(pack_kernel, side), out_shape=outs, in_s...  5.42 us
    unnamed x15, local copies, waits for them, and re-layouts  4.77 us
    ppermute x2, starting transfers between devices, on_device(): lax.ppermute(pay, 'user', within)  4.33 us
    pallas_call x1, Pallas kernels, second(): pl.pallas_call(second_kernel, out_shape=jax.ShapeDtypeStruct((parts, rows...  3.89 us
  transfers between devices with their start and end apart: 5, of which 1 were waited for; matrix products, arithmetic and copies ran while one was open for 3% of the time, Pallas kernels for 22%

profile of v6, /device:TPU:6, one launch (start us, length us, event | category | flops | bytes accessed | tf_op | source)
XLA Modules:
  0.0 63.7 jit_solution(9548118092336031355)
XLA Ops:
  0.0 2.8 %shard_map.82 = (bf16[8,512,256]{2,1,0:T(8,128)(2,1)}, bf16[4,512,256]{2,1,0:T(8,128)(2,1)}) custom-call(s32[8]{0:T(128)} %lengths.3, bf16[8,512,256]{2,1,0:T(8,128)(2,1)} %keys.7, bf16[8,512,256]{2,1,0:T(8,128)(2,1)} %values.7, bf16[512,256]{1,0:T(8,128)(2,1)} %events.1), custom_call_target="tpu_custom_call" | custom-call | bytes 4000000 | tf_op jit(solution)/shard_map/pallas_call | solution.py:76
  2.8 13.3 %collective-permute-start.2 = (bf16[8,512,256]{2,1,0:T(8,128)(2,1)}, bf16[8,512,256]{2,1,0:T(8,128)(2,1)}, u32[]{:S(2)}, u32[]{:S(2)}) collective-permute-start(bf16[8,512,256]{2,1,0:T(8,128)(2,1)} %get-tuple-element.15), channel_id=1, source_target_pairs={{0,508},{4,8},{8,4},{12,16},{16,12},{20,24},{24,20},{28,32},{32,28... | collective-permute-start | bytes 6291464 | tf_op jit(solution)/shard_map/ppermute | solution.py:352
  16.1 4.8 %all-to-all-start = ((bf16[4,512,256]{2,1,0:T(8,128)(2,1)}), bf16[4,512,256]{2,1,0:T(8,128)(2,1)S(1)}, u32[]{:S(2)}, u32[]{:S(2)}) async-start(bf16[4,512,256]{2,1,0:T(8,128)(2,1)} %get-tuple-element.14), calls=%async_computation | async-start | bytes 2097152 | tf_op jit(solution)/shard_map/all_to_all | solution.py:348
  20.9 0.0 copy-start.6
  20.9 2.6 %shard_map.84 = (bf16[4,512,256]{2,1,0:T(8,128)(2,1)}, bf16[4,512,256]{2,1,0:T(8,128)(2,1)}) custom-call(s32[8]{0:T(128)} %lengths.3, bf16[8,512,256]{2,1,0:T(8,128)(2,1)} %keys.7, bf16[8,512,256]{2,1,0:T(8,128)(2,1)} %values.7), custom_call_target="tpu_custom_call" | custom-call | bytes 15000000 | tf_op jit(solution)/shard_map/pallas_call | solution.py:76
  23.5 1.9 %collective-permute-start = (bf16[4,512,256]{2,1,0:T(8,128)(2,1)}, bf16[4,512,256]{2,1,0:T(8,128)(2,1)S(1)}, u32[]{:S(2)}, u32[]{:S(2)}) collective-permute-start(bf16[4,512,256]{2,1,0:T(8,128)(2,1)} %get-tuple-element.17), channel_id=1, source_target_pairs={{0,4},{4,0},{8,12},{12,8},{16,20},{20,16},{24,28},{28,24},{32,36},... | collective-permute-start | bytes 3145736 | tf_op jit(solution)/shard_map/ppermute | solution.py:356
  25.5 2.4 %collective-permute-start.1 = (bf16[4,512,256]{2,1,0:T(8,128)(2,1)}, bf16[4,512,256]{2,1,0:T(8,128)(2,1)S(1)}, u32[]{:S(2)}, u32[]{:S(2)}) collective-permute-start(bf16[4,512,256]{2,1,0:T(8,128)(2,1)} %get-tuple-element.18), channel_id=1, source_target_pairs={{0,4},{4,0},{8,12},{12,8},{16,20},{20,16},{24,28},{28,24},{32,36},... | collective-permute-start | bytes 3145736 | tf_op jit(solution)/shard_map/ppermute | solution.py:356
  27.9 0.0 copy-done.6
  27.9 1.9 %copy.9 = bf16[128,8,4,256]{3,1,2,0:T(8,128)(2,1)} copy(bf16[128,8,4,256]{3,2,1,0:T(4,128)(2,1)S(1)} %bitcast.4) | data formatting | bytes 4194304
  29.7 0.0 all-to-all-done.x_any
  29.7 0.0 copy-start
  29.7 1.0 %copy-done = bf16[4,512,256]{2,1,0:T(8,128)(2,1)} copy-done((bf16[4,512,256]{2,1,0:T(8,128)(2,1)}, bf16[4,512,256]{2,1,0:T(8,128)(2,1)S(1)}, u32[]{:S(2)}) %copy-start) | copy-done | bytes 1048600
  30.7 0.0 copy-start.3
  30.7 0.0 copy-start.5
  30.7 1.3 %shard_map.83.gain_ref = f32[1,1024]{1,0:T(1,128)} custom-call(bf16[4,512,256]{2,1,0:T(8,128)(2,1)} %copy-done, f32[1,1024]{1,0:T(1,128)} %bitcast.5), custom_call_target="tpu_custom_call" | custom-call | flops 8999999488 | tf_op jit(solution)/shard_map/pallas_call | solution.py:305
  32.0 0.0 collective-permute-done.moved_keys
  32.1 0.0 collective-permute-done.1.moved_values
  32.1 0.0 copy-done.3
  32.1 0.0 copy-done.5
  32.1 0.0 copy-start.1
  32.1 1.2 %copy-done.1 = bf16[4,512,256]{2,1,0:T(8,128)(2,1)S(1)} copy-done((bf16[4,512,256]{2,1,0:T(8,128)(2,1)S(1)}, bf16[4,512,256]{2,1,0:T(8,128)(2,1)}, u32[]{:S(2)}) %copy-start.1) | copy-done | bytes 1048600
  33.3 0.0 copy-start.4
  33.3 0.7 %copy-done.4 = f32[1,1024]{1,0:T(1,128)S(1)} copy-done((f32[1,1024]{1,0:T(1,128)S(1)}, f32[1,1024]{1,0:T(1,128)}, u32[]{:S(2)}) %copy-start.4) | copy-done | bytes 4120
  34.0 6.0 %shard_map.85 = (bf16[4,256,256]{2,1,0:T(8,128)(2,1)}, bf16[256,1024]{1,0:T(8,128)(2,1)}) custom-call(s32[8]{0:T(128)S(1)} %copy-done.3, s32[8]{0:T(128)S(1)} %copy-done.5, bf16[4,512,256]{2,1,0:T(8,128)(2,1)S(1)} %copy-done.1, f32[1,1024]{1,0:T(1,128)S(1)} %copy-done.4, bf16[1024,1024]{1,0:T(8,128)(2,1)} %bitcast.3, bf16[8,512,256]{2,1,0:T(8,128)(2,1)} %keys.7, ...), custom_call_target="tpu_custom_call" | custom-call | flops 100000000 | tf_op jit(solution)/shard_map/pallas_call | solution.py:254
  40.0 5.5 %all-to-all-start.1 = ((bf16[4,256,256]{2,1,0:T(8,128)(2,1)}), bf16[4,256,256]{2,1,0:T(8,128)(2,1)S(1)}, u32[]{:S(2)}, u32[]{:S(2)}) async-start(bf16[4,256,256]{2,1,0:T(8,128)(2,1)} %get-tuple-element.20), calls=%async_computation.1 | async-start | bytes 1048576 | tf_op jit(solution)/shard_map/all_to_all | solution.py:348
  45.5 0.0 collective-permute-done.2.moved
  45.5 0.0 copy-start.2
  45.5 3.9 %shard_map.86 = bf16[4,256,256]{2,1,0:T(8,128)(2,1)S(1)} custom-call(s32[8]{0:T(128)S(1)} %copy-done.3, s32[8]{0:T(128)S(1)} %copy-done.5, bf16[256,1024]{1,0:T(8,128)(2,1)} %get-tuple-element.19.b_hbm, bf16[8,512,256]{2,1,0:T(8,128)(2,1)} %keys.7, bf16[8,512,256]{2,1,0:T(8,128)(2,1)} %values.7, bf16[256,1024]{1,0:T(8,128)(2,1)} %w_hbm.1, ...), custom_call_target="tpu_custom_call" | custom-call | flops 3000000000 | tf_op jit(solution)/shard_map/pallas_call | solution.py:281
  49.4 3.0 %all-to-all-done.1.even = bf16[4,256,256]{2,1,0:T(8,128)(2,1)S(1)} async-done(((bf16[4,256,256]{2,1,0:T(8,128)(2,1)}), bf16[4,256,256]{2,1,0:T(8,128)(2,1)S(1)}, u32[]{:S(2)}, u32[]{:S(2)}) %all-to-all-start.1) | async-done | bytes 524320 | tf_op jit(solution)/shard_map/all_to_all | solution.py:348
  52.4 10.5 %all_to_all.15.odd = bf16[4,256,256]{2,1,0:T(8,128)(2,1)S(1)} all-to-all(bf16[4,256,256]{2,1,0:T(8,128)(2,1)S(1)} %shard_map.86), channel_id=1, replica_groups=mesh['user'=128,'head'=4] {'head'}, dimensions={0} | all-to-all | bytes 1048576 | tf_op jit(solution)/shard_map/all_to_all | solution.py:348
  62.8 0.0 copy-done.2
  62.8 0.9 %shard_map.87 = bf16[512,256]{1,0:T(8,128)(2,1)} custom-call(bf16[512,256]{1,0:T(8,128)(2,1)S(1)} %copy-done.2, bf16[4,256,256]{2,1,0:T(8,128)(2,1)S(1)} %all-to-all-done.1.even, bf16[4,256,256]{2,1,0:T(8,128)(2,1)S(1)} %all_to_all.15.odd), custom_call_target="tpu_custom_call" | custom-call | tf_op jit(solution)/shard_map/pallas_call | solution.py:328
Async XLA Ops:
  2.8 42.7 %collective-permute-start.2 = (bf16[8,512,256]{2,1,0:T(8,128)(2,1)}, bf16[8,512,256]{2,1,0:T(8,128)(2,1)}, u32[]{:S(2)}, u32[]{:S(2)}) collective-permute-start(bf16[8,512,256]{2,1,0:T(8,128)(2,1)} %get-tuple-element.15), channel_id=1, source_target_pairs={{0,508},{4,8},{8,4},{12,16},{16,12},{20,24},{24,20},{28,32},{32,28... | collective-permute-start | bytes 6291464 | tf_op jit(solution)/shard_map/ppermute | solution.py:352
  16.1 13.6 %all-to-all-start = ((bf16[4,512,256]{2,1,0:T(8,128)(2,1)}), bf16[4,512,256]{2,1,0:T(8,128)(2,1)S(1)}, u32[]{:S(2)}, u32[]{:S(2)}) async-start(bf16[4,512,256]{2,1,0:T(8,128)(2,1)} %get-tuple-element.14), calls=%async_computation | async-start | bytes 2097152 | tf_op jit(solution)/shard_map/all_to_all | solution.py:348
  20.9 7.0 %copy-start.6 = (bf16[1024,4,256]{2,1,0:T(4,128)(2,1)S(1)}, bf16[1024,4,256]{2,1,0:T(4,128)(2,1)}, u32[]{:S(2)}) copy-start(bf16[1024,4,256]{2,1,0:T(4,128)(2,1)} %param.10) | copy-start | bytes 6291460
  23.5 8.5 %collective-permute-start = (bf16[4,512,256]{2,1,0:T(8,128)(2,1)}, bf16[4,512,256]{2,1,0:T(8,128)(2,1)S(1)}, u32[]{:S(2)}, u32[]{:S(2)}) collective-permute-start(bf16[4,512,256]{2,1,0:T(8,128)(2,1)} %get-tuple-element.17), channel_id=1, source_target_pairs={{0,4},{4,0},{8,12},{12,8},{16,20},{20,16},{24,28},{28,24},{32,36},... | collective-permute-start | bytes 3145736 | tf_op jit(solution)/shard_map/ppermute | solution.py:356
  25.5 6.6 %collective-permute-start.1 = (bf16[4,512,256]{2,1,0:T(8,128)(2,1)}, bf16[4,512,256]{2,1,0:T(8,128)(2,1)S(1)}, u32[]{:S(2)}, u32[]{:S(2)}) collective-permute-start(bf16[4,512,256]{2,1,0:T(8,128)(2,1)} %get-tuple-element.18), channel_id=1, source_target_pairs={{0,4},{4,0},{8,12},{12,8},{16,20},{20,16},{24,28},{28,24},{32,36},... | collective-permute-start | bytes 3145736 | tf_op jit(solution)/shard_map/ppermute | solution.py:356
  29.7 1.0 %copy-start = (bf16[4,512,256]{2,1,0:T(8,128)(2,1)}, bf16[4,512,256]{2,1,0:T(8,128)(2,1)S(1)}, u32[]{:S(2)}) copy-start(bf16[4,512,256]{2,1,0:T(8,128)(2,1)S(1)} %all-to-all-done.x_any) | copy-start | bytes 3145732
  30.7 1.3 %copy-start.3 = (s32[8]{0:T(128)S(1)}, s32[8]{0:T(128)}, u32[]{:S(2)}) copy-start(s32[8]{0:T(128)} %lengths.3) | copy-start | bytes 100
  30.7 1.3 %copy-start.5 = (s32[8]{0:T(128)S(1)}, s32[8]{0:T(128)}, u32[]{:S(2)}) copy-start(s32[8]{0:T(128)} %offsets.3) | copy-start | bytes 100
  32.1 1.2 %copy-start.1 = (bf16[4,512,256]{2,1,0:T(8,128)(2,1)S(1)}, bf16[4,512,256]{2,1,0:T(8,128)(2,1)}, u32[]{:S(2)}) copy-start(bf16[4,512,256]{2,1,0:T(8,128)(2,1)} %copy-done) | copy-start | bytes 3145732
  33.3 0.7 %copy-start.4 = (f32[1,1024]{1,0:T(1,128)S(1)}, f32[1,1024]{1,0:T(1,128)}, u32[]{:S(2)}) copy-start(f32[1,1024]{1,0:T(1,128)} %shard_map.83.gain_ref) | copy-start | bytes 12292
  40.0 12.4 %all-to-all-start.1 = ((bf16[4,256,256]{2,1,0:T(8,128)(2,1)}), bf16[4,256,256]{2,1,0:T(8,128)(2,1)S(1)}, u32[]{:S(2)}, u32[]{:S(2)}) async-start(bf16[4,256,256]{2,1,0:T(8,128)(2,1)} %get-tuple-element.20), calls=%async_computation.1 | async-start | bytes 1048576 | tf_op jit(solution)/shard_map/all_to_all | solution.py:348
  45.5 17.4 %copy-start.2 = (bf16[512,256]{1,0:T(8,128)(2,1)S(1)}, bf16[512,256]{1,0:T(8,128)(2,1)}, u32[]{:S(2)}) copy-start(bf16[512,256]{1,0:T(8,128)(2,1)} %events.1) | copy-start | bytes 786436

commit v7 on v6

--- a/solution.py
+++ b/solution.py
@@ -178,20 +178,10 @@
         finish(s, *weights[s])
 
 
-def project_out(gated, w_ref, out_ref, width):
-    for p in range(out_ref.shape[0]):
-        out_ref[p] = lax.dot_general(
-            gated[...],
-            w_ref[:, p * width : (p + 1) * width],
-            NN,
-            preferred_element_type=jnp.float32,
-        ).astype(jnp.bfloat16)
-
-
 def first_kernel(
     lengths, offsets, x_any, gain_ref, w_hbm, keys, values, wo_hbm, moved_keys, moved_values,
-    out_ref, odd_hbm,
-    x_ref, w_ref, wo_ref, kv, normed_ref, even_ref, odd_ref, gated, sems, kv_sems,
+    out_hbm, odd_hbm,
+    x_ref, w_ref, wo_ref, kv, normed_ref, even_ref, odd_ref, gated, out_ref, sems, kv_sems, out_sems,
 ):
     parts, total, width = x_ref.shape
     features = parts * width
@@ -224,14 +214,25 @@
     odd_copy = pltpu.make_async_copy(odd_ref, odd_hbm, sems.at[3])
     odd_copy.start()
     attend_slots(0, lengths, offsets, even_ref, kv, gated)
-    project_out(gated, wo_ref, out_ref, width)
-    odd_copy.wait()
+    leave = [odd_copy]
+    for p in range(parts):
+        out_ref[p] = lax.dot_general(
+            gated[...],
+            wo_ref[:, p * width : (p + 1) * width],
+            NN,
+            preferred_element_type=jnp.float32,
+        ).astype(jnp.bfloat16)
+        leave.append(pltpu.make_async_copy(out_ref.at[p], out_hbm.at[p], out_sems.at[p]))
+        leave[-1].start()
+    for c in leave:
+        c.wait()
 
 
 def second_kernel(
-    lengths, offsets, b_hbm, keys, values, w_hbm, moved, out_ref, b_ref, w_ref, kv, gated, sems, kv_sems
+    lengths, offsets, head, b_hbm, keys, values, w_hbm, moved, *rest
 ):
-    half_slots, width = kv.shape[0] // 2, kv.shape[2]
+    *outs, b_ref, w_ref, kv, gated, sems, kv_sems = rest
+    parts, half_slots, width = len(outs), kv.shape[0] // 2, kv.shape[2]
     copies = [
         pltpu.make_async_copy(b_hbm, b_ref, sems.at[0]),
         pltpu.make_async_copy(w_hbm, w_ref, sems.at[1]),
@@ -243,7 +244,12 @@
     for c in copies:
         c.wait()
     attend_slots(1, lengths, offsets, b_ref, kv, gated)
-    project_out(gated, w_ref, out_ref, width)
+    for distance, out_ref in enumerate(outs):
+        target = lax.rem(head[0] + distance, parts)
+        at = pl.ds(pl.multiple_of(target * width, width), width)
+        out_ref[...] = lax.dot_general(
+            gated[...], w_ref[:, at], NN, preferred_element_type=jnp.float32
+        ).astype(jnp.bfloat16)
 
 
 def first(lengths, offsets, x4, gain, w, keys, values, w_out, moved):
@@ -253,9 +259,9 @@
     bf16 = jnp.bfloat16
     return pl.pallas_call(
         first_kernel,
-        out_shape=(jax.ShapeDtypeStruct((parts, half, width), bf16), pltpu.HBM((half, wide), bf16)),
+        out_shape=(pltpu.HBM((parts, half, width), bf16), pltpu.HBM((half, wide), bf16)),
         in_specs=[SMEM, SMEM, ANY, VMEM, HBM, HBM, HBM, HBM, ANY, ANY],
-        out_specs=(VMEM, HBM),
+        out_specs=(HBM, HBM),
         scratch_shapes=[
             pltpu.VMEM(x4.shape, bf16),
             pltpu.VMEM(w.shape, bf16),
@@ -265,24 +271,26 @@
             pltpu.VMEM((half, wide), bf16),
             pltpu.VMEM((half, wide), bf16),
             pltpu.VMEM((half, width), bf16),
+            pltpu.VMEM((parts, half, width), bf16),
             pltpu.SemaphoreType.DMA((4,)),
             pltpu.SemaphoreType.DMA((slots,)),
+            pltpu.SemaphoreType.DMA((parts,)),
         ],
         compiler_params=pltpu.CompilerParams(vmem_limit_bytes=28 * 2**20),
         cost_estimate=pl.CostEstimate(flops=10**8, bytes_accessed=0, transcendentals=0),
     )(lengths, offsets, x4, gain, in_hbm(w), in_hbm(keys), in_hbm(values), in_hbm(w_out), *moved)
 
 
-def second(lengths, offsets, branches, keys, values, w_out, moved):
+def second(lengths, offsets, head, branches, keys, values, w_out, moved):
     slots, cap, width = keys.shape
     parts, rows = w_out.shape[1] // width, branches.shape[0]
     bf16 = jnp.bfloat16
     operands = [in_hbm(a) for a in (branches, keys, values, w_out, moved)]
     return pl.pallas_call(
         second_kernel,
-        out_shape=jax.ShapeDtypeStruct((parts, rows, width), bf16),
-        in_specs=[SMEM, SMEM] + [HBM] * len(operands),
-        out_specs=VMEM,
+        out_shape=[jax.ShapeDtypeStruct((rows, width), bf16)] * parts,
+        in_specs=[SMEM, SMEM, SMEM] + [HBM] * len(operands),
+        out_specs=[VMEM] * parts,
         scratch_shapes=[
             pltpu.VMEM(branches.shape, bf16),
             pltpu.VMEM(w_out.shape, bf16),
@@ -293,7 +301,7 @@
         ],
         compiler_params=pltpu.CompilerParams(vmem_limit_bytes=20 * 2**20),
         cost_estimate=pl.CostEstimate(flops=3 * 10**9, bytes_accessed=0, transcendentals=0),
-    )(lengths, offsets, *operands)
+    )(lengths, offsets, head, *operands)
 
 
 def gate_kernel(x_any, gain_ref, out_ref):
@@ -307,20 +315,21 @@
         out_shape=jax.ShapeDtypeStruct(gain.shape, gain.dtype),
         in_specs=[ANY, VMEM],
         out_specs=VMEM,
+        compiler_params=pltpu.CompilerParams(vmem_limit_bytes=2**20),
         cost_estimate=pl.CostEstimate(flops=9 * 10**9, bytes_accessed=0, transcendentals=0),
     )(x4, gain)
 
 
-def combine_kernel(events, even, odd, out_ref):
-    parts, rows, _ = even.shape
-    half_slots = out_ref.shape[0] // 2 // NEW
-    for j in range(2 * half_slots):
+def combine_kernel(events, even, *rest):
+    *odd, out_ref = rest
+    even = [even.at[p] for p in range(even.shape[0])]
+    for j in range(out_ref.shape[0] // NEW):
         at = slice(j * NEW, (j + 1) * NEW)
         terms_at = slice((j // 2) * NEW, (j // 2 + 1) * NEW)
         terms = odd if j % 2 else even
-        total = terms[0, terms_at, :].astype(jnp.float32)
-        for p in range(1, parts):
-            total = total + terms[p, terms_at, :].astype(jnp.float32)
+        total = terms[0][terms_at, :].astype(jnp.float32)
+        for term in terms[1:]:
+            total = total + term[terms_at, :].astype(jnp.float32)
         out_ref[at, :] = (events[at, :].astype(jnp.float32) + total).astype(out_ref.dtype)
 
 
@@ -328,10 +337,10 @@
     return pl.pallas_call(
         combine_kernel,
         out_shape=jax.ShapeDtypeStruct(events.shape, events.dtype),
-        in_specs=[VMEM, VMEM, VMEM],
+        in_specs=[VMEM] * (2 + len(odd)),
         out_specs=VMEM,
         compiler_params=pltpu.CompilerParams(vmem_limit_bytes=6 * 2**20),
-    )(events, even, odd)
+    )(events, even, *odd)
 
 
 def in_hbm(array):
@@ -361,9 +370,13 @@
         lengths, swap_offset, gathered, gain, w, *caches, w_out, even
     )
     even_terms = to_heads(even_part)
-    odd_part = second(lengths, swap_offset, odd_branches, *caches, w_out, odd)
-    odd_part, even_terms = lax.optimization_barrier((odd_part, even_terms))
-    odd_terms = to_heads(odd_part)
+    head = lax.axis_index("head").astype(jnp.int32)[None]
+    odd_terms = list(
+        second(lengths, swap_offset, head, odd_branches, *caches, w_out, odd)
+    )
+    for distance in range(1, heads):
+        ahead = [(h, (h + distance) % heads) for h in range(heads)]
+        odd_terms[distance] = lax.ppermute(odd_terms[distance], "head", ahead)
     return combine(events, even_terms, odd_terms)
 
 

time: 64.9 us -> 62.1 us (0.957); the launches traced: 63.7 us -> 61.6 us
  blocking collectives: 10.5 us -> 0 us
  starting transfers between devices: 27.9 us -> 36.5 us
  waiting for transfers between devices: 2.99 us -> 6.68 us
  local copies, waits for them, and re-layouts: 4.77 us -> 1.97 us
  Pallas kernels: 17.5 us -> 16.3 us
    all_to_all x1 -> x0, blocking collectives: 10.5 us -> none  [to_heads(): return lax.all_to_all(blocks, 'head', 0, 0)]
    ppermute x0 -> x3, starting transfers between devices: none -> 8.66 us  [on_device(): odd_terms[distance] = lax.ppermute(odd_terms[distance], 'head', ahead)]
    ppermute x0 -> x3, waiting for transfers between devices: none -> 6.12 us  [on_device(): odd_terms[distance] = lax.ppermute(odd_terms[distance], 'head', ahead)]
    all_to_all x2, waiting for transfers between devices: 2.98 us -> 0.01 us  [to_heads(): return lax.all_to_all(blocks, 'head', 0, 0)]
    unnamed x15 -> x11, local copies, waits for them, and re-layouts: 4.77 us -> 1.97 us
    pallas_call x1, Pallas kernels: 1.31 us -> 0.01 us  [gain_after(): pl.pallas_call(gate_kernel, out_shape=jax.ShapeDtypeStruct(gain.shape, ga...]
  transfers between devices with their start and end apart: 5 -> 8, of which waited for: 1 -> 3; matrix products, arithmetic and copies ran while one was open for 3% -> 3% of each run, Pallas kernels for 22% -> 20%
where the time goes in v7:
time: 62.1 us; the launch traced here: 61.6 us
  starting transfers between devices  36.5 us (59%)
  Pallas kernels  16.3 us (26%)
  waiting for transfers between devices  6.68 us (11%)
  local copies, waits for them, and re-layouts  1.97 us (3%)
    ppermute x1, starting transfers between devices, on_device(): odd = lax.ppermute(odd_pay, 'user', across)  13.3 us
    all_to_all x2, starting transfers between devices, to_heads(): return lax.all_to_all(blocks, 'head', 0, 0)  10.3 us
    ppermute x3, starting transfers between devices, on_device(): odd_terms[distance] = lax.ppermute(odd_terms[distance], 'head', ahead)  8.66 us
    ppermute x3, waiting for transfers between devices, on_device(): odd_terms[distance] = lax.ppermute(odd_terms[distance], 'head', ahead)  6.12 us
    pallas_call x1, Pallas kernels, first(): pl.pallas_call(first_kernel, out_shape=(pltpu.HBM((parts, half, width), b...  6.07 us
    pallas_call x2, Pallas kernels, pack(): pl.pallas_call(functools.partial(pack_kernel, side), out_shape=outs, in_s...  5.41 us
    ppermute x2, starting transfers between devices, on_device(): lax.ppermute(pay, 'user', within)  4.33 us
    pallas_call x1, Pallas kernels, second(): pl.pallas_call(second_kernel, out_shape=[jax.ShapeDtypeStruct((rows, widt...  3.93 us
  transfers between devices with their start and end apart: 8, of which 3 were waited for; matrix products, arithmetic and copies ran while one was open for 3% of the time, Pallas kernels for 20%

profile of v7, /device:TPU:6, one launch (start us, length us, event | category | flops | bytes accessed | tf_op | source)
XLA Modules:
  0.0 61.6 jit_solution(8245947094255268623)
XLA Ops:
  0.0 2.8 %shard_map.82 = (bf16[8,512,256]{2,1,0:T(8,128)(2,1)}, bf16[4,512,256]{2,1,0:T(8,128)(2,1)}) custom-call(s32[8]{0:T(128)} %lengths.3, bf16[8,512,256]{2,1,0:T(8,128)(2,1)} %keys.7, bf16[8,512,256]{2,1,0:T(8,128)(2,1)} %values.7, bf16[512,256]{1,0:T(8,128)(2,1)} %events.1), custom_call_target="tpu_custom_call" | custom-call | bytes 4000000 | tf_op jit(solution)/shard_map/pallas_call | solution.py:76
  2.8 13.3 %collective-permute-start.2 = (bf16[8,512,256]{2,1,0:T(8,128)(2,1)}, bf16[8,512,256]{2,1,0:T(8,128)(2,1)}, u32[]{:S(2)}, u32[]{:S(2)}) collective-permute-start(bf16[8,512,256]{2,1,0:T(8,128)(2,1)} %get-tuple-element.17), channel_id=1, source_target_pairs={{0,508},{4,8},{8,4},{12,16},{16,12},{20,24},{24,20},{28,32},{32,28... | collective-permute-start | bytes 6291464 | tf_op jit(solution)/shard_map/ppermute | solution.py:361
  16.1 4.8 %all-to-all-start = ((bf16[4,512,256]{2,1,0:T(8,128)(2,1)}), bf16[4,512,256]{2,1,0:T(8,128)(2,1)S(1)}, u32[]{:S(2)}, u32[]{:S(2)}) async-start(bf16[4,512,256]{2,1,0:T(8,128)(2,1)} %get-tuple-element.16), calls=%async_computation | async-start | bytes 2097152 | tf_op jit(solution)/shard_map/all_to_all | solution.py:357
  20.9 0.0 copy-start.4
  20.9 2.6 %shard_map.84 = (bf16[4,512,256]{2,1,0:T(8,128)(2,1)}, bf16[4,512,256]{2,1,0:T(8,128)(2,1)}) custom-call(s32[8]{0:T(128)} %lengths.3, bf16[8,512,256]{2,1,0:T(8,128)(2,1)} %keys.7, bf16[8,512,256]{2,1,0:T(8,128)(2,1)} %values.7), custom_call_target="tpu_custom_call" | custom-call | bytes 15000000 | tf_op jit(solution)/shard_map/pallas_call | solution.py:76
  23.5 1.9 %collective-permute-start = (bf16[4,512,256]{2,1,0:T(8,128)(2,1)}, bf16[4,512,256]{2,1,0:T(8,128)(2,1)S(1)}, u32[]{:S(2)}, u32[]{:S(2)}) collective-permute-start(bf16[4,512,256]{2,1,0:T(8,128)(2,1)} %get-tuple-element.19), channel_id=1, source_target_pairs={{0,4},{4,0},{8,12},{12,8},{16,20},{20,16},{24,28},{28,24},{32,36},... | collective-permute-start | bytes 3145736 | tf_op jit(solution)/shard_map/ppermute | solution.py:365
  25.4 2.4 %collective-permute-start.1 = (bf16[4,512,256]{2,1,0:T(8,128)(2,1)}, bf16[4,512,256]{2,1,0:T(8,128)(2,1)S(1)}, u32[]{:S(2)}, u32[]{:S(2)}) collective-permute-start(bf16[4,512,256]{2,1,0:T(8,128)(2,1)} %get-tuple-element.20), channel_id=1, source_target_pairs={{0,4},{4,0},{8,12},{12,8},{16,20},{20,16},{24,28},{28,24},{32,36},... | collective-permute-start | bytes 3145736 | tf_op jit(solution)/shard_map/ppermute | solution.py:365
  27.9 0.0 copy-done.4
  27.9 0.0 copy-start.3
  27.9 1.9 %copy.9 = bf16[128,8,4,256]{3,1,2,0:T(8,128)(2,1)} copy(bf16[128,8,4,256]{3,2,1,0:T(4,128)(2,1)S(1)} %bitcast.6) | data formatting | bytes 4194304
  29.7 0.0 all-to-all-done.x_any
  29.7 0.0 copy-done.3
  29.8 0.0 copy-start.1
  29.8 0.0 copy-start.2
  29.8 0.0 collective-permute-done.moved_keys
  29.8 0.5 collective-permute-done.1.moved_values
  30.3 0.1 copy-done.1
  30.4 0.0 copy-done.2
  30.4 6.1 %shard_map.85 = (bf16[4,256,256]{2,1,0:T(8,128)(2,1)}, bf16[256,1024]{1,0:T(8,128)(2,1)}) custom-call(s32[8]{0:T(128)S(1)} %copy-done.1, s32[8]{0:T(128)S(1)} %copy-done.2, bf16[4,512,256]{2,1,0:T(8,128)(2,1)S(1)} %all-to-all-done.x_any, f32[1,1024]{1,0:T(1,128)S(1)} %shard_map.83.gain_ref, bf16[1024,1024]{1,0:T(8,128)(2,1)} %bitcast.5, ...), custom_call_target="tpu_custom_call" | custom-call | flops 100000000 | tf_op jit(solution)/shard_map/pallas_call | solution.py:260
  36.5 5.5 %all-to-all-start.1 = ((bf16[4,256,256]{2,1,0:T(8,128)(2,1)}), bf16[4,256,256]{2,1,0:T(8,128)(2,1)S(1)}, u32[]{:S(2)}, u32[]{:S(2)}) async-start(bf16[4,256,256]{2,1,0:T(8,128)(2,1)} %get-tuple-element.21), calls=%async_computation.1 | async-start | bytes 1048576 | tf_op jit(solution)/shard_map/all_to_all | solution.py:357
  42.0 0.0 collective-permute-done.2.moved
  42.0 0.0 copy-start
  42.0 3.9 %shard_map.86 = (bf16[256,256]{1,0:T(8,128)(2,1)S(1)}, bf16[256,256]{1,0:T(8,128)(2,1)S(1)}, bf16[256,256]{1,0:T(8,128)(2,1)S(1)}, bf16[256,256]{1,0:T(8,128)(2,1)S(1)}) custom-call(s32[8]{0:T(128)S(1)} %copy-done.1, s32[8]{0:T(128)S(1)} %copy-done.2, s32[1]{0:T(128)} %bitcast.1.head, bf16[256,1024]{1,0:T(8,128)(2,1)} %get-tuple-element.22.b_hbm, ...), custom_call_target="tpu_custom_call" | custom-call | flops 3000000000 | tf_op jit(solution)/shard_map/pallas_call | solution.py:289
  45.9 2.0 %collective-permute-start.3 = (bf16[256,256]{1,0:T(8,128)(2,1)S(1)}, bf16[256,256]{1,0:T(8,128)(2,1)S(1)}, u32[]{:S(2)}, u32[]{:S(2)}) collective-permute-start(bf16[256,256]{1,0:T(8,128)(2,1)S(1)} %get-tuple-element.24), channel_id=1, source_target_pairs={{0,1},{1,2},{2,3},{3,0},{4,5},{5,6},{6,7},{7,4},{8,9},{9,10},{10,1... | collective-permute-start | bytes 393224 | tf_op jit(solution)/shard_map/ppermute | solution.py:379
  47.9 4.8 %collective-permute-start.4 = (bf16[256,256]{1,0:T(8,128)(2,1)S(1)}, bf16[256,256]{1,0:T(8,128)(2,1)S(1)}, u32[]{:S(2)}, u32[]{:S(2)}) collective-permute-start(bf16[256,256]{1,0:T(8,128)(2,1)S(1)} %get-tuple-element.25), channel_id=1, source_target_pairs={{0,2},{1,3},{2,0},{3,1},{4,6},{5,7},{6,4},{7,5},{8,10},{9,11},{10,... | collective-permute-start | bytes 393224 | tf_op jit(solution)/shard_map/ppermute | solution.py:379
  52.7 1.9 %collective-permute-start.5 = (bf16[256,256]{1,0:T(8,128)(2,1)S(1)}, bf16[256,256]{1,0:T(8,128)(2,1)S(1)}, u32[]{:S(2)}, u32[]{:S(2)}) collective-permute-start(bf16[256,256]{1,0:T(8,128)(2,1)S(1)} %get-tuple-element.26), channel_id=1, source_target_pairs={{0,3},{1,0},{2,1},{3,2},{4,7},{5,4},{6,5},{7,6},{8,11},{9,8},{10,9... | collective-permute-start | bytes 393224 | tf_op jit(solution)/shard_map/ppermute | solution.py:379
  54.6 0.0 all-to-all-done.1.even
  54.6 0.0 collective-permute-done.3.rest_1_
  54.6 1.7 %collective-permute-done.4.rest_2_ = bf16[256,256]{1,0:T(8,128)(2,1)S(1)} collective-permute-done((bf16[256,256]{1,0:T(8,128)(2,1)S(1)}, bf16[256,256]{1,0:T(8,128)(2,1)S(1)}, u32[]{:S(2)}, u32[]{:S(2)}) %collective-permute-start.4) | collective-permute-done | bytes 131104 | tf_op jit(solution)/shard_map/ppermute | solution.py:379
  56.3 4.5 %collective-permute-done.5.rest_3_ = bf16[256,256]{1,0:T(8,128)(2,1)S(1)} collective-permute-done((bf16[256,256]{1,0:T(8,128)(2,1)S(1)}, bf16[256,256]{1,0:T(8,128)(2,1)S(1)}, u32[]{:S(2)}, u32[]{:S(2)}) %collective-permute-start.5) | collective-permute-done | bytes 131104 | tf_op jit(solution)/shard_map/ppermute | solution.py:379
  60.8 0.0 copy-done
  60.8 0.9 %shard_map.87 = bf16[512,256]{1,0:T(8,128)(2,1)} custom-call(bf16[512,256]{1,0:T(8,128)(2,1)S(1)} %copy-done, bf16[4,256,256]{2,1,0:T(8,128)(2,1)S(1)} %all-to-all-done.1.even, bf16[256,256]{1,0:T(8,128)(2,1)S(1)} %get-tuple-element.23.rest_0_, bf16[256,256]{1,0:T(8,128)(2,1)S(1)} %collective-permute-done.3.rest_1_, ...), custom_call_target="tpu_custom_call" | custom-call | tf_op jit(solution)/shard_map/pallas_call | solution.py:337
  (1 shorter events, 0.0 us)
Async XLA Ops:
  2.8 39.2 %collective-permute-start.2 = (bf16[8,512,256]{2,1,0:T(8,128)(2,1)}, bf16[8,512,256]{2,1,0:T(8,128)(2,1)}, u32[]{:S(2)}, u32[]{:S(2)}) collective-permute-start(bf16[8,512,256]{2,1,0:T(8,128)(2,1)} %get-tuple-element.17), channel_id=1, source_target_pairs={{0,508},{4,8},{8,4},{12,16},{16,12},{20,24},{24,20},{28,32},{32,28... | collective-permute-start | bytes 6291464 | tf_op jit(solution)/shard_map/ppermute | solution.py:361
  16.1 13.6 %all-to-all-start = ((bf16[4,512,256]{2,1,0:T(8,128)(2,1)}), bf16[4,512,256]{2,1,0:T(8,128)(2,1)S(1)}, u32[]{:S(2)}, u32[]{:S(2)}) async-start(bf16[4,512,256]{2,1,0:T(8,128)(2,1)} %get-tuple-element.16), calls=%async_computation | async-start | bytes 2097152 | tf_op jit(solution)/shard_map/all_to_all | solution.py:357
  20.9 7.0 %copy-start.4 = (bf16[1024,4,256]{2,1,0:T(4,128)(2,1)S(1)}, bf16[1024,4,256]{2,1,0:T(4,128)(2,1)}, u32[]{:S(2)}) copy-start(bf16[1024,4,256]{2,1,0:T(4,128)(2,1)} %param.10) | copy-start | bytes 6291460
  23.5 6.3 %collective-permute-start = (bf16[4,512,256]{2,1,0:T(8,128)(2,1)}, bf16[4,512,256]{2,1,0:T(8,128)(2,1)S(1)}, u32[]{:S(2)}, u32[]{:S(2)}) collective-permute-start(bf16[4,512,256]{2,1,0:T(8,128)(2,1)} %get-tuple-element.19), channel_id=1, source_target_pairs={{0,4},{4,0},{8,12},{12,8},{16,20},{20,16},{24,28},{28,24},{32,36},... | collective-permute-start | bytes 3145736 | tf_op jit(solution)/shard_map/ppermute | solution.py:365
  25.4 4.9 %collective-permute-start.1 = (bf16[4,512,256]{2,1,0:T(8,128)(2,1)}, bf16[4,512,256]{2,1,0:T(8,128)(2,1)S(1)}, u32[]{:S(2)}, u32[]{:S(2)}) collective-permute-start(bf16[4,512,256]{2,1,0:T(8,128)(2,1)} %get-tuple-element.20), channel_id=1, source_target_pairs={{0,4},{4,0},{8,12},{12,8},{16,20},{20,16},{24,28},{28,24},{32,36},... | collective-permute-start | bytes 3145736 | tf_op jit(solution)/shard_map/ppermute | solution.py:365
  27.9 1.9 %copy-start.3 = (f32[1024]{0:T(1024)S(1)}, f32[1024]{0:T(1024)}, u32[]{:S(2)}) copy-start(f32[1024]{0:T(1024)} %param.9) | copy-start | bytes 12292
  29.8 0.7 %copy-start.1 = (s32[8]{0:T(128)S(1)}, s32[8]{0:T(128)}, u32[]{:S(2)}) copy-start(s32[8]{0:T(128)} %lengths.3) | copy-start | bytes 100
  29.8 0.7 %copy-start.2 = (s32[8]{0:T(128)S(1)}, s32[8]{0:T(128)}, u32[]{:S(2)}) copy-start(s32[8]{0:T(128)} %offsets.3) | copy-start | bytes 100
  36.5 18.1 %all-to-all-start.1 = ((bf16[4,256,256]{2,1,0:T(8,128)(2,1)}), bf16[4,256,256]{2,1,0:T(8,128)(2,1)S(1)}, u32[]{:S(2)}, u32[]{:S(2)}) async-start(bf16[4,256,256]{2,1,0:T(8,128)(2,1)} %get-tuple-element.21), calls=%async_computation.1 | async-start | bytes 1048576 | tf_op jit(solution)/shard_map/all_to_all | solution.py:357
  42.0 18.8 %copy-start = (bf16[512,256]{1,0:T(8,128)(2,1)S(1)}, bf16[512,256]{1,0:T(8,128)(2,1)}, u32[]{:S(2)}) copy-start(bf16[512,256]{1,0:T(8,128)(2,1)} %events.1) | copy-start | bytes 786436
  45.9 8.7 %collective-permute-start.3 = (bf16[256,256]{1,0:T(8,128)(2,1)S(1)}, bf16[256,256]{1,0:T(8,128)(2,1)S(1)}, u32[]{:S(2)}, u32[]{:S(2)}) collective-permute-start(bf16[256,256]{1,0:T(8,128)(2,1)S(1)} %get-tuple-element.24), channel_id=1, source_target_pairs={{0,1},{1,2},{2,3},{3,0},{4,5},{5,6},{6,7},{7,4},{8,9},{9,10},{10,1... | collective-permute-start | bytes 393224 | tf_op jit(solution)/shard_map/ppermute | solution.py:379
  47.9 8.4 %collective-permute-start.4 = (bf16[256,256]{1,0:T(8,128)(2,1)S(1)}, bf16[256,256]{1,0:T(8,128)(2,1)S(1)}, u32[]{:S(2)}, u32[]{:S(2)}) collective-permute-start(bf16[256,256]{1,0:T(8,128)(2,1)S(1)} %get-tuple-element.25), channel_id=1, source_target_pairs={{0,2},{1,3},{2,0},{3,1},{4,6},{5,7},{6,4},{7,5},{8,10},{9,11},{10,... | collective-permute-start | bytes 393224 | tf_op jit(solution)/shard_map/ppermute | solution.py:379
  52.7 8.1 %collective-permute-start.5 = (bf16[256,256]{1,0:T(8,128)(2,1)S(1)}, bf16[256,256]{1,0:T(8,128)(2,1)S(1)}, u32[]{:S(2)}, u32[]{:S(2)}) collective-permute-start(bf16[256,256]{1,0:T(8,128)(2,1)S(1)} %get-tuple-element.26), channel_id=1, source_target_pairs={{0,3},{1,0},{2,1},{3,2},{4,7},{5,4},{6,5},{7,6},{8,11},{9,8},{10,9... | collective-permute-start | bytes 393224 | tf_op jit(solution)/shard_map/ppermute | solution.py:379

commit v8 on v6

--- a/solution.py
+++ b/solution.py
@@ -189,9 +189,10 @@
 
 
 def first_kernel(
-    lengths, offsets, x_any, gain_ref, w_hbm, keys, values, wo_hbm, moved_keys, moved_values,
-    out_ref, odd_hbm,
-    x_ref, w_ref, wo_ref, kv, normed_ref, even_ref, odd_ref, gated, sems, kv_sems,
+    lengths_hbm, offsets_hbm, x_any, gain_ref, w_hbm, keys, values, wo_hbm, moved_keys, moved_values,
+    out_hbm, odd_hbm,
+    x_ref, w_ref, wo_ref, kv, normed_ref, even_ref, odd_ref, gated, out_ref, lengths, offsets,
+    sems, kv_sems, out_sems,
 ):
     parts, total, width = x_ref.shape
     features = parts * width
@@ -200,8 +201,14 @@
         pltpu.make_async_copy(w_hbm, w_ref, sems.at[1]),
         pltpu.make_async_copy(wo_hbm, wo_ref, sems.at[2]),
     ]
-    for c in [x_copy] + rest:
+    layout = [
+        pltpu.make_async_copy(offsets_hbm, offsets, sems.at[4]),
+        pltpu.make_async_copy(lengths_hbm, lengths, sems.at[5]),
+    ]
+    for c in layout + [x_copy] + rest:
         c.start()
+    for c in layout:
+        c.wait()
     rest += cache_copies(0, offsets, keys, values, moved_keys, moved_values, kv, kv_sems)
     x_copy.wait()
     x = jnp.concatenate([x_ref[p] for p in range(parts)], axis=1).astype(jnp.float32)
@@ -224,8 +231,18 @@
     odd_copy = pltpu.make_async_copy(odd_ref, odd_hbm, sems.at[3])
     odd_copy.start()
     attend_slots(0, lengths, offsets, even_ref, kv, gated)
-    project_out(gated, wo_ref, out_ref, width)
-    odd_copy.wait()
+    leave = [odd_copy]
+    for p in range(parts):
+        out_ref[p] = lax.dot_general(
+            gated[...],
+            wo_ref[:, p * width : (p + 1) * width],
+            NN,
+            preferred_element_type=jnp.float32,
+        ).astype(jnp.bfloat16)
+        leave.append(pltpu.make_async_copy(out_ref.at[p], out_hbm.at[p], out_sems.at[p]))
+        leave[-1].start()
+    for c in leave:
+        c.wait()
 
 
 def second_kernel(
@@ -253,9 +270,9 @@
     bf16 = jnp.bfloat16
     return pl.pallas_call(
         first_kernel,
-        out_shape=(jax.ShapeDtypeStruct((parts, half, width), bf16), pltpu.HBM((half, wide), bf16)),
-        in_specs=[SMEM, SMEM, ANY, VMEM, HBM, HBM, HBM, HBM, ANY, ANY],
-        out_specs=(VMEM, HBM),
+        out_shape=(pltpu.HBM((parts, half, width), bf16), pltpu.HBM((half, wide), bf16)),
+        in_specs=[HBM, HBM, ANY, VMEM, HBM, HBM, HBM, HBM, ANY, ANY],
+        out_specs=(HBM, HBM),
         scratch_shapes=[
             pltpu.VMEM(x4.shape, bf16),
             pltpu.VMEM(w.shape, bf16),
@@ -265,12 +282,16 @@
             pltpu.VMEM((half, wide), bf16),
             pltpu.VMEM((half, wide), bf16),
             pltpu.VMEM((half, width), bf16),
-            pltpu.SemaphoreType.DMA((4,)),
+            pltpu.VMEM((parts, half, width), bf16),
+            pltpu.SMEM(lengths.shape, lengths.dtype),
+            pltpu.SMEM(offsets.shape, offsets.dtype),
+            pltpu.SemaphoreType.DMA((6,)),
             pltpu.SemaphoreType.DMA((slots,)),
+            pltpu.SemaphoreType.DMA((parts,)),
         ],
         compiler_params=pltpu.CompilerParams(vmem_limit_bytes=28 * 2**20),
         cost_estimate=pl.CostEstimate(flops=10**8, bytes_accessed=0, transcendentals=0),
-    )(lengths, offsets, x4, gain, in_hbm(w), in_hbm(keys), in_hbm(values), in_hbm(w_out), *moved)
+    )(in_hbm(lengths), in_hbm(offsets), x4, gain, in_hbm(w), in_hbm(keys), in_hbm(values), in_hbm(w_out), *moved)
 
 
 def second(lengths, offsets, branches, keys, values, w_out, moved):
@@ -307,6 +328,7 @@
         out_shape=jax.ShapeDtypeStruct(gain.shape, gain.dtype),
         in_specs=[ANY, VMEM],
         out_specs=VMEM,
+        compiler_params=pltpu.CompilerParams(vmem_limit_bytes=2**20),
         cost_estimate=pl.CostEstimate(flops=9 * 10**9, bytes_accessed=0, transcendentals=0),
     )(x4, gain)
 

time: 64.9 us -> 62.2 us (0.958)
  local copies, waits for them, and re-layouts: 4.77 us -> 1.86 us
  Pallas kernels: 17.5 us -> 16 us
  waiting for transfers between devices: 2.99 us -> 4.49 us
  blocking collectives: 10.5 us -> 11.4 us
    unnamed x15 -> x11, local copies, waits for them, and re-layouts: 4.77 us -> 1.86 us
    pallas_call x1, Pallas kernels: 1.31 us -> 0.01 us  [gain_after(): pl.pallas_call(gate_kernel, out_shape=jax.ShapeDtypeStruct(gain.shape, ga...]
    all_to_all x1, blocking collectives: 10.5 us -> 11.4 us  [to_heads(): return lax.all_to_all(blocks, 'head', 0, 0)]
    all_to_all x2, waiting for transfers between devices: 2.98 us -> 3.88 us  [to_heads(): return lax.all_to_all(blocks, 'head', 0, 0)]
  transfers between devices with their start and end apart: 5 -> 5, of which waited for: 1 -> 2; matrix products, arithmetic and copies ran while one was open for 3% -> 3% of each run, Pallas kernels for 22% -> 20%
where the time goes in v8:
time: 62.2 us; the launch traced here: 61.1 us
  starting transfers between devices  27.3 us (44%)
  Pallas kernels  16 us (26%)
  blocking collectives  11.4 us (18%)
  waiting for transfers between devices  4.49 us (7%)
  local copies, waits for them, and re-layouts  1.86 us (3%)
    ppermute x1, starting transfers between devices, on_device(): odd = lax.ppermute(odd_pay, 'user', across)  13.3 us
    all_to_all x1, blocking collectives, to_heads(): return lax.all_to_all(blocks, 'head', 0, 0)  11.4 us
    all_to_all x2, starting transfers between devices, to_heads(): return lax.all_to_all(blocks, 'head', 0, 0)  9.72 us
    pallas_call x1, Pallas kernels, first(): pl.pallas_call(first_kernel, out_shape=(pltpu.HBM((parts, half, width), b...  5.74 us
    pallas_call x2, Pallas kernels, pack(): pl.pallas_call(functools.partial(pack_kernel, side), out_shape=outs, in_s...  5.44 us
    ppermute x2, starting transfers between devices, on_device(): lax.ppermute(pay, 'user', within)  4.33 us
    pallas_call x1, Pallas kernels, second(): pl.pallas_call(second_kernel, out_shape=jax.ShapeDtypeStruct((parts, rows...  3.9 us
    all_to_all x2, waiting for transfers between devices, to_heads(): return lax.all_to_all(blocks, 'head', 0, 0)  3.88 us
  transfers between devices with their start and end apart: 5, of which 2 were waited for; matrix products, arithmetic and copies ran while one was open for 3% of the time, Pallas kernels for 20%

profile of v8, /device:TPU:6, one launch (start us, length us, event | category | flops | bytes accessed | tf_op | source)
XLA Modules:
  0.0 61.1 jit_solution(1747627246974744205)
XLA Ops:
  0.0 2.8 %shard_map.82 = (bf16[8,512,256]{2,1,0:T(8,128)(2,1)}, bf16[4,512,256]{2,1,0:T(8,128)(2,1)}) custom-call(s32[8]{0:T(128)} %lengths.1, bf16[8,512,256]{2,1,0:T(8,128)(2,1)} %keys.7, bf16[8,512,256]{2,1,0:T(8,128)(2,1)} %values.7, bf16[512,256]{1,0:T(8,128)(2,1)} %events.1), custom_call_target="tpu_custom_call" | custom-call | bytes 4000000 | tf_op jit(solution)/shard_map/pallas_call | solution.py:76
  2.8 13.3 %collective-permute-start.2 = (bf16[8,512,256]{2,1,0:T(8,128)(2,1)}, bf16[8,512,256]{2,1,0:T(8,128)(2,1)}, u32[]{:S(2)}, u32[]{:S(2)}) collective-permute-start(bf16[8,512,256]{2,1,0:T(8,128)(2,1)} %get-tuple-element.15), channel_id=1, source_target_pairs={{0,508},{4,8},{8,4},{12,16},{16,12},{20,24},{24,20},{28,32},{32,28... | collective-permute-start | bytes 6291464 | tf_op jit(solution)/shard_map/ppermute | solution.py:374
  16.1 4.8 %all-to-all-start = ((bf16[4,512,256]{2,1,0:T(8,128)(2,1)}), bf16[4,512,256]{2,1,0:T(8,128)(2,1)S(1)}, u32[]{:S(2)}, u32[]{:S(2)}) async-start(bf16[4,512,256]{2,1,0:T(8,128)(2,1)} %get-tuple-element.14), calls=%async_computation | async-start | bytes 2097152 | tf_op jit(solution)/shard_map/all_to_all | solution.py:370
  20.9 0.0 copy-start.4
  20.9 2.6 %shard_map.84 = (bf16[4,512,256]{2,1,0:T(8,128)(2,1)}, bf16[4,512,256]{2,1,0:T(8,128)(2,1)}) custom-call(s32[8]{0:T(128)} %lengths.1, bf16[8,512,256]{2,1,0:T(8,128)(2,1)} %keys.7, bf16[8,512,256]{2,1,0:T(8,128)(2,1)} %values.7), custom_call_target="tpu_custom_call" | custom-call | bytes 15000000 | tf_op jit(solution)/shard_map/pallas_call | solution.py:76
  23.6 1.9 %collective-permute-start = (bf16[4,512,256]{2,1,0:T(8,128)(2,1)}, bf16[4,512,256]{2,1,0:T(8,128)(2,1)S(1)}, u32[]{:S(2)}, u32[]{:S(2)}) collective-permute-start(bf16[4,512,256]{2,1,0:T(8,128)(2,1)} %get-tuple-element.17), channel_id=1, source_target_pairs={{0,4},{4,0},{8,12},{12,8},{16,20},{20,16},{24,28},{28,24},{32,36},... | collective-permute-start | bytes 3145736 | tf_op jit(solution)/shard_map/ppermute | solution.py:378
  25.5 2.4 %collective-permute-start.1 = (bf16[4,512,256]{2,1,0:T(8,128)(2,1)}, bf16[4,512,256]{2,1,0:T(8,128)(2,1)S(1)}, u32[]{:S(2)}, u32[]{:S(2)}) collective-permute-start(bf16[4,512,256]{2,1,0:T(8,128)(2,1)} %get-tuple-element.18), channel_id=1, source_target_pairs={{0,4},{4,0},{8,12},{12,8},{16,20},{20,16},{24,28},{28,24},{32,36},... | collective-permute-start | bytes 3145736 | tf_op jit(solution)/shard_map/ppermute | solution.py:378
  27.9 0.0 copy-done.4
  27.9 0.0 copy-start.3
  27.9 1.8 %copy.9 = bf16[128,8,4,256]{3,1,2,0:T(8,128)(2,1)} copy(bf16[128,8,4,256]{3,2,1,0:T(4,128)(2,1)S(1)} %bitcast.5) | data formatting | bytes 4194304
  29.8 0.0 all-to-all-done.x_any
  29.8 0.0 copy-done.3
  29.8 0.0 collective-permute-done.moved_keys
  29.8 0.6 collective-permute-done.1.moved_values
  30.4 0.0 copy-start.1
  30.4 0.0 copy-start.2
  30.4 5.7 %shard_map.85 = (bf16[4,256,256]{2,1,0:T(8,128)(2,1)}, bf16[256,1024]{1,0:T(8,128)(2,1)}) custom-call(s32[8]{0:T(128)} %lengths.1, s32[8]{0:T(128)} %offsets.1, bf16[4,512,256]{2,1,0:T(8,128)(2,1)S(1)} %all-to-all-done.x_any, f32[1,1024]{1,0:T(1,128)S(1)} %shard_map.83.gain_ref, bf16[1024,1024]{1,0:T(8,128)(2,1)} %bitcast.4, bf16[8,512,256]{2,1,0:T(8,128)(2,1)} %keys.7, ...), custom_call_target="tpu_custom_call" | custom-call | flops 100000000 | tf_op jit(solution)/shard_map/pallas_call | solution.py:271
  36.1 4.9 %all-to-all-start.1 = ((bf16[4,256,256]{2,1,0:T(8,128)(2,1)}), bf16[4,256,256]{2,1,0:T(8,128)(2,1)S(1)}, u32[]{:S(2)}, u32[]{:S(2)}) async-start(bf16[4,256,256]{2,1,0:T(8,128)(2,1)} %get-tuple-element.20), calls=%async_computation.1 | async-start | bytes 1048576 | tf_op jit(solution)/shard_map/all_to_all | solution.py:370
  41.1 0.0 collective-permute-done.2.moved
  41.1 0.0 copy-done.1
  41.1 0.0 copy-done.2
  41.1 0.0 copy-start
  41.1 3.9 %shard_map.86 = bf16[4,256,256]{2,1,0:T(8,128)(2,1)S(1)} custom-call(s32[8]{0:T(128)S(1)} %copy-done.1, s32[8]{0:T(128)S(1)} %copy-done.2, bf16[256,1024]{1,0:T(8,128)(2,1)} %get-tuple-element.19.b_hbm, bf16[8,512,256]{2,1,0:T(8,128)(2,1)} %keys.7, bf16[8,512,256]{2,1,0:T(8,128)(2,1)} %values.7, bf16[256,1024]{1,0:T(8,128)(2,1)} %w_hbm.1, ...), custom_call_target="tpu_custom_call" | custom-call | flops 3000000000 | tf_op jit(solution)/shard_map/pallas_call | solution.py:302
  45.0 3.9 %all-to-all-done.1.even = bf16[4,256,256]{2,1,0:T(8,128)(2,1)S(1)} async-done(((bf16[4,256,256]{2,1,0:T(8,128)(2,1)}), bf16[4,256,256]{2,1,0:T(8,128)(2,1)S(1)}, u32[]{:S(2)}, u32[]{:S(2)}) %all-to-all-start.1) | async-done | bytes 524320 | tf_op jit(solution)/shard_map/all_to_all | solution.py:370
  48.9 11.4 %all_to_all.15.odd = bf16[4,256,256]{2,1,0:T(8,128)(2,1)S(1)} all-to-all(bf16[4,256,256]{2,1,0:T(8,128)(2,1)S(1)} %shard_map.86), channel_id=1, replica_groups=mesh['user'=128,'head'=4] {'head'}, dimensions={0} | all-to-all | bytes 1048576 | tf_op jit(solution)/shard_map/all_to_all | solution.py:370
  60.3 0.0 copy-done
  60.3 0.9 %shard_map.87 = bf16[512,256]{1,0:T(8,128)(2,1)} custom-call(bf16[512,256]{1,0:T(8,128)(2,1)S(1)} %copy-done, bf16[4,256,256]{2,1,0:T(8,128)(2,1)S(1)} %all-to-all-done.1.even, bf16[4,256,256]{2,1,0:T(8,128)(2,1)S(1)} %all_to_all.15.odd), custom_call_target="tpu_custom_call" | custom-call | tf_op jit(solution)/shard_map/pallas_call | solution.py:350
  (1 shorter events, 0.0 us)
Async XLA Ops:
  2.8 38.2 %collective-permute-start.2 = (bf16[8,512,256]{2,1,0:T(8,128)(2,1)}, bf16[8,512,256]{2,1,0:T(8,128)(2,1)}, u32[]{:S(2)}, u32[]{:S(2)}) collective-permute-start(bf16[8,512,256]{2,1,0:T(8,128)(2,1)} %get-tuple-element.15), channel_id=1, source_target_pairs={{0,508},{4,8},{8,4},{12,16},{16,12},{20,24},{24,20},{28,32},{32,28... | collective-permute-start | bytes 6291464 | tf_op jit(solution)/shard_map/ppermute | solution.py:374
  16.1 13.6 %all-to-all-start = ((bf16[4,512,256]{2,1,0:T(8,128)(2,1)}), bf16[4,512,256]{2,1,0:T(8,128)(2,1)S(1)}, u32[]{:S(2)}, u32[]{:S(2)}) async-start(bf16[4,512,256]{2,1,0:T(8,128)(2,1)} %get-tuple-element.14), calls=%async_computation | async-start | bytes 2097152 | tf_op jit(solution)/shard_map/all_to_all | solution.py:370
  20.9 7.0 %copy-start.4 = (bf16[1024,4,256]{2,1,0:T(4,128)(2,1)S(1)}, bf16[1024,4,256]{2,1,0:T(4,128)(2,1)}, u32[]{:S(2)}) copy-start(bf16[1024,4,256]{2,1,0:T(4,128)(2,1)} %param.10) | copy-start | bytes 6291460
  23.6 6.2 %collective-permute-start = (bf16[4,512,256]{2,1,0:T(8,128)(2,1)}, bf16[4,512,256]{2,1,0:T(8,128)(2,1)S(1)}, u32[]{:S(2)}, u32[]{:S(2)}) collective-permute-start(bf16[4,512,256]{2,1,0:T(8,128)(2,1)} %get-tuple-element.17), channel_id=1, source_target_pairs={{0,4},{4,0},{8,12},{12,8},{16,20},{20,16},{24,28},{28,24},{32,36},... | collective-permute-start | bytes 3145736 | tf_op jit(solution)/shard_map/ppermute | solution.py:378
  25.5 4.9 %collective-permute-start.1 = (bf16[4,512,256]{2,1,0:T(8,128)(2,1)}, bf16[4,512,256]{2,1,0:T(8,128)(2,1)S(1)}, u32[]{:S(2)}, u32[]{:S(2)}) collective-permute-start(bf16[4,512,256]{2,1,0:T(8,128)(2,1)} %get-tuple-element.18), channel_id=1, source_target_pairs={{0,4},{4,0},{8,12},{12,8},{16,20},{20,16},{24,28},{28,24},{32,36},... | collective-permute-start | bytes 3145736 | tf_op jit(solution)/shard_map/ppermute | solution.py:378
  27.9 1.9 %copy-start.3 = (f32[1024]{0:T(1024)S(1)}, f32[1024]{0:T(1024)}, u32[]{:S(2)}) copy-start(f32[1024]{0:T(1024)} %param.9) | copy-start | bytes 12292
  30.4 10.7 %copy-start.1 = (s32[8]{0:T(128)S(1)}, s32[8]{0:T(128)}, u32[]{:S(2)}) copy-start(s32[8]{0:T(128)} %lengths.1) | copy-start | bytes 100
  30.4 10.7 %copy-start.2 = (s32[8]{0:T(128)S(1)}, s32[8]{0:T(128)}, u32[]{:S(2)}) copy-start(s32[8]{0:T(128)} %offsets.1) | copy-start | bytes 100
  36.1 12.7 %all-to-all-start.1 = ((bf16[4,256,256]{2,1,0:T(8,128)(2,1)}), bf16[4,256,256]{2,1,0:T(8,128)(2,1)S(1)}, u32[]{:S(2)}, u32[]{:S(2)}) async-start(bf16[4,256,256]{2,1,0:T(8,128)(2,1)} %get-tuple-element.20), calls=%async_computation.1 | async-start | bytes 1048576 | tf_op jit(solution)/shard_map/all_to_all | solution.py:370
  41.1 19.2 %copy-start = (bf16[512,256]{1,0:T(8,128)(2,1)S(1)}, bf16[512,256]{1,0:T(8,128)(2,1)}, u32[]{:S(2)}) copy-start(bf16[512,256]{1,0:T(8,128)(2,1)} %events.1) | copy-start | bytes 786436

commit v9 on v8

--- a/solution.py
+++ b/solution.py
@@ -190,7 +190,7 @@
 
 def first_kernel(
     lengths_hbm, offsets_hbm, x_any, gain_ref, w_hbm, keys, values, wo_hbm, moved_keys, moved_values,
-    out_hbm, odd_hbm,
+    out_hbm, late_hbm, odd_hbm,
     x_ref, w_ref, wo_ref, kv, normed_ref, even_ref, odd_ref, gated, out_ref, lengths, offsets,
     sems, kv_sems, out_sems,
 ):
@@ -231,10 +231,12 @@
     odd_copy = pltpu.make_async_copy(odd_ref, odd_hbm, sems.at[3])
     odd_copy.start()
     attend_slots(0, lengths, offsets, even_ref, kv, gated)
-    leave = [odd_copy]
+    early = out_ref.shape[1]
+    leave = [odd_copy, pltpu.make_async_copy(gated.at[early:], late_hbm, sems.at[6])]
+    leave[-1].start()
     for p in range(parts):
         out_ref[p] = lax.dot_general(
-            gated[...],
+            gated[:early, :],
             wo_ref[:, p * width : (p + 1) * width],
             NN,
             preferred_element_type=jnp.float32,
@@ -246,12 +248,14 @@
 
 
 def second_kernel(
-    lengths, offsets, b_hbm, keys, values, w_hbm, moved, out_ref, b_ref, w_ref, kv, gated, sems, kv_sems
+    lengths, offsets, b_hbm, keys, values, w_hbm, late_hbm, moved,
+    out_ref, b_ref, w_ref, kv, gated, sems, kv_sems,
 ):
     half_slots, width = kv.shape[0] // 2, kv.shape[2]
     copies = [
         pltpu.make_async_copy(b_hbm, b_ref, sems.at[0]),
         pltpu.make_async_copy(w_hbm, w_ref, sems.at[1]),
+        pltpu.make_async_copy(late_hbm, gated.at[: late_hbm.shape[0]], sems.at[2]),
     ]
     for c in copies:
         c.start()
@@ -259,7 +263,7 @@
     copies += cache_copies(1, offsets, keys, values, moved_keys, moved_values, kv, kv_sems)
     for c in copies:
         c.wait()
-    attend_slots(1, lengths, offsets, b_ref, kv, gated)
+    attend_slots(1, lengths, offsets, b_ref, kv, gated.at[late_hbm.shape[0] :])
     project_out(gated, w_ref, out_ref, width)
 
 
@@ -270,9 +274,13 @@
     bf16 = jnp.bfloat16
     return pl.pallas_call(
         first_kernel,
-        out_shape=(pltpu.HBM((parts, half, width), bf16), pltpu.HBM((half, wide), bf16)),
+        out_shape=(
+            pltpu.HBM((parts, half // 2, width), bf16),
+            pltpu.HBM((half // 2, width), bf16),
+            pltpu.HBM((half, wide), bf16),
+        ),
         in_specs=[HBM, HBM, ANY, VMEM, HBM, HBM, HBM, HBM, ANY, ANY],
-        out_specs=(HBM, HBM),
+        out_specs=(HBM, HBM, HBM),
         scratch_shapes=[
             pltpu.VMEM(x4.shape, bf16),
             pltpu.VMEM(w.shape, bf16),
@@ -282,10 +290,10 @@
             pltpu.VMEM((half, wide), bf16),
             pltpu.VMEM((half, wide), bf16),
             pltpu.VMEM((half, width), bf16),
-            pltpu.VMEM((parts, half, width), bf16),
+            pltpu.VMEM((parts, half // 2, width), bf16),
             pltpu.SMEM(lengths.shape, lengths.dtype),
             pltpu.SMEM(offsets.shape, offsets.dtype),
-            pltpu.SemaphoreType.DMA((6,)),
+            pltpu.SemaphoreType.DMA((7,)),
             pltpu.SemaphoreType.DMA((slots,)),
             pltpu.SemaphoreType.DMA((parts,)),
         ],
@@ -294,11 +302,11 @@
     )(in_hbm(lengths), in_hbm(offsets), x4, gain, in_hbm(w), in_hbm(keys), in_hbm(values), in_hbm(w_out), *moved)
 
 
-def second(lengths, offsets, branches, keys, values, w_out, moved):
+def second(lengths, offsets, branches, late, keys, values, w_out, moved):
     slots, cap, width = keys.shape
-    parts, rows = w_out.shape[1] // width, branches.shape[0]
+    parts, rows = w_out.shape[1] // width, late.shape[0] + branches.shape[0]
     bf16 = jnp.bfloat16
-    operands = [in_hbm(a) for a in (branches, keys, values, w_out, moved)]
+    operands = [in_hbm(a) for a in (branches, keys, values, w_out, late, moved)]
     return pl.pallas_call(
         second_kernel,
         out_shape=jax.ShapeDtypeStruct((parts, rows, width), bf16),
@@ -309,7 +317,7 @@
             pltpu.VMEM(w_out.shape, bf16),
             pltpu.VMEM((slots, cap, width), bf16),
             pltpu.VMEM((rows, width), bf16),
-            pltpu.SemaphoreType.DMA((2,)),
+            pltpu.SemaphoreType.DMA((3,)),
             pltpu.SemaphoreType.DMA((slots,)),
         ],
         compiler_params=pltpu.CompilerParams(vmem_limit_bytes=20 * 2**20),
@@ -333,27 +341,29 @@
     )(x4, gain)
 
 
-def combine_kernel(events, even, odd, out_ref):
-    parts, rows, _ = even.shape
-    half_slots = out_ref.shape[0] // 2 // NEW
-    for j in range(2 * half_slots):
+def combine_kernel(events, early, late, out_ref):
+    parts, early_rows, _ = early.shape
+    for j in range(out_ref.shape[0] // NEW):
         at = slice(j * NEW, (j + 1) * NEW)
-        terms_at = slice((j // 2) * NEW, (j // 2 + 1) * NEW)
-        terms = odd if j % 2 else even
-        total = terms[0, terms_at, :].astype(jnp.float32)
+        terms, start = early, j // 2 * NEW
+        if j % 2:
+            terms, start = late, start + late.shape[1] - out_ref.shape[0] // 2
+        elif start >= early_rows:
+            terms, start = late, start - early_rows
+        total = terms[0, start : start + NEW, :].astype(jnp.float32)
         for p in range(1, parts):
-            total = total + terms[p, terms_at, :].astype(jnp.float32)
+            total = total + terms[p, start : start + NEW, :].astype(jnp.float32)
         out_ref[at, :] = (events[at, :].astype(jnp.float32) + total).astype(out_ref.dtype)
 
 
-def combine(events, even, odd):
+def combine(events, early, late):
     return pl.pallas_call(
         combine_kernel,
         out_shape=jax.ShapeDtypeStruct(events.shape, events.dtype),
         in_specs=[VMEM, VMEM, VMEM],
         out_specs=VMEM,
         compiler_params=pltpu.CompilerParams(vmem_limit_bytes=6 * 2**20),
-    )(events, even, odd)
+    )(events, early, late)
 
 
 def in_hbm(array):
@@ -379,14 +389,14 @@
 
     w = w_uvqk.reshape(w_uvqk.shape[0], 4 * width)
     gain = gain_after(gathered, norm_gain[None, :])
-    even_part, odd_branches = first(
+    early_part, late_gated, odd_branches = first(
         lengths, swap_offset, gathered, gain, w, *caches, w_out, even
     )
-    even_terms = to_heads(even_part)
-    odd_part = second(lengths, swap_offset, odd_branches, *caches, w_out, odd)
-    odd_part, even_terms = lax.optimization_barrier((odd_part, even_terms))
-    odd_terms = to_heads(odd_part)
-    return combine(events, even_terms, odd_terms)
+    early_terms = to_heads(early_part)
+    late_part = second(lengths, swap_offset, odd_branches, late_gated, *caches, w_out, odd)
+    late_part, early_terms = lax.optimization_barrier((late_part, early_terms))
+    late_terms = to_heads(late_part)
+    return combine(events, early_terms, late_terms)
 
 
 def solution(mesh):

time: 62.2 us -> 61.9 us (level)
  waiting for transfers between devices: 4.49 us -> 1.68 us
  blocking collectives: 11.4 us -> 14 us
    all_to_all x2, waiting for transfers between devices: 3.88 us -> 1.08 us  [to_heads(): return lax.all_to_all(blocks, 'head', 0, 0)]
    all_to_all x1, blocking collectives: 11.4 us -> 14 us  [to_heads(): return lax.all_to_all(blocks, 'head', 0, 0)]
where the time goes in v9:
time: 61.9 us; the launch traced here: 60.8 us
  starting transfers between devices  27.3 us (44%)
  Pallas kernels  15.9 us (26%)
  blocking collectives  14 us (23%)
  local copies, waits for them, and re-layouts  1.86 us (3%)
  waiting for transfers between devices  1.68 us (3%)
    all_to_all x1, blocking collectives, to_heads(): return lax.all_to_all(blocks, 'head', 0, 0)  14 us
    ppermute x1, starting transfers between devices, on_device(): odd = lax.ppermute(odd_pay, 'user', across)  13.3 us
    all_to_all x2, starting transfers between devices, to_heads(): return lax.all_to_all(blocks, 'head', 0, 0)  9.66 us
    pallas_call x1, Pallas kernels, first(): pl.pallas_call(first_kernel, out_shape=(pltpu.HBM((parts, half // 2, widt...  5.61 us
    pallas_call x2, Pallas kernels, pack(): pl.pallas_call(functools.partial(pack_kernel, side), out_shape=outs, in_s...  5.45 us
    ppermute x2, starting transfers between devices, on_device(): lax.ppermute(pay, 'user', within)  4.33 us
    pallas_call x1, Pallas kernels, second(): pl.pallas_call(second_kernel, out_shape=jax.ShapeDtypeStruct((parts, rows...  3.96 us
    unnamed x11, local copies, waits for them, and re-layouts  1.86 us
  transfers between devices with their start and end apart: 5, of which 2 were waited for; matrix products, arithmetic and copies ran while one was open for 3% of the time, Pallas kernels for 20%

profile of v9, /device:TPU:6, one launch (start us, length us, event | category | flops | bytes accessed | tf_op | source)
XLA Modules:
  0.0 60.8 jit_solution(10368851353348567356)
XLA Ops:
  0.0 2.8 %shard_map.82 = (bf16[8,512,256]{2,1,0:T(8,128)(2,1)}, bf16[4,512,256]{2,1,0:T(8,128)(2,1)}) custom-call(s32[8]{0:T(128)} %lengths.1, bf16[8,512,256]{2,1,0:T(8,128)(2,1)} %keys.7, bf16[8,512,256]{2,1,0:T(8,128)(2,1)} %values.7, bf16[512,256]{1,0:T(8,128)(2,1)} %events.1), custom_call_target="tpu_custom_call" | custom-call | bytes 4000000 | tf_op jit(solution)/shard_map/pallas_call | solution.py:76
  2.8 13.3 %collective-permute-start.2 = (bf16[8,512,256]{2,1,0:T(8,128)(2,1)}, bf16[8,512,256]{2,1,0:T(8,128)(2,1)}, u32[]{:S(2)}, u32[]{:S(2)}) collective-permute-start(bf16[8,512,256]{2,1,0:T(8,128)(2,1)} %get-tuple-element.16), channel_id=1, source_target_pairs={{0,508},{4,8},{8,4},{12,16},{16,12},{20,24},{24,20},{28,32},{32,28... | collective-permute-start | bytes 6291464 | tf_op jit(solution)/shard_map/ppermute | solution.py:384
  16.1 4.8 %all-to-all-start = ((bf16[4,512,256]{2,1,0:T(8,128)(2,1)}), bf16[4,512,256]{2,1,0:T(8,128)(2,1)S(1)}, u32[]{:S(2)}, u32[]{:S(2)}) async-start(bf16[4,512,256]{2,1,0:T(8,128)(2,1)} %get-tuple-element.15), calls=%async_computation | async-start | bytes 2097152 | tf_op jit(solution)/shard_map/all_to_all | solution.py:380
  20.9 0.0 copy-start.4
  20.9 2.6 %shard_map.84 = (bf16[4,512,256]{2,1,0:T(8,128)(2,1)}, bf16[4,512,256]{2,1,0:T(8,128)(2,1)}) custom-call(s32[8]{0:T(128)} %lengths.1, bf16[8,512,256]{2,1,0:T(8,128)(2,1)} %keys.7, bf16[8,512,256]{2,1,0:T(8,128)(2,1)} %values.7), custom_call_target="tpu_custom_call" | custom-call | bytes 15000000 | tf_op jit(solution)/shard_map/pallas_call | solution.py:76
  23.6 1.9 %collective-permute-start = (bf16[4,512,256]{2,1,0:T(8,128)(2,1)}, bf16[4,512,256]{2,1,0:T(8,128)(2,1)S(1)}, u32[]{:S(2)}, u32[]{:S(2)}) collective-permute-start(bf16[4,512,256]{2,1,0:T(8,128)(2,1)} %get-tuple-element.18), channel_id=1, source_target_pairs={{0,4},{4,0},{8,12},{12,8},{16,20},{20,16},{24,28},{28,24},{32,36},... | collective-permute-start | bytes 3145736 | tf_op jit(solution)/shard_map/ppermute | solution.py:388
  25.5 2.4 %collective-permute-start.1 = (bf16[4,512,256]{2,1,0:T(8,128)(2,1)}, bf16[4,512,256]{2,1,0:T(8,128)(2,1)S(1)}, u32[]{:S(2)}, u32[]{:S(2)}) collective-permute-start(bf16[4,512,256]{2,1,0:T(8,128)(2,1)} %get-tuple-element.19), channel_id=1, source_target_pairs={{0,4},{4,0},{8,12},{12,8},{16,20},{20,16},{24,28},{28,24},{32,36},... | collective-permute-start | bytes 3145736 | tf_op jit(solution)/shard_map/ppermute | solution.py:388
  27.9 0.0 copy-done.4
  27.9 0.0 copy-start.3
  27.9 1.8 %copy.9 = bf16[128,8,4,256]{3,1,2,0:T(8,128)(2,1)} copy(bf16[128,8,4,256]{3,2,1,0:T(4,128)(2,1)S(1)} %bitcast.5) | data formatting | bytes 4194304
  29.8 0.0 all-to-all-done.x_any
  29.8 0.0 copy-done.3
  29.8 0.0 collective-permute-done.moved_keys
  29.8 0.6 collective-permute-done.1.moved_values
  30.4 0.0 copy-start.1
  30.4 0.0 copy-start.2
  30.4 5.6 %shard_map.85 = (bf16[4,128,256]{2,1,0:T(8,128)(2,1)}, bf16[128,256]{1,0:T(8,128)(2,1)}, bf16[256,1024]{1,0:T(8,128)(2,1)}) custom-call(s32[8]{0:T(128)} %lengths.1, s32[8]{0:T(128)} %offsets.1, bf16[4,512,256]{2,1,0:T(8,128)(2,1)S(1)} %all-to-all-done.x_any, f32[1,1024]{1,0:T(1,128)S(1)} %shard_map.83.gain_ref, bf16[1024,1024]{1,0:T(8,128)(2,1)} %bitcast.4, ...), custom_call_target="tpu_custom_call" | custom-call | flops 100000000 | tf_op jit(solution)/shard_map/pallas_call | solution.py:275
  36.0 4.9 %all-to-all-start.1 = ((bf16[4,128,256]{2,1,0:T(8,128)(2,1)}), bf16[4,128,256]{2,1,0:T(8,128)(2,1)S(1)}, u32[]{:S(2)}, u32[]{:S(2)}) async-start(bf16[4,128,256]{2,1,0:T(8,128)(2,1)} %get-tuple-element.22), calls=%async_computation.1 | async-start | bytes 524288 | tf_op jit(solution)/shard_map/all_to_all | solution.py:380
  40.9 0.0 collective-permute-done.2.moved
  40.9 0.0 copy-done.1
  40.9 0.0 copy-done.2
  40.9 0.0 copy-start
  40.9 4.0 %shard_map.86 = bf16[4,384,256]{2,1,0:T(8,128)(2,1)S(1)} custom-call(s32[8]{0:T(128)S(1)} %copy-done.1, s32[8]{0:T(128)S(1)} %copy-done.2, bf16[256,1024]{1,0:T(8,128)(2,1)} %get-tuple-element.20.b_hbm, bf16[8,512,256]{2,1,0:T(8,128)(2,1)} %keys.7, bf16[8,512,256]{2,1,0:T(8,128)(2,1)} %values.7, bf16[256,1024]{1,0:T(8,128)(2,1)} %w_hbm.1, ...), custom_call_target="tpu_custom_call" | custom-call | flops 3000000000 | tf_op jit(solution)/shard_map/pallas_call | solution.py:310
  44.9 1.1 %all-to-all-done.1.early = bf16[4,128,256]{2,1,0:T(8,128)(2,1)S(1)} async-done(((bf16[4,128,256]{2,1,0:T(8,128)(2,1)}), bf16[4,128,256]{2,1,0:T(8,128)(2,1)S(1)}, u32[]{:S(2)}, u32[]{:S(2)}) %all-to-all-start.1) | async-done | bytes 262176 | tf_op jit(solution)/shard_map/all_to_all | solution.py:380
  45.9 14.0 %all_to_all.15.late = bf16[4,384,256]{2,1,0:T(8,128)(2,1)S(1)} all-to-all(bf16[4,384,256]{2,1,0:T(8,128)(2,1)S(1)} %shard_map.86), channel_id=1, replica_groups=mesh['user'=128,'head'=4] {'head'}, dimensions={0} | all-to-all | bytes 1572864 | tf_op jit(solution)/shard_map/all_to_all | solution.py:380
  59.9 0.0 copy-done
  59.9 0.9 %shard_map.87 = bf16[512,256]{1,0:T(8,128)(2,1)} custom-call(bf16[512,256]{1,0:T(8,128)(2,1)S(1)} %copy-done, bf16[4,128,256]{2,1,0:T(8,128)(2,1)S(1)} %all-to-all-done.1.early, bf16[4,384,256]{2,1,0:T(8,128)(2,1)S(1)} %all_to_all.15.late), custom_call_target="tpu_custom_call" | custom-call | tf_op jit(solution)/shard_map/pallas_call | solution.py:360
  (1 shorter events, 0.0 us)
Async XLA Ops:
  2.8 38.0 %collective-permute-start.2 = (bf16[8,512,256]{2,1,0:T(8,128)(2,1)}, bf16[8,512,256]{2,1,0:T(8,128)(2,1)}, u32[]{:S(2)}, u32[]{:S(2)}) collective-permute-start(bf16[8,512,256]{2,1,0:T(8,128)(2,1)} %get-tuple-element.16), channel_id=1, source_target_pairs={{0,508},{4,8},{8,4},{12,16},{16,12},{20,24},{24,20},{28,32},{32,28... | collective-permute-start | bytes 6291464 | tf_op jit(solution)/shard_map/ppermute | solution.py:384
  16.1 13.6 %all-to-all-start = ((bf16[4,512,256]{2,1,0:T(8,128)(2,1)}), bf16[4,512,256]{2,1,0:T(8,128)(2,1)S(1)}, u32[]{:S(2)}, u32[]{:S(2)}) async-start(bf16[4,512,256]{2,1,0:T(8,128)(2,1)} %get-tuple-element.15), calls=%async_computation | async-start | bytes 2097152 | tf_op jit(solution)/shard_map/all_to_all | solution.py:380
  20.9 7.0 %copy-start.4 = (bf16[1024,4,256]{2,1,0:T(4,128)(2,1)S(1)}, bf16[1024,4,256]{2,1,0:T(4,128)(2,1)}, u32[]{:S(2)}) copy-start(bf16[1024,4,256]{2,1,0:T(4,128)(2,1)} %param.10) | copy-start | bytes 6291460
  23.6 6.2 %collective-permute-start = (bf16[4,512,256]{2,1,0:T(8,128)(2,1)}, bf16[4,512,256]{2,1,0:T(8,128)(2,1)S(1)}, u32[]{:S(2)}, u32[]{:S(2)}) collective-permute-start(bf16[4,512,256]{2,1,0:T(8,128)(2,1)} %get-tuple-element.18), channel_id=1, source_target_pairs={{0,4},{4,0},{8,12},{12,8},{16,20},{20,16},{24,28},{28,24},{32,36},... | collective-permute-start | bytes 3145736 | tf_op jit(solution)/shard_map/ppermute | solution.py:388
  25.5 4.9 %collective-permute-start.1 = (bf16[4,512,256]{2,1,0:T(8,128)(2,1)}, bf16[4,512,256]{2,1,0:T(8,128)(2,1)S(1)}, u32[]{:S(2)}, u32[]{:S(2)}) collective-permute-start(bf16[4,512,256]{2,1,0:T(8,128)(2,1)} %get-tuple-element.19), channel_id=1, source_target_pairs={{0,4},{4,0},{8,12},{12,8},{16,20},{20,16},{24,28},{28,24},{32,36},... | collective-permute-start | bytes 3145736 | tf_op jit(solution)/shard_map/ppermute | solution.py:388
  27.9 1.9 %copy-start.3 = (f32[1024]{0:T(1024)S(1)}, f32[1024]{0:T(1024)}, u32[]{:S(2)}) copy-start(f32[1024]{0:T(1024)} %param.9) | copy-start | bytes 12292
  30.4 10.5 %copy-start.1 = (s32[8]{0:T(128)S(1)}, s32[8]{0:T(128)}, u32[]{:S(2)}) copy-start(s32[8]{0:T(128)} %lengths.1) | copy-start | bytes 100
  30.4 10.5 %copy-start.2 = (s32[8]{0:T(128)S(1)}, s32[8]{0:T(128)}, u32[]{:S(2)}) copy-start(s32[8]{0:T(128)} %offsets.1) | copy-start | bytes 100
  36.0 9.9 %all-to-all-start.1 = ((bf16[4,128,256]{2,1,0:T(8,128)(2,1)}), bf16[4,128,256]{2,1,0:T(8,128)(2,1)S(1)}, u32[]{:S(2)}, u32[]{:S(2)}) async-start(bf16[4,128,256]{2,1,0:T(8,128)(2,1)} %get-tuple-element.22), calls=%async_computation.1 | async-start | bytes 524288 | tf_op jit(solution)/shard_map/all_to_all | solution.py:380
  40.9 19.1 %copy-start = (bf16[512,256]{1,0:T(8,128)(2,1)S(1)}, bf16[512,256]{1,0:T(8,128)(2,1)}, u32[]{:S(2)}) copy-start(bf16[512,256]{1,0:T(8,128)(2,1)} %events.1) | copy-start | bytes 786436

commit v10 on v8

--- a/solution.py
+++ b/solution.py
@@ -329,7 +329,7 @@
         in_specs=[ANY, VMEM],
         out_specs=VMEM,
         compiler_params=pltpu.CompilerParams(vmem_limit_bytes=2**20),
-        cost_estimate=pl.CostEstimate(flops=9 * 10**9, bytes_accessed=0, transcendentals=0),
+        cost_estimate=pl.CostEstimate(flops=40 * 10**9, bytes_accessed=0, transcendentals=0),
     )(x4, gain)
 
 

time: 62.2 us -> 61.3 us (0.986)
  waiting for transfers between devices: 4.49 us -> 5.23 us
  Pallas kernels: 16 us -> 15.3 us
    ppermute x1, starting transfers between devices: 13.3 us -> 8.29 us  [on_device(): odd = lax.ppermute(odd_pay, 'user', across)]
    ppermute x1, waiting for transfers between devices: 0.01 us -> 4.62 us  [on_device(): odd = lax.ppermute(odd_pay, 'user', across)]
    all_to_all x2, starting transfers between devices: 9.72 us -> 14.2 us  [to_heads(): return lax.all_to_all(blocks, 'head', 0, 0)]
    all_to_all x2, waiting for transfers between devices: 3.88 us -> 0.01 us  [to_heads(): return lax.all_to_all(blocks, 'head', 0, 0)]
  transfers between devices with their start and end apart: 5 -> 5, of which waited for: 2 -> 2; matrix products, arithmetic and copies ran while one was open for 3% -> 3% of each run, Pallas kernels for 20% -> 19%
where the time goes in v10:
time: 61.3 us; the launch traced here: 60.2 us
  starting transfers between devices  26.8 us (44%)
  Pallas kernels  15.3 us (25%)
  blocking collectives  10.9 us (18%)
  waiting for transfers between devices  5.23 us (9%)
  local copies, waits for them, and re-layouts  1.86 us (3%)
    all_to_all x2, starting transfers between devices, to_heads(): return lax.all_to_all(blocks, 'head', 0, 0)  14.2 us
    all_to_all x1, blocking collectives, to_heads(): return lax.all_to_all(blocks, 'head', 0, 0)  10.9 us
    ppermute x1, starting transfers between devices, on_device(): odd = lax.ppermute(odd_pay, 'user', across)  8.29 us
    pallas_call x2, Pallas kernels, pack(): pl.pallas_call(functools.partial(pack_kernel, side), out_shape=outs, in_s...  5.29 us
    pallas_call x1, Pallas kernels, first(): pl.pallas_call(first_kernel, out_shape=(pltpu.HBM((parts, half, width), b...  5.27 us
    ppermute x1, waiting for transfers between devices, on_device(): odd = lax.ppermute(odd_pay, 'user', across)  4.62 us
    ppermute x2, starting transfers between devices, on_device(): lax.ppermute(pay, 'user', within)  4.33 us
    pallas_call x1, Pallas kernels, second(): pl.pallas_call(second_kernel, out_shape=jax.ShapeDtypeStruct((parts, rows...  3.9 us
  transfers between devices with their start and end apart: 5, of which 2 were waited for; matrix products, arithmetic and copies ran while one was open for 3% of the time, Pallas kernels for 19%

profile of v10, /device:TPU:6, one launch (start us, length us, event | category | flops | bytes accessed | tf_op | source)
XLA Modules:
  0.0 60.2 jit_solution(17008064847520446753)
XLA Ops:
  0.0 2.8 %shard_map.82 = (bf16[8,512,256]{2,1,0:T(8,128)(2,1)}, bf16[4,512,256]{2,1,0:T(8,128)(2,1)}) custom-call(s32[8]{0:T(128)} %lengths.1, bf16[8,512,256]{2,1,0:T(8,128)(2,1)} %keys.7, bf16[8,512,256]{2,1,0:T(8,128)(2,1)} %values.7, bf16[512,256]{1,0:T(8,128)(2,1)} %events.1), custom_call_target="tpu_custom_call" | custom-call | bytes 4000000 | tf_op jit(solution)/shard_map/pallas_call | solution.py:76
  2.8 9.4 %all-to-all-start = ((bf16[4,512,256]{2,1,0:T(8,128)(2,1)}), bf16[4,512,256]{2,1,0:T(8,128)(2,1)S(1)}, u32[]{:S(2)}, u32[]{:S(2)}) async-start(bf16[4,512,256]{2,1,0:T(8,128)(2,1)} %get-tuple-element.14), calls=%async_computation | async-start | bytes 2097152 | tf_op jit(solution)/shard_map/all_to_all | solution.py:370
  12.2 0.0 copy-start.4
  12.2 8.3 %collective-permute-start.2 = (bf16[8,512,256]{2,1,0:T(8,128)(2,1)}, bf16[8,512,256]{2,1,0:T(8,128)(2,1)}, u32[]{:S(2)}, u32[]{:S(2)}) collective-permute-start(bf16[8,512,256]{2,1,0:T(8,128)(2,1)} %get-tuple-element.15), channel_id=1, source_target_pairs={{0,508},{4,8},{8,4},{12,16},{16,12},{20,24},{24,20},{28,32},{32,28... | collective-permute-start | bytes 6291464 | tf_op jit(solution)/shard_map/ppermute | solution.py:374
  20.5 2.5 %shard_map.84 = (bf16[4,512,256]{2,1,0:T(8,128)(2,1)}, bf16[4,512,256]{2,1,0:T(8,128)(2,1)}) custom-call(s32[8]{0:T(128)} %lengths.1, bf16[8,512,256]{2,1,0:T(8,128)(2,1)} %keys.7, bf16[8,512,256]{2,1,0:T(8,128)(2,1)} %values.7), custom_call_target="tpu_custom_call" | custom-call | bytes 15000000 | tf_op jit(solution)/shard_map/pallas_call | solution.py:76
  23.0 1.9 %collective-permute-start = (bf16[4,512,256]{2,1,0:T(8,128)(2,1)}, bf16[4,512,256]{2,1,0:T(8,128)(2,1)S(1)}, u32[]{:S(2)}, u32[]{:S(2)}) collective-permute-start(bf16[4,512,256]{2,1,0:T(8,128)(2,1)} %get-tuple-element.17), channel_id=1, source_target_pairs={{0,4},{4,0},{8,12},{12,8},{16,20},{20,16},{24,28},{28,24},{32,36},... | collective-permute-start | bytes 3145736 | tf_op jit(solution)/shard_map/ppermute | solution.py:378
  24.9 2.4 %collective-permute-start.1 = (bf16[4,512,256]{2,1,0:T(8,128)(2,1)}, bf16[4,512,256]{2,1,0:T(8,128)(2,1)S(1)}, u32[]{:S(2)}, u32[]{:S(2)}) collective-permute-start(bf16[4,512,256]{2,1,0:T(8,128)(2,1)} %get-tuple-element.18), channel_id=1, source_target_pairs={{0,4},{4,0},{8,12},{12,8},{16,20},{20,16},{24,28},{28,24},{32,36},... | collective-permute-start | bytes 3145736 | tf_op jit(solution)/shard_map/ppermute | solution.py:378
  27.3 0.0 copy-done.4
  27.3 0.0 copy-start.3
  27.3 1.8 %copy.9 = bf16[128,8,4,256]{3,1,2,0:T(8,128)(2,1)} copy(bf16[128,8,4,256]{3,2,1,0:T(4,128)(2,1)S(1)} %bitcast.5) | data formatting | bytes 4194304
  29.2 0.0 all-to-all-done.x_any
  29.2 0.0 copy-done.3
  29.2 0.0 collective-permute-done.moved_keys
  29.2 0.6 collective-permute-done.1.moved_values
  29.8 0.0 copy-start.1
  29.8 0.0 copy-start.2
  29.8 5.3 %shard_map.85 = (bf16[4,256,256]{2,1,0:T(8,128)(2,1)}, bf16[256,1024]{1,0:T(8,128)(2,1)}) custom-call(s32[8]{0:T(128)} %lengths.1, s32[8]{0:T(128)} %offsets.1, bf16[4,512,256]{2,1,0:T(8,128)(2,1)S(1)} %all-to-all-done.x_any, f32[1,1024]{1,0:T(1,128)S(1)} %shard_map.83.gain_ref, bf16[1024,1024]{1,0:T(8,128)(2,1)} %bitcast.4, bf16[8,512,256]{2,1,0:T(8,128)(2,1)} %keys.7, ...), custom_call_target="tpu_custom_call" | custom-call | flops 100000000 | tf_op jit(solution)/shard_map/pallas_call | solution.py:271
  35.1 4.8 %all-to-all-start.1 = ((bf16[4,256,256]{2,1,0:T(8,128)(2,1)}), bf16[4,256,256]{2,1,0:T(8,128)(2,1)S(1)}, u32[]{:S(2)}, u32[]{:S(2)}) async-start(bf16[4,256,256]{2,1,0:T(8,128)(2,1)} %get-tuple-element.20), calls=%async_computation.1 | async-start | bytes 1048576 | tf_op jit(solution)/shard_map/all_to_all | solution.py:370
  39.9 4.6 %collective-permute-done.2.moved = bf16[8,512,256]{2,1,0:T(8,128)(2,1)} collective-permute-done((bf16[8,512,256]{2,1,0:T(8,128)(2,1)}, bf16[8,512,256]{2,1,0:T(8,128)(2,1)}, u32[]{:S(2)}, u32[]{:S(2)}) %collective-permute-start.2) | collective-permute-done | bytes 2097184 | tf_op jit(solution)/shard_map/ppermute | solution.py:374
  44.5 0.0 copy-done.1
  44.5 0.0 copy-done.2
  44.5 0.0 copy-start
  44.5 3.9 %shard_map.86 = bf16[4,256,256]{2,1,0:T(8,128)(2,1)S(1)} custom-call(s32[8]{0:T(128)S(1)} %copy-done.1, s32[8]{0:T(128)S(1)} %copy-done.2, bf16[256,1024]{1,0:T(8,128)(2,1)} %get-tuple-element.19.b_hbm, bf16[8,512,256]{2,1,0:T(8,128)(2,1)} %keys.7, bf16[8,512,256]{2,1,0:T(8,128)(2,1)} %values.7, bf16[256,1024]{1,0:T(8,128)(2,1)} %w_hbm.1, ...), custom_call_target="tpu_custom_call" | custom-call | flops 3000000000 | tf_op jit(solution)/shard_map/pallas_call | solution.py:302
  48.4 0.0 all-to-all-done.1.even
  48.4 10.9 %all_to_all.15.odd = bf16[4,256,256]{2,1,0:T(8,128)(2,1)S(1)} all-to-all(bf16[4,256,256]{2,1,0:T(8,128)(2,1)S(1)} %shard_map.86), channel_id=1, replica_groups=mesh['user'=128,'head'=4] {'head'}, dimensions={0} | all-to-all | bytes 1048576 | tf_op jit(solution)/shard_map/all_to_all | solution.py:370
  59.3 0.0 copy-done
  59.3 0.9 %shard_map.87 = bf16[512,256]{1,0:T(8,128)(2,1)} custom-call(bf16[512,256]{1,0:T(8,128)(2,1)S(1)} %copy-done, bf16[4,256,256]{2,1,0:T(8,128)(2,1)S(1)} %all-to-all-done.1.even, bf16[4,256,256]{2,1,0:T(8,128)(2,1)S(1)} %all_to_all.15.odd), custom_call_target="tpu_custom_call" | custom-call | tf_op jit(solution)/shard_map/pallas_call | solution.py:350
  (1 shorter events, 0.0 us)
Async XLA Ops:
  2.8 26.3 %all-to-all-start = ((bf16[4,512,256]{2,1,0:T(8,128)(2,1)}), bf16[4,512,256]{2,1,0:T(8,128)(2,1)S(1)}, u32[]{:S(2)}, u32[]{:S(2)}) async-start(bf16[4,512,256]{2,1,0:T(8,128)(2,1)} %get-tuple-element.14), calls=%async_computation | async-start | bytes 2097152 | tf_op jit(solution)/shard_map/all_to_all | solution.py:370
  12.2 15.1 %copy-start.4 = (bf16[1024,4,256]{2,1,0:T(4,128)(2,1)S(1)}, bf16[1024,4,256]{2,1,0:T(4,128)(2,1)}, u32[]{:S(2)}) copy-start(bf16[1024,4,256]{2,1,0:T(4,128)(2,1)} %param.10) | copy-start | bytes 6291460
  12.2 32.3 %collective-permute-start.2 = (bf16[8,512,256]{2,1,0:T(8,128)(2,1)}, bf16[8,512,256]{2,1,0:T(8,128)(2,1)}, u32[]{:S(2)}, u32[]{:S(2)}) collective-permute-start(bf16[8,512,256]{2,1,0:T(8,128)(2,1)} %get-tuple-element.15), channel_id=1, source_target_pairs={{0,508},{4,8},{8,4},{12,16},{16,12},{20,24},{24,20},{28,32},{32,28... | collective-permute-start | bytes 6291464 | tf_op jit(solution)/shard_map/ppermute | solution.py:374
  23.0 6.2 %collective-permute-start = (bf16[4,512,256]{2,1,0:T(8,128)(2,1)}, bf16[4,512,256]{2,1,0:T(8,128)(2,1)S(1)}, u32[]{:S(2)}, u32[]{:S(2)}) collective-permute-start(bf16[4,512,256]{2,1,0:T(8,128)(2,1)} %get-tuple-element.17), channel_id=1, source_target_pairs={{0,4},{4,0},{8,12},{12,8},{16,20},{20,16},{24,28},{28,24},{32,36},... | collective-permute-start | bytes 3145736 | tf_op jit(solution)/shard_map/ppermute | solution.py:378
  24.9 4.9 %collective-permute-start.1 = (bf16[4,512,256]{2,1,0:T(8,128)(2,1)}, bf16[4,512,256]{2,1,0:T(8,128)(2,1)S(1)}, u32[]{:S(2)}, u32[]{:S(2)}) collective-permute-start(bf16[4,512,256]{2,1,0:T(8,128)(2,1)} %get-tuple-element.18), channel_id=1, source_target_pairs={{0,4},{4,0},{8,12},{12,8},{16,20},{20,16},{24,28},{28,24},{32,36},... | collective-permute-start | bytes 3145736 | tf_op jit(solution)/shard_map/ppermute | solution.py:378
  27.3 1.9 %copy-start.3 = (f32[1024]{0:T(1024)S(1)}, f32[1024]{0:T(1024)}, u32[]{:S(2)}) copy-start(f32[1024]{0:T(1024)} %param.9) | copy-start | bytes 12292
  29.8 14.7 %copy-start.1 = (s32[8]{0:T(128)S(1)}, s32[8]{0:T(128)}, u32[]{:S(2)}) copy-start(s32[8]{0:T(128)} %lengths.1) | copy-start | bytes 100
  29.8 14.7 %copy-start.2 = (s32[8]{0:T(128)S(1)}, s32[8]{0:T(128)}, u32[]{:S(2)}) copy-start(s32[8]{0:T(128)} %offsets.1) | copy-start | bytes 100
  35.1 13.4 %all-to-all-start.1 = ((bf16[4,256,256]{2,1,0:T(8,128)(2,1)}), bf16[4,256,256]{2,1,0:T(8,128)(2,1)S(1)}, u32[]{:S(2)}, u32[]{:S(2)}) async-start(bf16[4,256,256]{2,1,0:T(8,128)(2,1)} %get-tuple-element.20), calls=%async_computation.1 | async-start | bytes 1048576 | tf_op jit(solution)/shard_map/all_to_all | solution.py:370
  44.5 14.8 %copy-start = (bf16[512,256]{1,0:T(8,128)(2,1)S(1)}, bf16[512,256]{1,0:T(8,128)(2,1)}, u32[]{:S(2)}) copy-start(bf16[512,256]{1,0:T(8,128)(2,1)} %events.1) | copy-start | bytes 786436

commit v11 on v10

--- a/solution.py
+++ b/solution.py
@@ -189,7 +189,7 @@
 
 
 def first_kernel(
-    lengths_hbm, offsets_hbm, x_any, gain_ref, w_hbm, keys, values, wo_hbm, moved_keys, moved_values,
+    lengths_hbm, offsets_hbm, x_any, gain_ref, w_hbm, keys, values, wo_hbm, moved,
     out_hbm, odd_hbm,
     x_ref, w_ref, wo_ref, kv, normed_ref, even_ref, odd_ref, gated, out_ref, lengths, offsets,
     sems, kv_sems, out_sems,
@@ -209,6 +209,8 @@
         c.start()
     for c in layout:
         c.wait()
+    half_slots = kv.shape[0] // 2
+    moved_keys, moved_values = moved.at[:half_slots], moved.at[half_slots:]
     rest += cache_copies(0, offsets, keys, values, moved_keys, moved_values, kv, kv_sems)
     x_copy.wait()
     x = jnp.concatenate([x_ref[p] for p in range(parts)], axis=1).astype(jnp.float32)
@@ -271,7 +273,7 @@
     return pl.pallas_call(
         first_kernel,
         out_shape=(pltpu.HBM((parts, half, width), bf16), pltpu.HBM((half, wide), bf16)),
-        in_specs=[HBM, HBM, ANY, VMEM, HBM, HBM, HBM, HBM, ANY, ANY],
+        in_specs=[HBM, HBM, ANY, VMEM, HBM, HBM, HBM, HBM, ANY],
         out_specs=(HBM, HBM),
         scratch_shapes=[
             pltpu.VMEM(x4.shape, bf16),
@@ -291,7 +293,7 @@
         ],
         compiler_params=pltpu.CompilerParams(vmem_limit_bytes=28 * 2**20),
         cost_estimate=pl.CostEstimate(flops=10**8, bytes_accessed=0, transcendentals=0),
-    )(in_hbm(lengths), in_hbm(offsets), x4, gain, in_hbm(w), in_hbm(keys), in_hbm(values), in_hbm(w_out), *moved)
+    )(in_hbm(lengths), in_hbm(offsets), x4, gain, in_hbm(w), in_hbm(keys), in_hbm(values), in_hbm(w_out), moved)
 
 
 def second(lengths, offsets, branches, keys, values, w_out, moved):
@@ -375,7 +377,8 @@
     gathered = to_heads(spread)
     later_lengths, _ = lax.optimization_barrier((lengths, odd_pay))
     within = [(i, i ^ 1) for i in range(users)]
-    even = [lax.ppermute(pay, "user", within) for pay in pack(0, 2, later_lengths, *caches)]
+    (even_pay,) = pack(0, 1, later_lengths, *caches)
+    even = lax.ppermute(even_pay, "user", within)
 
     w = w_uvqk.reshape(w_uvqk.shape[0], 4 * width)
     gain = gain_after(gathered, norm_gain[None, :])

time: 61.3 us -> 61 us (level)
  starting transfers between devices: 26.8 us -> 24.4 us
  waiting for transfers between devices: 5.23 us -> 7.35 us
    ppermute x2 -> x1, starting transfers between devices: 4.33 us -> 1.92 us  [on_device(): even = lax.ppermute(even_pay, 'user', within)]
    ppermute x2 -> x1, waiting for transfers between devices: 0.6 us -> 2.49 us  [on_device(): even = lax.ppermute(even_pay, 'user', within)]
  transfers between devices with their start and end apart: 5 -> 4, of which waited for: 2 -> 2; matrix products, arithmetic and copies ran while one was open for 3% -> 3% of each run, Pallas kernels for 19% -> 20%
where the time goes in v11:
time: 61 us; the launch traced here: 59.9 us
  starting transfers between devices  24.4 us (40%)
  Pallas kernels  15.7 us (26%)
  blocking collectives  10.6 us (17%)
  waiting for transfers between devices  7.35 us (12%)
  local copies, waits for them, and re-layouts  1.84 us (3%)
    all_to_all x2, starting transfers between devices, to_heads(): return lax.all_to_all(blocks, 'head', 0, 0)  14.2 us
    all_to_all x1, blocking collectives, to_heads(): return lax.all_to_all(blocks, 'head', 0, 0)  10.6 us
    ppermute x1, starting transfers between devices, on_device(): odd = lax.ppermute(odd_pay, 'user', across)  8.29 us
    pallas_call x1, Pallas kernels, first(): pl.pallas_call(first_kernel, out_shape=(pltpu.HBM((parts, half, width), b...  5.61 us
    pallas_call x2, Pallas kernels, pack(): pl.pallas_call(functools.partial(pack_kernel, side), out_shape=outs, in_s...  5.3 us
    ppermute x1, waiting for transfers between devices, on_device(): odd = lax.ppermute(odd_pay, 'user', across)  4.86 us
    pallas_call x1, Pallas kernels, second(): pl.pallas_call(second_kernel, out_shape=jax.ShapeDtypeStruct((parts, rows...  3.9 us
    ppermute x1, waiting for transfers between devices, on_device(): even = lax.ppermute(even_pay, 'user', within)  2.49 us
  transfers between devices with their start and end apart: 4, of which 2 were waited for; matrix products, arithmetic and copies ran while one was open for 3% of the time, Pallas kernels for 20%

profile of v11, /device:TPU:6, one launch (start us, length us, event | category | flops | bytes accessed | tf_op | source)
XLA Modules:
  0.0 59.9 jit_solution(6091914931080461589)
XLA Ops:
  0.0 2.8 %shard_map.82 = (bf16[8,512,256]{2,1,0:T(8,128)(2,1)}, bf16[4,512,256]{2,1,0:T(8,128)(2,1)}) custom-call(s32[8]{0:T(128)} %lengths.1, bf16[8,512,256]{2,1,0:T(8,128)(2,1)} %keys.7, bf16[8,512,256]{2,1,0:T(8,128)(2,1)} %values.7, bf16[512,256]{1,0:T(8,128)(2,1)} %events.1), custom_call_target="tpu_custom_call" | custom-call | bytes 4000000 | tf_op jit(solution)/shard_map/pallas_call | solution.py:76
  2.9 9.4 %all-to-all-start = ((bf16[4,512,256]{2,1,0:T(8,128)(2,1)}), bf16[4,512,256]{2,1,0:T(8,128)(2,1)S(1)}, u32[]{:S(2)}, u32[]{:S(2)}) async-start(bf16[4,512,256]{2,1,0:T(8,128)(2,1)} %get-tuple-element.12), calls=%async_computation | async-start | bytes 2097152 | tf_op jit(solution)/shard_map/all_to_all | solution.py:372
  12.2 0.0 copy-start.4
  12.2 8.3 %collective-permute-start.1 = (bf16[8,512,256]{2,1,0:T(8,128)(2,1)}, bf16[8,512,256]{2,1,0:T(8,128)(2,1)}, u32[]{:S(2)}, u32[]{:S(2)}) collective-permute-start(bf16[8,512,256]{2,1,0:T(8,128)(2,1)} %get-tuple-element.13), channel_id=1, source_target_pairs={{0,508},{4,8},{8,4},{12,16},{16,12},{20,24},{24,20},{28,32},{32,28... | collective-permute-start | bytes 6291464 | tf_op jit(solution)/shard_map/ppermute | solution.py:376
  20.5 2.5 %shard_map.84 = bf16[8,512,256]{2,1,0:T(8,128)(2,1)} custom-call(s32[8]{0:T(128)} %lengths.1, bf16[8,512,256]{2,1,0:T(8,128)(2,1)} %keys.7, bf16[8,512,256]{2,1,0:T(8,128)(2,1)} %values.7), custom_call_target="tpu_custom_call" | custom-call | bytes 15000000 | tf_op jit(solution)/shard_map/pallas_call | solution.py:76
  23.0 1.9 %collective-permute-start = (bf16[8,512,256]{2,1,0:T(8,128)(2,1)}, bf16[8,512,256]{2,1,0:T(8,128)(2,1)S(1)}, u32[]{:S(2)}, u32[]{:S(2)}) collective-permute-start(bf16[8,512,256]{2,1,0:T(8,128)(2,1)} %shard_map.84), channel_id=1, source_target_pairs={{0,4},{4,0},{8,12},{12,8},{16,20},{20,16},{24,28},{28,24},{32,36},... | collective-permute-start | bytes 6291464 | tf_op jit(solution)/shard_map/ppermute | solution.py:381
  24.9 0.0 copy-done.4
  24.9 0.0 copy-start.3
  24.9 1.8 %copy.9 = bf16[128,8,4,256]{3,1,2,0:T(8,128)(2,1)} copy(bf16[128,8,4,256]{3,2,1,0:T(4,128)(2,1)S(1)} %bitcast.5) | data formatting | bytes 4194304
  26.7 0.0 all-to-all-done.x_any
  26.7 0.0 copy-done.3
  26.7 2.5 %collective-permute-done.moved = bf16[8,512,256]{2,1,0:T(8,128)(2,1)S(1)} collective-permute-done((bf16[8,512,256]{2,1,0:T(8,128)(2,1)}, bf16[8,512,256]{2,1,0:T(8,128)(2,1)S(1)}, u32[]{:S(2)}, u32[]{:S(2)}) %collective-permute-start) | collective-permute-done | bytes 2097184 | tf_op jit(solution)/shard_map/ppermute | solution.py:381
  29.2 0.0 copy-start.1
  29.2 0.0 copy-start.2
  29.2 5.6 %shard_map.85 = (bf16[4,256,256]{2,1,0:T(8,128)(2,1)}, bf16[256,1024]{1,0:T(8,128)(2,1)}) custom-call(s32[8]{0:T(128)} %lengths.1, s32[8]{0:T(128)} %offsets.1, bf16[4,512,256]{2,1,0:T(8,128)(2,1)S(1)} %all-to-all-done.x_any, f32[1,1024]{1,0:T(1,128)S(1)} %shard_map.83.gain_ref, bf16[1024,1024]{1,0:T(8,128)(2,1)} %bitcast.4, bf16[8,512,256]{2,1,0:T(8,128)(2,1)} %keys.7, ...), custom_call_target="tpu_custom_call" | custom-call | flops 100000000 | tf_op jit(solution)/shard_map/pallas_call | solution.py:273
  34.8 4.8 %all-to-all-start.1 = ((bf16[4,256,256]{2,1,0:T(8,128)(2,1)}), bf16[4,256,256]{2,1,0:T(8,128)(2,1)S(1)}, u32[]{:S(2)}, u32[]{:S(2)}) async-start(bf16[4,256,256]{2,1,0:T(8,128)(2,1)} %get-tuple-element.16), calls=%async_computation.1 | async-start | bytes 1048576 | tf_op jit(solution)/shard_map/all_to_all | solution.py:372
  39.7 4.9 %collective-permute-done.1.moved = bf16[8,512,256]{2,1,0:T(8,128)(2,1)} collective-permute-done((bf16[8,512,256]{2,1,0:T(8,128)(2,1)}, bf16[8,512,256]{2,1,0:T(8,128)(2,1)}, u32[]{:S(2)}, u32[]{:S(2)}) %collective-permute-start.1) | collective-permute-done | bytes 2097184 | tf_op jit(solution)/shard_map/ppermute | solution.py:376
  44.5 0.0 copy-done.1
  44.5 0.0 copy-done.2
  44.5 0.0 copy-start
  44.5 3.9 %shard_map.86 = bf16[4,256,256]{2,1,0:T(8,128)(2,1)S(1)} custom-call(s32[8]{0:T(128)S(1)} %copy-done.1, s32[8]{0:T(128)S(1)} %copy-done.2, bf16[256,1024]{1,0:T(8,128)(2,1)} %get-tuple-element.15.b_hbm, bf16[8,512,256]{2,1,0:T(8,128)(2,1)} %keys.7, bf16[8,512,256]{2,1,0:T(8,128)(2,1)} %values.7, bf16[256,1024]{1,0:T(8,128)(2,1)} %w_hbm.1, ...), custom_call_target="tpu_custom_call" | custom-call | flops 3000000000 | tf_op jit(solution)/shard_map/pallas_call | solution.py:304
  48.4 0.0 all-to-all-done.1.even
  48.4 10.6 %all_to_all.15.odd = bf16[4,256,256]{2,1,0:T(8,128)(2,1)S(1)} all-to-all(bf16[4,256,256]{2,1,0:T(8,128)(2,1)S(1)} %shard_map.86), channel_id=1, replica_groups=mesh['user'=128,'head'=4] {'head'}, dimensions={0} | all-to-all | bytes 1048576 | tf_op jit(solution)/shard_map/all_to_all | solution.py:372
  59.1 0.0 copy-done
  59.1 0.9 %shard_map.87 = bf16[512,256]{1,0:T(8,128)(2,1)} custom-call(bf16[512,256]{1,0:T(8,128)(2,1)S(1)} %copy-done, bf16[4,256,256]{2,1,0:T(8,128)(2,1)S(1)} %all-to-all-done.1.even, bf16[4,256,256]{2,1,0:T(8,128)(2,1)S(1)} %all_to_all.15.odd), custom_call_target="tpu_custom_call" | custom-call | tf_op jit(solution)/shard_map/pallas_call | solution.py:352
  (1 shorter events, 0.0 us)
Async XLA Ops:
  2.9 23.9 %all-to-all-start = ((bf16[4,512,256]{2,1,0:T(8,128)(2,1)}), bf16[4,512,256]{2,1,0:T(8,128)(2,1)S(1)}, u32[]{:S(2)}, u32[]{:S(2)}) async-start(bf16[4,512,256]{2,1,0:T(8,128)(2,1)} %get-tuple-element.12), calls=%async_computation | async-start | bytes 2097152 | tf_op jit(solution)/shard_map/all_to_all | solution.py:372
  12.2 12.7 %copy-start.4 = (bf16[1024,4,256]{2,1,0:T(4,128)(2,1)S(1)}, bf16[1024,4,256]{2,1,0:T(4,128)(2,1)}, u32[]{:S(2)}) copy-start(bf16[1024,4,256]{2,1,0:T(4,128)(2,1)} %param.10) | copy-start | bytes 6291460
  12.2 32.3 %collective-permute-start.1 = (bf16[8,512,256]{2,1,0:T(8,128)(2,1)}, bf16[8,512,256]{2,1,0:T(8,128)(2,1)}, u32[]{:S(2)}, u32[]{:S(2)}) collective-permute-start(bf16[8,512,256]{2,1,0:T(8,128)(2,1)} %get-tuple-element.13), channel_id=1, source_target_pairs={{0,508},{4,8},{8,4},{12,16},{16,12},{20,24},{24,20},{28,32},{32,28... | collective-permute-start | bytes 6291464 | tf_op jit(solution)/shard_map/ppermute | solution.py:376
  23.0 6.3 %collective-permute-start = (bf16[8,512,256]{2,1,0:T(8,128)(2,1)}, bf16[8,512,256]{2,1,0:T(8,128)(2,1)S(1)}, u32[]{:S(2)}, u32[]{:S(2)}) collective-permute-start(bf16[8,512,256]{2,1,0:T(8,128)(2,1)} %shard_map.84), channel_id=1, source_target_pairs={{0,4},{4,0},{8,12},{12,8},{16,20},{20,16},{24,28},{28,24},{32,36},... | collective-permute-start | bytes 6291464 | tf_op jit(solution)/shard_map/ppermute | solution.py:381
  24.9 1.8 %copy-start.3 = (f32[1024]{0:T(1024)S(1)}, f32[1024]{0:T(1024)}, u32[]{:S(2)}) copy-start(f32[1024]{0:T(1024)} %param.9) | copy-start | bytes 12292
  29.2 15.3 %copy-start.1 = (s32[8]{0:T(128)S(1)}, s32[8]{0:T(128)}, u32[]{:S(2)}) copy-start(s32[8]{0:T(128)} %lengths.1) | copy-start | bytes 100
  29.2 15.3 %copy-start.2 = (s32[8]{0:T(128)S(1)}, s32[8]{0:T(128)}, u32[]{:S(2)}) copy-start(s32[8]{0:T(128)} %offsets.1) | copy-start | bytes 100
  34.8 13.6 %all-to-all-start.1 = ((bf16[4,256,256]{2,1,0:T(8,128)(2,1)}), bf16[4,256,256]{2,1,0:T(8,128)(2,1)S(1)}, u32[]{:S(2)}, u32[]{:S(2)}) async-start(bf16[4,256,256]{2,1,0:T(8,128)(2,1)} %get-tuple-element.16), calls=%async_computation.1 | async-start | bytes 1048576 | tf_op jit(solution)/shard_map/all_to_all | solution.py:372
  44.5 14.5 %copy-start = (bf16[512,256]{1,0:T(8,128)(2,1)S(1)}, bf16[512,256]{1,0:T(8,128)(2,1)}, u32[]{:S(2)}) copy-start(bf16[512,256]{1,0:T(8,128)(2,1)} %events.1) | copy-start | bytes 786436

commit v12 on v11

--- a/solution.py
+++ b/solution.py
@@ -335,17 +335,25 @@
     )(x4, gain)
 
 
-def combine_kernel(events, even, odd, out_ref):
-    parts, rows, _ = even.shape
-    half_slots = out_ref.shape[0] // 2 // NEW
-    for j in range(2 * half_slots):
-        at = slice(j * NEW, (j + 1) * NEW)
-        terms_at = slice((j // 2) * NEW, (j // 2 + 1) * NEW)
-        terms = odd if j % 2 else even
-        total = terms[0, terms_at, :].astype(jnp.float32)
-        for p in range(1, parts):
-            total = total + terms[p, terms_at, :].astype(jnp.float32)
-        out_ref[at, :] = (events[at, :].astype(jnp.float32) + total).astype(out_ref.dtype)
+def combine_kernel(events, even, odd, out_hbm, out_ref, sems):
+    parts = even.shape[0]
+    chunks = sems.shape[0]
+    rows = out_ref.shape[0] // chunks
+    leave = []
+    for chunk in range(chunks):
+        for j in range(chunk * rows // NEW, (chunk + 1) * rows // NEW):
+            at = slice(j * NEW, (j + 1) * NEW)
+            terms_at = slice((j // 2) * NEW, (j // 2 + 1) * NEW)
+            terms = odd if j % 2 else even
+            total = terms[0, terms_at, :].astype(jnp.float32)
+            for p in range(1, parts):
+                total = total + terms[p, terms_at, :].astype(jnp.float32)
+            out_ref[at, :] = (events[at, :].astype(jnp.float32) + total).astype(out_ref.dtype)
+        at = pl.ds(chunk * rows, rows)
+        leave.append(pltpu.make_async_copy(out_ref.at[at], out_hbm.at[at], sems.at[chunk]))
+        leave[-1].start()
+    for c in leave:
+        c.wait()
 
 
 def combine(events, even, odd):
@@ -353,7 +361,11 @@
         combine_kernel,
         out_shape=jax.ShapeDtypeStruct(events.shape, events.dtype),
         in_specs=[VMEM, VMEM, VMEM],
-        out_specs=VMEM,
+        out_specs=HBM,
+        scratch_shapes=[
+            pltpu.VMEM(events.shape, events.dtype),
+            pltpu.SemaphoreType.DMA((4,)),
+        ],
         compiler_params=pltpu.CompilerParams(vmem_limit_bytes=6 * 2**20),
     )(events, even, odd)
 

time: 61 us -> 61 us (level)
  no operation moved by 1% of the time
where the time goes in v12:
time: 61 us; the launch traced here: 59.9 us
  starting transfers between devices  24.4 us (40%)
  Pallas kernels  15.8 us (26%)
  blocking collectives  10.6 us (17%)
  waiting for transfers between devices  7.21 us (12%)
  local copies, waits for them, and re-layouts  1.84 us (3%)
    all_to_all x2, starting transfers between devices, to_heads(): return lax.all_to_all(blocks, 'head', 0, 0)  14.2 us
    all_to_all x1, blocking collectives, to_heads(): return lax.all_to_all(blocks, 'head', 0, 0)  10.6 us
    ppermute x1, starting transfers between devices, on_device(): odd = lax.ppermute(odd_pay, 'user', across)  8.28 us
    pallas_call x1, Pallas kernels, first(): pl.pallas_call(first_kernel, out_shape=(pltpu.HBM((parts, half, width), b...  5.75 us
    pallas_call x2, Pallas kernels, pack(): pl.pallas_call(functools.partial(pack_kernel, side), out_shape=outs, in_s...  5.31 us
    ppermute x1, waiting for transfers between devices, on_device(): odd = lax.ppermute(odd_pay, 'user', across)  4.72 us
    pallas_call x1, Pallas kernels, second(): pl.pallas_call(second_kernel, out_shape=jax.ShapeDtypeStruct((parts, rows...  3.92 us
    ppermute x1, waiting for transfers between devices, on_device(): even = lax.ppermute(even_pay, 'user', within)  2.49 us
  transfers between devices with their start and end apart: 4, of which 2 were waited for; matrix products, arithmetic and copies ran while one was open for 3% of the time, Pallas kernels for 20%

profile of v12, /device:TPU:6, one launch (start us, length us, event | category | flops | bytes accessed | tf_op | source)
XLA Modules:
  0.0 59.9 jit_solution(644137354870889617)
XLA Ops:
  0.0 2.8 %shard_map.82 = (bf16[8,512,256]{2,1,0:T(8,128)(2,1)}, bf16[4,512,256]{2,1,0:T(8,128)(2,1)}) custom-call(s32[8]{0:T(128)} %lengths.1, bf16[8,512,256]{2,1,0:T(8,128)(2,1)} %keys.7, bf16[8,512,256]{2,1,0:T(8,128)(2,1)} %values.7, bf16[512,256]{1,0:T(8,128)(2,1)} %events.1), custom_call_target="tpu_custom_call" | custom-call | bytes 4000000 | tf_op jit(solution)/shard_map/pallas_call | solution.py:76
  2.9 9.4 %all-to-all-start = ((bf16[4,512,256]{2,1,0:T(8,128)(2,1)}), bf16[4,512,256]{2,1,0:T(8,128)(2,1)S(1)}, u32[]{:S(2)}, u32[]{:S(2)}) async-start(bf16[4,512,256]{2,1,0:T(8,128)(2,1)} %get-tuple-element.12), calls=%async_computation | async-start | bytes 2097152 | tf_op jit(solution)/shard_map/all_to_all | solution.py:384
  12.2 0.0 copy-start.4
  12.2 8.3 %collective-permute-start.1 = (bf16[8,512,256]{2,1,0:T(8,128)(2,1)}, bf16[8,512,256]{2,1,0:T(8,128)(2,1)}, u32[]{:S(2)}, u32[]{:S(2)}) collective-permute-start(bf16[8,512,256]{2,1,0:T(8,128)(2,1)} %get-tuple-element.13), channel_id=1, source_target_pairs={{0,508},{4,8},{8,4},{12,16},{16,12},{20,24},{24,20},{28,32},{32,28... | collective-permute-start | bytes 6291464 | tf_op jit(solution)/shard_map/ppermute | solution.py:388
  20.5 2.5 %shard_map.84 = bf16[8,512,256]{2,1,0:T(8,128)(2,1)} custom-call(s32[8]{0:T(128)} %lengths.1, bf16[8,512,256]{2,1,0:T(8,128)(2,1)} %keys.7, bf16[8,512,256]{2,1,0:T(8,128)(2,1)} %values.7), custom_call_target="tpu_custom_call" | custom-call | bytes 15000000 | tf_op jit(solution)/shard_map/pallas_call | solution.py:76
  23.0 1.9 %collective-permute-start = (bf16[8,512,256]{2,1,0:T(8,128)(2,1)}, bf16[8,512,256]{2,1,0:T(8,128)(2,1)S(1)}, u32[]{:S(2)}, u32[]{:S(2)}) collective-permute-start(bf16[8,512,256]{2,1,0:T(8,128)(2,1)} %shard_map.84), channel_id=1, source_target_pairs={{0,4},{4,0},{8,12},{12,8},{16,20},{20,16},{24,28},{28,24},{32,36},... | collective-permute-start | bytes 6291464 | tf_op jit(solution)/shard_map/ppermute | solution.py:393
  24.9 0.0 copy-done.4
  24.9 0.0 copy-start.3
  24.9 1.8 %copy.9 = bf16[128,8,4,256]{3,1,2,0:T(8,128)(2,1)} copy(bf16[128,8,4,256]{3,2,1,0:T(4,128)(2,1)S(1)} %bitcast.5) | data formatting | bytes 4194304
  26.7 0.0 all-to-all-done.x_any
  26.7 0.0 copy-done.3
  26.7 2.5 %collective-permute-done.moved = bf16[8,512,256]{2,1,0:T(8,128)(2,1)S(1)} collective-permute-done((bf16[8,512,256]{2,1,0:T(8,128)(2,1)}, bf16[8,512,256]{2,1,0:T(8,128)(2,1)S(1)}, u32[]{:S(2)}, u32[]{:S(2)}) %collective-permute-start) | collective-permute-done | bytes 2097184 | tf_op jit(solution)/shard_map/ppermute | solution.py:393
  29.2 0.0 copy-start.1
  29.2 0.0 copy-start.2
  29.2 5.8 %shard_map.85 = (bf16[4,256,256]{2,1,0:T(8,128)(2,1)}, bf16[256,1024]{1,0:T(8,128)(2,1)}) custom-call(s32[8]{0:T(128)} %lengths.1, s32[8]{0:T(128)} %offsets.1, bf16[4,512,256]{2,1,0:T(8,128)(2,1)S(1)} %all-to-all-done.x_any, f32[1,1024]{1,0:T(1,128)S(1)} %shard_map.83.gain_ref, bf16[1024,1024]{1,0:T(8,128)(2,1)} %bitcast.4, bf16[8,512,256]{2,1,0:T(8,128)(2,1)} %keys.7, ...), custom_call_target="tpu_custom_call" | custom-call | flops 100000000 | tf_op jit(solution)/shard_map/pallas_call | solution.py:273
  35.0 4.8 %all-to-all-start.1 = ((bf16[4,256,256]{2,1,0:T(8,128)(2,1)}), bf16[4,256,256]{2,1,0:T(8,128)(2,1)S(1)}, u32[]{:S(2)}, u32[]{:S(2)}) async-start(bf16[4,256,256]{2,1,0:T(8,128)(2,1)} %get-tuple-element.16), calls=%async_computation.1 | async-start | bytes 1048576 | tf_op jit(solution)/shard_map/all_to_all | solution.py:384
  39.8 4.7 %collective-permute-done.1.moved = bf16[8,512,256]{2,1,0:T(8,128)(2,1)} collective-permute-done((bf16[8,512,256]{2,1,0:T(8,128)(2,1)}, bf16[8,512,256]{2,1,0:T(8,128)(2,1)}, u32[]{:S(2)}, u32[]{:S(2)}) %collective-permute-start.1) | collective-permute-done | bytes 2097184 | tf_op jit(solution)/shard_map/ppermute | solution.py:388
  44.5 0.0 copy-done.1
  44.5 0.0 copy-done.2
  44.5 0.0 copy-start
  44.5 3.9 %shard_map.86 = bf16[4,256,256]{2,1,0:T(8,128)(2,1)S(1)} custom-call(s32[8]{0:T(128)S(1)} %copy-done.1, s32[8]{0:T(128)S(1)} %copy-done.2, bf16[256,1024]{1,0:T(8,128)(2,1)} %get-tuple-element.15.b_hbm, bf16[8,512,256]{2,1,0:T(8,128)(2,1)} %keys.7, bf16[8,512,256]{2,1,0:T(8,128)(2,1)} %values.7, bf16[256,1024]{1,0:T(8,128)(2,1)} %w_hbm.1, ...), custom_call_target="tpu_custom_call" | custom-call | flops 3000000000 | tf_op jit(solution)/shard_map/pallas_call | solution.py:304
  48.5 0.0 all-to-all-done.1.even
  48.5 10.6 %all_to_all.15.odd = bf16[4,256,256]{2,1,0:T(8,128)(2,1)S(1)} all-to-all(bf16[4,256,256]{2,1,0:T(8,128)(2,1)S(1)} %shard_map.86), channel_id=1, replica_groups=mesh['user'=128,'head'=4] {'head'}, dimensions={0} | all-to-all | bytes 1048576 | tf_op jit(solution)/shard_map/all_to_all | solution.py:384
  59.1 0.0 copy-done
  59.1 0.8 %shard_map.87 = bf16[512,256]{1,0:T(8,128)(2,1)} custom-call(bf16[512,256]{1,0:T(8,128)(2,1)S(1)} %copy-done, bf16[4,256,256]{2,1,0:T(8,128)(2,1)S(1)} %all-to-all-done.1.even, bf16[4,256,256]{2,1,0:T(8,128)(2,1)S(1)} %all_to_all.15.odd), custom_call_target="tpu_custom_call" | custom-call | tf_op jit(solution)/shard_map/pallas_call | solution.py:360
  (1 shorter events, 0.0 us)
Async XLA Ops:
  2.9 23.9 %all-to-all-start = ((bf16[4,512,256]{2,1,0:T(8,128)(2,1)}), bf16[4,512,256]{2,1,0:T(8,128)(2,1)S(1)}, u32[]{:S(2)}, u32[]{:S(2)}) async-start(bf16[4,512,256]{2,1,0:T(8,128)(2,1)} %get-tuple-element.12), calls=%async_computation | async-start | bytes 2097152 | tf_op jit(solution)/shard_map/all_to_all | solution.py:384
  12.2 12.7 %copy-start.4 = (bf16[1024,4,256]{2,1,0:T(4,128)(2,1)S(1)}, bf16[1024,4,256]{2,1,0:T(4,128)(2,1)}, u32[]{:S(2)}) copy-start(bf16[1024,4,256]{2,1,0:T(4,128)(2,1)} %param.10) | copy-start | bytes 6291460
  12.2 32.3 %collective-permute-start.1 = (bf16[8,512,256]{2,1,0:T(8,128)(2,1)}, bf16[8,512,256]{2,1,0:T(8,128)(2,1)}, u32[]{:S(2)}, u32[]{:S(2)}) collective-permute-start(bf16[8,512,256]{2,1,0:T(8,128)(2,1)} %get-tuple-element.13), channel_id=1, source_target_pairs={{0,508},{4,8},{8,4},{12,16},{16,12},{20,24},{24,20},{28,32},{32,28... | collective-permute-start | bytes 6291464 | tf_op jit(solution)/shard_map/ppermute | solution.py:388
  23.0 6.3 %collective-permute-start = (bf16[8,512,256]{2,1,0:T(8,128)(2,1)}, bf16[8,512,256]{2,1,0:T(8,128)(2,1)S(1)}, u32[]{:S(2)}, u32[]{:S(2)}) collective-permute-start(bf16[8,512,256]{2,1,0:T(8,128)(2,1)} %shard_map.84), channel_id=1, source_target_pairs={{0,4},{4,0},{8,12},{12,8},{16,20},{20,16},{24,28},{28,24},{32,36},... | collective-permute-start | bytes 6291464 | tf_op jit(solution)/shard_map/ppermute | solution.py:393
  24.9 1.8 %copy-start.3 = (f32[1024]{0:T(1024)S(1)}, f32[1024]{0:T(1024)}, u32[]{:S(2)}) copy-start(f32[1024]{0:T(1024)} %param.9) | copy-start | bytes 12292
  29.2 15.3 %copy-start.1 = (s32[8]{0:T(128)S(1)}, s32[8]{0:T(128)}, u32[]{:S(2)}) copy-start(s32[8]{0:T(128)} %lengths.1) | copy-start | bytes 100
  29.2 15.3 %copy-start.2 = (s32[8]{0:T(128)S(1)}, s32[8]{0:T(128)}, u32[]{:S(2)}) copy-start(s32[8]{0:T(128)} %offsets.1) | copy-start | bytes 100
  35.0 13.5 %all-to-all-start.1 = ((bf16[4,256,256]{2,1,0:T(8,128)(2,1)}), bf16[4,256,256]{2,1,0:T(8,128)(2,1)S(1)}, u32[]{:S(2)}, u32[]{:S(2)}) async-start(bf16[4,256,256]{2,1,0:T(8,128)(2,1)} %get-tuple-element.16), calls=%async_computation.1 | async-start | bytes 1048576 | tf_op jit(solution)/shard_map/all_to_all | solution.py:384
  44.5 14.6 %copy-start = (bf16[512,256]{1,0:T(8,128)(2,1)S(1)}, bf16[512,256]{1,0:T(8,128)(2,1)}, u32[]{:S(2)}) copy-start(bf16[512,256]{1,0:T(8,128)(2,1)} %events.1) | copy-start | bytes 786436
